TPU v7x, 32 devices: a whole 2x2x4 slice. The times are simulated.
32 devices in a mesh: group: 2 (over y), member: 16 (over z, x, core).
Axes of the slice: x: 2, y: 2, z: 4, core: 2. Of those that a mesh axis runs over, the one named last changes fastest.
Arguments:
- student: bfloat16 [12288, 768], P(('group', 'member')), may hold values from -0.29882812 to 0.29882812
- teacher: bfloat16 [12288, 1024], P(('group', 'member')), may hold values from -14 to 14
- counts: int32 [12288], P(('group', 'member')), may hold values from 1 to 7, as said below
- plan: int32 [2, 16, 5], P('group', 'member'), may hold values from 0 to 1, as said below
Outputs:
- grad_student: float32 [12288, 768], P(('group', 'member'))
- loss: float32 [], replicated
Inputs may be any that keep to these rules, and one draw needn't show every extreme that they name: `counts`: each row's count is a whole number from 1 up. The pairing is symmetric: plan[g, m, 2 + k - 1] equals plan[g, (m + k) mod 16, k - 1] for k = 1 to 2, and plan[g, m, 4] equals plan[g xor 1, m, 4].
All inputs are finite; a program needn't handle non-finite values.
Results may differ from a plain program's by a relative error of at most 0.0046.
Values may be sent and summed in bfloat16 or wider, within the bound.
No kernel may reach another device: no remote copies, remote signals or barrier semaphores. Data moves between devices by JAX's collectives and lax.ppermute only.
A program may use at most 64 MiB of HBM per device.

v0:
```python
import jax
import jax.numpy as jnp
from jax import lax
from jax.sharding import PartitionSpec as P

EPS = 1e-06


def passed_along(value, axis, steps):
    count = lax.axis_size(axis)
    pairs = [(source, (source + steps) % count) for source in range(count)]
    return lax.ppermute(value, axis, pairs)


def partner_2(block, axis, bit):
    count = lax.axis_size(axis)
    route = []
    for low in range(count):
        high = low | 1 << bit
        if high != low and high < count:
            route += [(low, high), (high, low)]
    return lax.ppermute(block, axis, route)


def normalize(embeddings):
    widened = embeddings.astype(jnp.float32)
    row_scale = lax.rsqrt(jnp.sum(widened * widened, axis=-1, keepdims=True) + EPS)
    return ((widened * row_scale).astype(jnp.bfloat16), row_scale)


def block_terms(local_rows, partner, switch):
    local_s, local_t, local_w = local_rows
    partner_s, partner_t, partner_w = partner
    local_count = local_s.shape[0]
    features = local_s.shape[1]

    def compute(operand):
        student_sim = jnp.einsum(
            "id,jd->ij", local_s, partner_s, preferred_element_type=jnp.float32
        )
        teacher_sim = jnp.einsum(
            "id,jd->ij", local_t, partner_t, preferred_element_type=jnp.float32
        )
        mismatch = student_sim - teacher_sim
        pair_weight = local_w[:, None] * partner_w.astype(jnp.float32)[None, :]
        coefficient = (pair_weight * mismatch).astype(jnp.bfloat16)
        contrib = jnp.dot(coefficient, partner_s, preferred_element_type=jnp.float32)
        results = (contrib, jnp.sum(pair_weight * mismatch * mismatch), jnp.sum(pair_weight))
        return results

    def skipped(operand):
        results = (
            jnp.zeros((local_count, features), jnp.float32),
            jnp.float32(0.0),
            jnp.float32(0.0),
        )
        return results

    return lax.cond(switch > 0, compute, skipped, 0)


def per_device(student, teacher, counts, plan):
    unit_student, row_scale = normalize(student)
    unit_teacher, unused_scale = normalize(teacher)
    weights = counts.astype(jnp.float32)
    switches = plan.reshape(-1).astype(jnp.float32)
    span_blocks = (switches.shape[0] - 1) // 2
    local_rows = (unit_student, unit_teacher, weights)
    outgoing = (unit_student, unit_teacher, weights.astype(jnp.bfloat16))
    summed_grad, loss_sum, weight_sum = block_terms(local_rows, outgoing, jnp.float32(1.0))
    for offset in range(1, span_blocks + 1):
        lower = passed_along((outgoing[0], outgoing[1], outgoing[2]), "member", offset)
        upper = passed_along((outgoing[0], outgoing[1], outgoing[2]), "member", -offset)
        for column, partner in ((offset - 1, lower), (span_blocks + offset - 1, upper)):
            contrib, loss_part, weight_part = block_terms(local_rows, partner, switches[column])
            summed_grad = summed_grad + contrib
            loss_sum = loss_sum + loss_part
            weight_sum = weight_sum + weight_part
    partner = partner_2((outgoing[0], outgoing[1], outgoing[2]), "group", 0)
    contrib, loss_part, weight_part = block_terms(local_rows, partner, switches[2 * span_blocks])
    summed_grad = summed_grad + contrib
    loss_sum = loss_sum + loss_part
    weight_sum = weight_sum + weight_part
    loss_sum, weight_sum = lax.psum((loss_sum, weight_sum), ("group", "member"))
    unit_float = unit_student.astype(jnp.float32)
    along_unit = jnp.sum(summed_grad * unit_float, axis=-1, keepdims=True)
    grad_student = 4.0 * row_scale * (summed_grad - along_unit * unit_float)
    loss = student.shape[1] * loss_sum / weight_sum
    return (grad_student, loss)


def solution(mesh):
    return jax.shard_map(
        per_device,
        mesh=mesh,
        in_specs=(
            P(("group", "member"), None),
            P(("group", "member"), None),
            P(("group", "member")),
            P("group", "member", None),
        ),
        out_specs=(P(("group", "member"), None), P()),
        check_vma=False,
    )
```

profile of v0, /device:TPU:0, one launch (start us, length us, event | category | flops | bytes accessed | tf_op | source)
XLA Modules:
  0.0 166.2 jit_solution(10395199438841692117)
XLA Ops:
  0.7 1.5 fusion.35
  2.9 5.0 %collective-permute-start.5 = (bf16[384,1024]{1,0:T(8,128)(2,1)S(1)}, bf16[384,1024]{1,0:T(8,128)(2,1)S(1)}, u32[]{:S(2)}, u32[]{:S(2)}) collective-permute-start(bf16[384,1024]{1,0:T(8,128)(2,1)S(1)} %fusion.36), channel_id=1, source_target_pairs={{0,15},{1,0},{2,1},{3,2},{4,3},{5,4},{6,5},{7,6},{8,7},{9,8},{10,9... | collective-permute-start | bytes 2359304 | tf_op jit(solution)/shard_map/ppermute | solution.py:12
  7.9 4.4 %collective-permute-start.3 = (bf16[384]{0:T(512)(128)(2,1)S(1)}, bf16[384]{0:T(512)(128)(2,1)S(1)}, u32[]{:S(2)}, u32[]{:S(2)}) collective-permute-start(bf16[384]{0:T(512)(128)(2,1)S(1)} %get-tuple-element.139), channel_id=1, source_target_pairs={{0,15},{1,0},{2,1},{3,2},{4,3},{5,4},{6,5},{7,6},{8,7},{9,8},{10,9... | collective-permute-start | bytes 2312 | tf_op jit(solution)/shard_map/ppermute | solution.py:12
  12.7 4.9 %collective-permute-done = bf16[384]{0:T(512)(128)(2,1)S(1)} collective-permute-done((bf16[384]{0:T(512)(128)(2,1)S(1)}, bf16[384]{0:T(512)(128)(2,1)S(1)}, u32[]{:S(2)}, u32[]{:S(2)}) %collective-permute-start) | collective-permute-done | bytes 800 | tf_op jit(solution)/shard_map/ppermute | solution.py:12
  17.6 5.2 %collective-permute-start.1 = (bf16[384,768]{1,0:T(8,128)(2,1)S(1)}, bf16[384,768]{1,0:T(8,128)(2,1)S(1)}, u32[]{:S(2)}, u32[]{:S(2)}) collective-permute-start(bf16[384,768]{1,0:T(8,128)(2,1)S(1)} %fusion.38), channel_id=1, source_target_pairs={{0,1},{1,2},{2,3},{3,4},{4,5},{5,6},{6,7},{7,8},{8,9},{9,10},{10,1... | collective-permute-start | bytes 1769480 | tf_op jit(solution)/shard_map/ppermute | solution.py:12
  22.9 10.7 %collective-permute-start.9 = (bf16[384]{0:T(512)(128)(2,1)S(1)}, bf16[384]{0:T(512)(128)(2,1)S(1)}, u32[]{:S(2)}, u32[]{:S(2)}) collective-permute-start(bf16[384]{0:T(512)(128)(2,1)S(1)} %get-tuple-element.139), channel_id=1, source_target_pairs={{0,14},{1,15},{2,0},{3,1},{4,2},{5,3},{6,4},{7,5},{8,6},{9,7},{10,... | collective-permute-start | bytes 2312 | tf_op jit(solution)/shard_map/ppermute | solution.py:12
  33.6 1.6 collective-permute-start.4
  35.2 0.7 collective-permute-start.7
  36.0 6.6 %collective-permute-done.4 = bf16[384,768]{1,0:T(8,128)(2,1)S(1)} collective-permute-done((bf16[384,768]{1,0:T(8,128)(2,1)S(1)}, bf16[384,768]{1,0:T(8,128)(2,1)S(1)}, u32[]{:S(2)}, u32[]{:S(2)}) %collective-permute-start.4) | collective-permute-done | bytes 589856 | tf_op jit(solution)/shard_map/ppermute | solution.py:12
  42.6 29.8 %collective-permute-start.11 = (bf16[384,1024]{1,0:T(8,128)(2,1)S(1)}, bf16[384,1024]{1,0:T(8,128)(2,1)}, u32[]{:S(2)}, u32[]{:S(2)}) collective-permute-start(bf16[384,1024]{1,0:T(8,128)(2,1)S(1)} %fusion.36), channel_id=1, source_target_pairs={{0,14},{1,15},{2,0},{3,1},{4,2},{5,3},{6,4},{7,5},{8,6},{9,7},{10,... | collective-permute-start | bytes 2359304 | tf_op jit(solution)/shard_map/ppermute | solution.py:12
  72.4 0.8 copy-done.5
  73.3 1.5 collective-permute-start.14
  74.8 0.9 collective-permute-start.10
  80.6 2.0 %multiply_reduce_fusion.5 = (f32[]{:T(128)}, f32[]{:T(128)}, f32[384,384]{1,0:T(8,128)}) fusion(f32[384]{0:T(512)S(1)} %get-tuple-element.138, f32[384]{0:T(512)S(1)} %get-tuple-element.147, f32[384,384]{1,0:T(8,128)S(1)} %fusion.56, bf16[384,768]{1,0:T(8,128)(2,1)S(1)} %fusion.38), kind=kOutput, calls=%fused_computation.60 | convolution fusion | flops 227377152 | bytes 1772552 | tf_op jit(solution)/shard_map/cond/branch_1_fun/id,jd->ij/dot_general | solution.py:38
  83.3 1.6 collective-permute-start.12
  84.9 5.8 %conditional.6 = (f32[384,768]{1,0:T(8,128)}, f32[]{:T(128)}, f32[]{:T(128)}) conditional(s32[]{:T(128)} %bitcast.1, () %tuple.50, (f32[384]{0:T(512)S(1)}, bf16[384]{0:T(512)(128)(2,1)S(1)}, bf16[384,768]{1,0:T(8,128)(2,1)S(1)}, bf16[384,768]{1,0:T(8,128)(2,1)}, bf16[384,1024]{1,0:T(8,128)(2,1)S(1)}, /*index=5*/bf16[384,1024]{1,0:T(8,128)(2,1)}) %tuple.92), branch_computations={%region_6.7_spmd, %region_7.10_spmd} | conditional | flops 756302208 | bytes 9249084 | solution.py:59
  84.9 1.8 %fusion.52 = f32[384,384]{1,0:T(8,128)S(1)} fusion(bf16[384,1024]{1,0:T(8,128)(2,1)S(1)} %get-tuple-element.70, bf16[384,1024]{1,0:T(8,128)(2,1)} %get-tuple-element.71), kind=kOutput, calls=%fused_computation.75 | convolution fusion | flops 301989888 | bytes 2162688 | tf_op jit(solution)/shard_map/cond/branch_1_fun/id,jd->ij/dot_general | solution.py:41
  86.7 1.2 multiply_reduce_fusion.1
  87.9 1.6 fusion.10
  90.9 9.6 %collective-permute-done.10 = bf16[384,768]{1,0:T(8,128)(2,1)} collective-permute-done((bf16[384,768]{1,0:T(8,128)(2,1)S(1)}, bf16[384,768]{1,0:T(8,128)(2,1)}, u32[]{:S(2)}, u32[]{:S(2)}) %collective-permute-start.10) | collective-permute-done | bytes 589856 | tf_op jit(solution)/shard_map/ppermute | solution.py:12
  100.4 7.9 %conditional.8 = (f32[384,768]{1,0:T(8,128)}, f32[]{:T(128)}, f32[]{:T(128)}) conditional(s32[]{:T(128)} %bitcast.3, () %tuple.54, (f32[384]{0:T(512)S(1)}, bf16[384]{0:T(512)(128)(2,1)S(1)}, bf16[384,768]{1,0:T(8,128)(2,1)S(1)}, bf16[384,768]{1,0:T(8,128)(2,1)}, bf16[384,1024]{1,0:T(8,128)(2,1)S(1)}, /*index=5*/bf16[384,1024]{1,0:T(8,128)(2,1)}) %tuple.55), branch_computations={%region_14.15_spmd, %region_15.18_spmd} | conditional | flops 756302208 | bytes 6889760 | solution.py:59
  100.4 1.7 %fusion.54 = f32[384,384]{1,0:T(8,128)S(1)} fusion(bf16[384,1024]{1,0:T(8,128)(2,1)S(1)} %get-tuple-element.82, bf16[384,1024]{1,0:T(8,128)(2,1)} %get-tuple-element.83), kind=kOutput, calls=%fused_computation.77 | convolution fusion | flops 301989888 | bytes 2162688 | tf_op jit(solution)/shard_map/cond/branch_1_fun/id,jd->ij/dot_general | solution.py:41
  102.2 2.3 %multiply_reduce_fusion.3 = (f32[]{:T(128)}, f32[]{:T(128)}, f32[384,384]{1,0:T(8,128)S(1)}) fusion(f32[384]{0:T(512)S(1)} %convert_element_type.72, f32[384]{0:T(512)S(1)} %get-tuple-element.78, f32[384,384]{1,0:T(8,128)S(1)} %fusion.54, bf16[384,768]{1,0:T(8,128)(2,1)S(1)} %get-tuple-element.80, bf16[384,768]{1,0:T(8,128)(2,1)} %get-tuple-element.81), kind=kOutput, calls=%fused_computation.28 | convolution fusion | flops 227377152 | bytes 2362376 | tf_op jit(solution)/shard_map/cond/branch_1_fun/id,jd->ij/dot_general | solution.py:38
  104.5 2.6 %fusion.24 = f32[384,768]{1,0:T(8,128)} fusion(bf16[384,768]{1,0:T(8,128)(2,1)} %get-tuple-element.81, f32[384,384]{1,0:T(8,128)S(1)} %get-tuple-element.143, f32[384]{0:T(512)S(1)} %convert_element_type.72, f32[384]{0:T(512)S(1)} %get-tuple-element.78), kind=kOutput, calls=%fused_computation.33 | convolution fusion | flops 226934784 | bytes 2362368 | tf_op jit(solution)/shard_map/cond/branch_1_fun/dot_general | solution.py:47
  108.4 6.7 %conditional.9 = (f32[384,768]{1,0:T(8,128)S(1)}, f32[]{:T(128)}, f32[]{:T(128)}) conditional(s32[]{:T(128)} %bitcast.4, () %tuple.56, (f32[384]{0:T(512)S(1)}, bf16[384]{0:T(512)(128)(2,1)S(1)}, bf16[384,768]{1,0:T(8,128)(2,1)S(1)}, bf16[384,768]{1,0:T(8,128)(2,1)}, bf16[384,1024]{1,0:T(8,128)(2,1)S(1)}, ...), branch_computations={%region_18.19_spmd, %region_19.22_spmd} | conditional | flops 756302208 | bytes 6889760 | solution.py:59
  108.5 1.7 %fusion.55 = f32[384,384]{1,0:T(8,128)S(1)} fusion(bf16[384,1024]{1,0:T(8,128)(2,1)S(1)} %get-tuple-element.88, bf16[384,1024]{1,0:T(8,128)(2,1)} %get-tuple-element.89), kind=kOutput, calls=%fused_computation.78 | convolution fusion | flops 301989888 | bytes 2162688 | tf_op jit(solution)/shard_map/cond/branch_1_fun/id,jd->ij/dot_general | solution.py:41
  110.2 2.2 %multiply_reduce_fusion.4 = (f32[]{:T(128)}, f32[]{:T(128)}, f32[384,384]{1,0:T(8,128)S(1)}) fusion(f32[384]{0:T(512)S(1)} %convert_element_type.74, f32[384]{0:T(512)S(1)} %get-tuple-element.84, f32[384,384]{1,0:T(8,128)S(1)} %fusion.55, bf16[384,768]{1,0:T(8,128)(2,1)S(1)} %get-tuple-element.86, bf16[384,768]{1,0:T(8,128)(2,1)} %get-tuple-element.87), kind=kOutput, calls=%fused_computation.37 | convolution fusion | flops 227377152 | bytes 2362376 | tf_op jit(solution)/shard_map/cond/branch_1_fun/id,jd->ij/dot_general | solution.py:38
  112.4 1.6 fusion.31
  116.1 1.6 fusion.45
  117.7 41.5 %all-reduce = (f32[]{:T(128)}, f32[]{:T(128)}) all-reduce(f32[]{:T(128)S(6)} %add.79, f32[]{:T(128)S(6)} %add.84), channel_id=1, replica_groups=mesh['group'=2,'member'=16] {'group','member'}, use_global_device_ids=true, to_apply=%region_24.0 | all-reduce | flops 2 | bytes 16 | tf_op jit(solution)/shard_map/psum | solution.py:84
  160.6 3.2 %fusion.39 = (f32[384]{0:T(512)S(1)}, f32[384,768]{1,0:T(8,128)S(1)}) fusion(f32[384,768]{1,0:T(8,128)} %copy-done.3, f32[384,768]{1,0:T(8,128)} %get-tuple-element.110, f32[384,768]{1,0:T(8,128)} %copy-done.2, f32[384,768]{1,0:T(8,128)} %get-tuple-element.108, f32[384,768]{1,0:T(8,128)S(1)} %fusion.45, f32[384,768]{1,0:T(8,128)} %copy-done.1, ...), kind=kLoop, calls=%fused_computation.56 | loop fusion | flops 3243648 | bytes 8850432 | tf_op jit(solution)/shard_map/reduce_sum | solution.py:86
  163.7 1.3 fusion.41
  (56 shorter events, 3.7 us)
Async XLA Ops:
  0.6 1.5 copy-start.4
  0.6 7.3 %copy-start.13 = (s32[384]{0:T(512)S(1)}, s32[384]{0:T(512)}, u32[]{:S(2)}) copy-start(s32[384]{0:T(512)} %param.16) | copy-start | bytes 4612
  0.6 11.7 %copy-start = (bf16[384,768]{1,0:T(8,128)(2,1)S(1)}, bf16[384,768]{1,0:T(8,128)(2,1)}, u32[]{:S(2)}) copy-start(bf16[384,768]{1,0:T(8,128)(2,1)} %param.14) | copy-start | bytes 1769476
  2.3 72.4 %copy-start.14 = (s32[1,1,5]{2,1,0:T(1,128)S(1)}, s32[1,1,5]{2,1,0:T(1,128)}, u32[]{:S(2)}) copy-start(s32[1,1,5]{2,1,0:T(1,128)} %param.17) | copy-start | bytes 64
  2.4 72.4 %collective-permute-start.2 = (bf16[384,1024]{1,0:T(8,128)(2,1)S(1)}, bf16[384,1024]{1,0:T(8,128)(2,1)S(1)}, u32[]{:S(2)}, u32[]{:S(2)}) collective-permute-start(bf16[384,1024]{1,0:T(8,128)(2,1)S(1)} %fusion.36), channel_id=1, source_target_pairs={{0,1},{1,2},{2,3},{3,4},{4,5},{5,6},{6,7},{7,8},{8,9},{9,10},{10,1... | collective-permute-start | bytes 2359304 | tf_op jit(solution)/shard_map/ppermute | solution.py:12
  2.9 72.8 %collective-permute-start.5 = (bf16[384,1024]{1,0:T(8,128)(2,1)S(1)}, bf16[384,1024]{1,0:T(8,128)(2,1)S(1)}, u32[]{:S(2)}, u32[]{:S(2)}) collective-permute-start(bf16[384,1024]{1,0:T(8,128)(2,1)S(1)} %fusion.36), channel_id=1, source_target_pairs={{0,15},{1,0},{2,1},{3,2},{4,3},{5,4},{6,5},{7,6},{8,7},{9,8},{10,9... | collective-permute-start | bytes 2359304 | tf_op jit(solution)/shard_map/ppermute | solution.py:12
  7.9 9.7 %collective-permute-start = (bf16[384]{0:T(512)(128)(2,1)S(1)}, bf16[384]{0:T(512)(128)(2,1)S(1)}, u32[]{:S(2)}, u32[]{:S(2)}) collective-permute-start(bf16[384]{0:T(512)(128)(2,1)S(1)} %get-tuple-element.139), channel_id=1, source_target_pairs={{0,1},{1,2},{2,3},{3,4},{4,5},{5,6},{6,7},{7,8},{8,9},{9,10},{10,1... | collective-permute-start | bytes 2312 | tf_op jit(solution)/shard_map/ppermute | solution.py:12
  7.9 15.0 %collective-permute-start.3 = (bf16[384]{0:T(512)(128)(2,1)S(1)}, bf16[384]{0:T(512)(128)(2,1)S(1)}, u32[]{:S(2)}, u32[]{:S(2)}) collective-permute-start(bf16[384]{0:T(512)(128)(2,1)S(1)} %get-tuple-element.139), channel_id=1, source_target_pairs={{0,15},{1,0},{2,1},{3,2},{4,3},{5,4},{6,5},{7,6},{8,7},{9,8},{10,9... | collective-permute-start | bytes 2312 | tf_op jit(solution)/shard_map/ppermute | solution.py:12
  12.3 21.2 %collective-permute-start.6 = (bf16[384]{0:T(512)(128)(2,1)S(1)}, bf16[384]{0:T(512)(128)(2,1)S(1)}, u32[]{:S(2)}, u32[]{:S(2)}) collective-permute-start(bf16[384]{0:T(512)(128)(2,1)S(1)} %get-tuple-element.139), channel_id=1, source_target_pairs={{0,2},{1,3},{2,4},{3,5},{4,6},{5,7},{6,8},{7,9},{8,10},{9,11},{10,... | collective-permute-start | bytes 2312 | tf_op jit(solution)/shard_map/ppermute | solution.py:12
  17.6 18.2 %collective-permute-start.1 = (bf16[384,768]{1,0:T(8,128)(2,1)S(1)}, bf16[384,768]{1,0:T(8,128)(2,1)S(1)}, u32[]{:S(2)}, u32[]{:S(2)}) collective-permute-start(bf16[384,768]{1,0:T(8,128)(2,1)S(1)} %fusion.38), channel_id=1, source_target_pairs={{0,1},{1,2},{2,3},{3,4},{4,5},{5,6},{6,7},{7,8},{8,9},{9,10},{10,1... | collective-permute-start | bytes 1769480 | tf_op jit(solution)/shard_map/ppermute | solution.py:12
  22.9 12.3 %collective-permute-start.9 = (bf16[384]{0:T(512)(128)(2,1)S(1)}, bf16[384]{0:T(512)(128)(2,1)S(1)}, u32[]{:S(2)}, u32[]{:S(2)}) collective-permute-start(bf16[384]{0:T(512)(128)(2,1)S(1)} %get-tuple-element.139), channel_id=1, source_target_pairs={{0,14},{1,15},{2,0},{3,1},{4,2},{5,3},{6,4},{7,5},{8,6},{9,7},{10,... | collective-permute-start | bytes 2312 | tf_op jit(solution)/shard_map/ppermute | solution.py:12
  33.6 9.0 %collective-permute-start.4 = (bf16[384,768]{1,0:T(8,128)(2,1)S(1)}, bf16[384,768]{1,0:T(8,128)(2,1)S(1)}, u32[]{:S(2)}, u32[]{:S(2)}) collective-permute-start(bf16[384,768]{1,0:T(8,128)(2,1)S(1)} %fusion.38), channel_id=1, source_target_pairs={{0,15},{1,0},{2,1},{3,2},{4,3},{5,4},{6,5},{7,6},{8,7},{9,8},{10,9... | collective-permute-start | bytes 1769480 | tf_op jit(solution)/shard_map/ppermute | solution.py:12
  35.2 37.2 %collective-permute-start.7 = (bf16[384,768]{1,0:T(8,128)(2,1)S(1)}, bf16[384,768]{1,0:T(8,128)(2,1)S(1)}, u32[]{:S(2)}, u32[]{:S(2)}) collective-permute-start(bf16[384,768]{1,0:T(8,128)(2,1)S(1)} %fusion.38), channel_id=1, source_target_pairs={{0,2},{1,3},{2,4},{3,5},{4,6},{5,7},{6,8},{7,9},{8,10},{9,11},{10,... | collective-permute-start | bytes 1769480 | tf_op jit(solution)/shard_map/ppermute | solution.py:12
  35.9 36.5 %copy-start.9 = (bf16[384,768]{1,0:T(8,128)(2,1)}, bf16[384,768]{1,0:T(8,128)(2,1)S(1)}, u32[]{:S(2)}) copy-start(bf16[384,768]{1,0:T(8,128)(2,1)S(1)} %collective-permute-done.1) | copy-start | bytes 1769476
  35.9 47.4 %collective-permute-start.8 = (bf16[384,1024]{1,0:T(8,128)(2,1)S(1)}, bf16[384,1024]{1,0:T(8,128)(2,1)}, u32[]{:S(2)}, u32[]{:S(2)}) collective-permute-start(bf16[384,1024]{1,0:T(8,128)(2,1)S(1)} %fusion.36), channel_id=1, source_target_pairs={{0,2},{1,3},{2,4},{3,5},{4,6},{5,7},{6,8},{7,9},{8,10},{9,11},{10,... | collective-permute-start | bytes 2359304 | tf_op jit(solution)/shard_map/ppermute | solution.py:12
  42.6 29.8 %copy-start.7 = (bf16[384,768]{1,0:T(8,128)(2,1)}, bf16[384,768]{1,0:T(8,128)(2,1)S(1)}, u32[]{:S(2)}) copy-start(bf16[384,768]{1,0:T(8,128)(2,1)S(1)} %collective-permute-done.4) | copy-start | bytes 1769476
  42.6 57.8 %collective-permute-start.11 = (bf16[384,1024]{1,0:T(8,128)(2,1)S(1)}, bf16[384,1024]{1,0:T(8,128)(2,1)}, u32[]{:S(2)}, u32[]{:S(2)}) collective-permute-start(bf16[384,1024]{1,0:T(8,128)(2,1)S(1)} %fusion.36), channel_id=1, source_target_pairs={{0,14},{1,15},{2,0},{3,1},{4,2},{5,3},{6,4},{7,5},{8,6},{9,7},{10,... | collective-permute-start | bytes 2359304 | tf_op jit(solution)/shard_map/ppermute | solution.py:12
  72.4 0.8 copy-start.5
  73.3 35.2 %collective-permute-start.14 = (bf16[384,1024]{1,0:T(8,128)(2,1)S(1)}, bf16[384,1024]{1,0:T(8,128)(2,1)}, u32[]{:S(2)}, u32[]{:S(2)}) collective-permute-start(bf16[384,1024]{1,0:T(8,128)(2,1)S(1)} %fusion.36), channel_id=1, source_target_pairs={{0,16},{16,0},{1,17},{17,1},{2,18},{18,2},{3,19},{19,3},{4,20},{20... | collective-permute-start | bytes 2359304 | tf_op jit(solution)/shard_map/ppermute | solution.py:22
  74.8 25.6 %collective-permute-start.10 = (bf16[384,768]{1,0:T(8,128)(2,1)S(1)}, bf16[384,768]{1,0:T(8,128)(2,1)}, u32[]{:S(2)}, u32[]{:S(2)}) collective-permute-start(bf16[384,768]{1,0:T(8,128)(2,1)S(1)} %fusion.38), channel_id=1, source_target_pairs={{0,14},{1,15},{2,0},{3,1},{4,2},{5,3},{6,4},{7,5},{8,6},{9,7},{10,... | collective-permute-start | bytes 1769480 | tf_op jit(solution)/shard_map/ppermute | solution.py:12
  75.7 4.4 %copy-start.11 = (bf16[384,1024]{1,0:T(8,128)(2,1)}, bf16[384,1024]{1,0:T(8,128)(2,1)S(1)}, u32[]{:S(2)}) copy-start(bf16[384,1024]{1,0:T(8,128)(2,1)S(1)} %collective-permute-done.5) | copy-start | bytes 2359300
  75.7 32.7 %collective-permute-start.13 = (bf16[384,768]{1,0:T(8,128)(2,1)S(1)}, bf16[384,768]{1,0:T(8,128)(2,1)}, u32[]{:S(2)}, u32[]{:S(2)}) collective-permute-start(bf16[384,768]{1,0:T(8,128)(2,1)S(1)} %fusion.38), channel_id=1, source_target_pairs={{0,16},{16,0},{1,17},{17,1},{2,18},{18,2},{3,19},{19,3},{4,20},{20... | collective-permute-start | bytes 1769480 | tf_op jit(solution)/shard_map/ppermute | solution.py:22
  82.7 2.2 %copy-start.1 = (f32[384,768]{1,0:T(8,128)}, f32[384,768]{1,0:T(8,128)S(1)}, u32[]{:S(2)}) copy-start(f32[384,768]{1,0:T(8,128)S(1)} %get-tuple-element.107) | copy-start | bytes 3538948
  83.3 25.1 %collective-permute-start.12 = (bf16[384]{0:T(512)(128)(2,1)S(1)}, bf16[384]{0:T(512)(128)(2,1)S(1)}, u32[]{:S(2)}, u32[]{:S(2)}) collective-permute-start(bf16[384]{0:T(512)(128)(2,1)S(1)} %get-tuple-element.139), channel_id=1, source_target_pairs={{0,16},{16,0},{1,17},{17,1},{2,18},{18,2},{3,19},{19,3},{4,20},{20... | collective-permute-start | bytes 2312 | tf_op jit(solution)/shard_map/ppermute | solution.py:22
  84.9 1.8 %copy-start.8 = (bf16[384,768]{1,0:T(8,128)(2,1)S(1)}, bf16[384,768]{1,0:T(8,128)(2,1)}, u32[]{:S(2)}) copy-start(bf16[384,768]{1,0:T(8,128)(2,1)} %get-tuple-element.69) | copy-start | bytes 1769476 | tf_op jit(solution)/shard_map/cond
  90.9 9.6 %copy-start.2 = (f32[384,768]{1,0:T(8,128)}, f32[384,768]{1,0:T(8,128)S(1)}, u32[]{:S(2)}) copy-start(f32[384,768]{1,0:T(8,128)S(1)} %get-tuple-element.109) | copy-start | bytes 3538948
  115.1 1.0 copy-start.3
where the time goes:
time: 167 us; the launch traced here: 166 us
  starting transfers between devices  62.6 us (37%)
  blocking collectives  41.5 us (25%)
  waiting for transfers between devices  21.1 us (13%)
  matrix products  20.8 us (12%)
  between operations  7.79 us (5%)
  other arithmetic  6.53 us (4%)
  loops' own time  3.85 us (2%)
  local copies, waits for them, and re-layouts  2 us (1%)
    ppermute x12, starting transfers between devices, passed_along(): return lax.ppermute(value, axis, pairs)  59 us
    psum x1, blocking collectives, per_device(): loss_sum, weight_sum = lax.psum((loss_sum, weight_sum), ('group', 'member'))  41.5 us
    ppermute x12, waiting for transfers between devices, passed_along(): return lax.ppermute(value, axis, pairs)  21.1 us
    dot_general x4, matrix products, compute(): jnp.einsum('id,jd->ij', local_s, partner_s, preferred_element_type=jnp.fl...  7.63 us
    dot_general x4, matrix products, compute(): jnp.dot(coefficient, partner_s, preferred_element_type=jnp.float32)  7.31 us
    dot_general x4, matrix products, compute(): jnp.einsum('id,jd->ij', local_t, partner_t, preferred_element_type=jnp.fl...  5.82 us
    another operation x5, loops' own time, block_terms(): return lax.cond(switch > 0, compute, skipped, 0)  3.85 us
    ppermute x3, starting transfers between devices, partner_2(): return lax.ppermute(block, axis, route)  3.62 us
  transfers between devices with their start and end apart: 15, of which 3 were waited for; matrix products, arithmetic and copies ran while one was open for 9% of the time, Pallas kernels for 0%

commit v1 on v0

v1 whole, which is shorter than its diff:
```python
import functools

import jax
import jax.numpy as jnp
from jax import lax
from jax.experimental import pallas as pl
from jax.experimental.pallas import tpu as pltpu
from jax.sharding import PartitionSpec as P

EPS = 1e-06
AXES = ("group", "member")
F32 = jnp.float32
BF16 = jnp.bfloat16
OWN_NEAR, OWN_FAR, OWN_CROSS, OUTER_NEAR = range(4)


def units(raw):
    wide = raw.astype(F32)
    scale = lax.rsqrt(jnp.sum(wide * wide, axis=-1, keepdims=True) + EPS)
    return (wide * scale).astype(BF16), scale


def similarity(left, right):
    return lax.dot_general(left, right, (((1,), (1,)), ((), ())), preferred_element_type=F32)


def column(row):
    wide = jnp.broadcast_to(row, (128, row.shape[1]))
    return jnp.transpose(wide)[:, :1]


def lanes(values):
    row = jnp.sum(values, axis=0, keepdims=True)
    return sum(row[:, k : k + 128] for k in range(0, row.shape[1], 128))


def pair(left, right, weight_column, weight_row):
    mismatch = similarity(left[0], right[0]) - similarity(left[1], right[1])
    weight = weight_column * weight_row
    weighted = weight * mismatch
    return weighted.astype(BF16), lanes(weighted * mismatch), lanes(weight)


def tile(loss, weight):
    rows = lax.broadcasted_iota(jnp.int32, (8, 128), 0)
    zero = jnp.zeros((8, 128), F32)
    return jnp.where(rows == 0, loss, zero) + jnp.where(rows == 1, weight, zero)


def dot(left, right):
    return jnp.dot(left, right, preferred_element_type=F32)


def local_kernel(count, s, t, near_s, near_t, meta, near_meta, us, ut, near_us, near_ut, scale, total, sums):
    us[...], factor = units(s[...])
    ut[...], _ = units(t[...])
    near_us[...], _ = units(near_s[...])
    near_ut[...], _ = units(near_t[...])
    scale[...] = jnp.broadcast_to(factor, scale.shape)
    own_row = meta[:, :count]
    own = column(own_row)
    switch = meta[:, count + OWN_NEAR : count + OWN_NEAR + 1]
    here = (us[...], ut[...])
    coefficient, loss, weight = pair(here, here, own, own_row)
    total[...] = dot(coefficient, us[...])
    coefficient, loss_2, weight_2 = pair(here, (near_us[...], near_ut[...]), own, near_meta[:, :count] * switch)
    total[...] += dot(coefficient, near_us[...])
    sums[...] = tile(loss + loss_2, weight + weight_2)


def cross_kernel(count, us, ut, far_s, far_t, meta, far_meta, before, sums_before, total, sums):
    far_us, _ = units(far_s[...])
    far_ut, _ = units(far_t[...])
    switch = meta[:, count + OWN_CROSS : count + OWN_CROSS + 1]
    coefficient, loss, weight = pair(
        (us[...], ut[...]), (far_us, far_ut), column(meta[:, :count]), far_meta[:, :count] * switch
    )
    total[...] = before[...] + dot(coefficient, far_us)
    sums[...] = sums_before[...] + tile(loss, weight)


def ring_kernel(
    count, us, ut, near_us, near_ut, far_s, far_t, meta, near_meta, far_meta, before, sums_before,
    total, to_near, to_far, sums,
):
    far_us, _ = units(far_s[...])
    far_ut, _ = units(far_t[...])
    far = (far_us, far_ut)
    far_row = far_meta[:, :count]
    switch = meta[:, count + OWN_FAR : count + OWN_FAR + 1]
    coefficient, loss, weight = pair((us[...], ut[...]), far, column(meta[:, :count]), far_row * switch)
    total[...] = before[...] + dot(coefficient, far_us)
    to_far[...] = lax.dot_general(
        coefficient, us[...], (((0,), (0,)), ((), ())), preferred_element_type=F32
    ).astype(BF16)
    switch = near_meta[:, count + OUTER_NEAR : count + OUTER_NEAR + 1]
    coefficient, loss_2, weight_2 = pair(
        (near_us[...], near_ut[...]), far, column(near_meta[:, :count]), far_row * switch
    )
    to_near[...] = dot(coefficient, far_us).astype(BF16)
    sums[...] = sums_before[...] + tile(2.0 * loss + loss_2, 2.0 * weight + weight_2)


def final_kernel(us, scale, total, from_near, from_far, grad):
    unit = us[...].astype(F32)
    summed = total[...] + from_near[...].astype(F32) + from_far[...].astype(F32)
    along = jnp.sum(summed * unit, axis=-1, keepdims=True)
    grad[...] = 4.0 * scale[:, :1] * (summed - along * unit)


def call(kernel, outs, flops, *operands):
    size = sum(x.size * x.dtype.itemsize for x in operands)
    size += sum(x.size * x.dtype.itemsize for x in outs)
    return pl.pallas_call(
        kernel,
        out_shape=outs,
        compiler_params=pltpu.CompilerParams(vmem_limit_bytes=48 << 20),
        cost_estimate=pl.CostEstimate(flops=flops, bytes_accessed=size, transcendentals=0),
    )(*operands)


def per_device(student, teacher, counts, plan):
    groups, members = lax.axis_size("group"), lax.axis_size("member")
    rows, ds = student.shape
    dt = teacher.shape[1]

    def route(target):
        pairs = []
        for g in range(groups):
            for m in range(members):
                to_g, to_m = target(g, m)
                pairs.append((g * members + m, to_g * members + to_m % members))
        return functools.partial(lax.ppermute, axis_name=AXES, perm=pairs)

    to_ring = route(lambda g, m: (g, m - 2 + 4 * (m % 2)))
    back = route(lambda g, m: (g, m + 2 - 4 * (m % 2)))
    to_near = route(lambda g, m: (g, m ^ 1))
    to_cross = route(lambda g, m: (g ^ 1, m))

    odd = lax.axis_index("member") % 2
    switches = plan.reshape(-1).astype(F32)
    even_slots = jnp.stack([switches[i] for i in (2, 3, 4, 0)])
    odd_slots = jnp.stack([switches[i] for i in (0, 1, 4, 2)])
    slots = jnp.where(odd == 1, odd_slots, even_slots)
    meta = jnp.concatenate([counts.astype(F32), slots, jnp.zeros((124,), F32)]).reshape(1, rows + 128)

    ring_s, ring_t = to_ring(student), to_ring(teacher)
    cross_s, cross_t = to_cross(student), to_cross(teacher)
    near_s, near_t, near_meta = to_near(student), to_near(teacher), to_near(meta)
    ring_meta, cross_meta = to_ring(meta), to_cross(meta)

    f = jax.ShapeDtypeStruct
    sim = 2 * rows * rows * (ds + dt)
    mix = 2 * rows * rows * ds
    acc, sums_shape = f((rows, ds), F32), f((8, 128), F32)
    unit_s, unit_t = f((rows, ds), BF16), f((rows, dt), BF16)
    us, ut, near_us, near_ut, scale, total, sums = call(
        functools.partial(local_kernel, rows),
        (unit_s, unit_t, unit_s, unit_t, f((rows, 128), F32), acc, sums_shape),
        2 * (sim + mix),
        student, teacher, near_s, near_t, meta, near_meta,
    )
    total, sums = call(
        functools.partial(cross_kernel, rows),
        (acc, sums_shape),
        sim + mix,
        us, ut, cross_s, cross_t, meta, cross_meta, total, sums,
    )
    total, give_near, give_back, sums = call(
        functools.partial(ring_kernel, rows),
        (acc, unit_s, unit_s, sums_shape),
        2 * sim + 3 * mix,
        us, ut, near_us, near_ut, ring_s, ring_t, meta, near_meta, ring_meta, total, sums,
    )
    from_far = back(give_back)
    from_near = to_near(give_near)

    step = 1
    while step < members:
        sums = sums + route(lambda g, m: (g, m ^ step))(sums)
        step *= 2
    step = 1
    while step < groups:
        sums = sums + route(lambda g, m: (g ^ step, m))(sums)
        step *= 2
    loss = ds * jnp.sum(sums[0]) / jnp.sum(sums[1])

    (grad,) = call(final_kernel, (acc,), 0, us, scale, total, from_near, from_far)
    return grad, loss


def solution(mesh):
    return jax.shard_map(
        per_device,
        mesh=mesh,
        in_specs=(
            P(AXES, None),
            P(AXES, None),
            P(AXES),
            P("group", "member", None),
        ),
        out_specs=(P(AXES, None), P()),
        check_vma=False,
    )
```

time: 167 us -> 77.6 us (0.46)
  blocking collectives: 41.5 us -> 0 us
  starting transfers between devices: 62.6 us -> 21.7 us
  matrix products: 20.8 us -> 0 us
  Pallas kernels: 0 us -> 11 us
  waiting for transfers between devices: 21.1 us -> 29 us
  local copies, waits for them, and re-layouts: 2 us -> 8.31 us
  between operations: 7.79 us -> 3.17 us
  loops' own time: 3.85 us -> 0 us
  other arithmetic: 6.53 us -> 4.04 us
    psum x1 -> x0, blocking collectives: 41.5 us -> none  [per_device(): loss_sum, weight_sum = lax.psum((loss_sum, weight_sum), ('group', 'member'))]
    ppermute x15 -> x16, starting transfers between devices: 62.6 us -> 21.7 us  [the longest x2 6.29 us: per_device(): ring_meta, cross_meta = (to_ring(meta), to_cross(meta))]
    dot_general x12 -> x0, matrix products: 20.8 us -> none  [the longest x4 7.63 us: compute(): jnp.einsum('id,jd->ij', local_s, partner_s, preferred_element_type=jnp.fl...]
    pallas_call x0 -> x4, Pallas kernels: none -> 11 us  [call(): pl.pallas_call(kernel, out_shape=outs, compiler_params=pltpu.CompilerPara...]
    ppermute x15 -> x16, waiting for transfers between devices: 21.1 us -> 29 us  [the longest x4 15.3 us: per_device(): sums = sums + route(lambda g, m: (g, m ^ step))(sums)]
    unnamed x22 -> x14, local copies, waits for them, and re-layouts: 1.19 us -> 7.62 us
    reduce_sum x3 -> x1, other arithmetic: 4.84 us -> 0.61 us  [per_device(): loss = ds * jnp.sum(sums[0]) / jnp.sum(sums[1])]
    another operation x5 -> x0, loops' own time: 3.85 us -> none  [block_terms(): return lax.cond(switch > 0, compute, skipped, 0)]
  transfers between devices with their start and end apart: 15 -> 16, of which waited for: 3 -> 7; matrix products, arithmetic and copies ran while one was open for 9% -> 6% of each run, Pallas kernels for 0% -> 7%
where the time goes in v1:
time: 77.6 us; the launch traced here: 77.2 us
  waiting for transfers between devices  29 us (37%)
  starting transfers between devices  21.7 us (28%)
  Pallas kernels  11 us (14%)
  local copies, waits for them, and re-layouts  8.31 us (11%)
  other arithmetic  4.04 us (5%)
  between operations  3.17 us (4%)
    ppermute x4, waiting for transfers between devices, per_device(): sums = sums + route(lambda g, m: (g, m ^ step))(sums)  15.3 us
    pallas_call x4, Pallas kernels, call(): pl.pallas_call(kernel, out_shape=outs, compiler_params=pltpu.CompilerPara...  11 us
    ppermute x2, waiting for transfers between devices, per_device(): ring_meta, cross_meta = (to_ring(meta), to_cross(meta))  10.8 us
    unnamed x14, local copies, waits for them, and re-layouts  7.62 us
    ppermute x2, starting transfers between devices, per_device(): ring_meta, cross_meta = (to_ring(meta), to_cross(meta))  6.29 us
    ppermute x2, starting transfers between devices, per_device(): ring_s, ring_t = (to_ring(student), to_ring(teacher))  5.06 us
    ppermute x4, starting transfers between devices, per_device(): sums = sums + route(lambda g, m: (g, m ^ step))(sums)  4.66 us
    ppermute x2, starting transfers between devices, per_device(): cross_s, cross_t = (to_cross(student), to_cross(teacher))  3.1 us
  transfers between devices with their start and end apart: 16, of which 7 were waited for; matrix products, arithmetic and copies ran while one was open for 6% of the time, Pallas kernels for 7%

profile of v1, /device:TPU:0, one launch (start us, length us, event | category | flops | bytes accessed | tf_op | source)
XLA Modules:
  0.0 77.2 jit_solution(5865251176131605391)
XLA Ops:
  0.6 0.5 collective-permute-start.1
  1.1 2.6 %collective-permute-start.7 = (bf16[384,1024]{1,0:T(8,128)(2,1)}, bf16[384,1024]{1,0:T(8,128)(2,1)S(1)}, u32[]{:S(2)}, u32[]{:S(2)}) collective-permute-start(bf16[384,1024]{1,0:T(8,128)(2,1)} %t.1), channel_id=1, source_target_pairs={{0,16},{1,17},{2,18},{3,19},{4,20},{5,21},{6,22},{7,23},{8,24},{9,... | collective-permute-start | bytes 2359304 | tf_op jit(solution)/shard_map/ppermute | solution.py:148
  3.7 4.5 %collective-permute-start.4 = (bf16[384,1024]{1,0:T(8,128)(2,1)}, bf16[384,1024]{1,0:T(8,128)(2,1)S(1)}, u32[]{:S(2)}, u32[]{:S(2)}) collective-permute-start(bf16[384,1024]{1,0:T(8,128)(2,1)} %t.1), channel_id=1, source_target_pairs={{0,14},{1,3},{2,0},{3,5},{4,2},{5,7},{6,4},{7,9},{8,6},{9,11},{10,... | collective-permute-start | bytes 2359304 | tf_op jit(solution)/shard_map/ppermute | solution.py:147
  8.3 0.7 convert_element_type.8
  9.0 0.6 fusion
  9.6 2.0 %broadcast_select_fusion = f32[4]{0:T(128)S(1)} fusion(pred[]{:T(512)S(6)} %eq.5, f32[1]{0:T(128)} %bitcast.2, f32[1]{0:T(128)} %bitcast.1, f32[2]{0:T(128)S(1)} %slice_bitcast_fusion.1, f32[1]{0:T(128)} %bitcast.4, f32[3]{0:T(128)S(1)} %slice_bitcast_fusion), kind=kLoop, calls=%fused_computation.1 | loop fusion | flops 16 | bytes 49 | tf_op jit(solution)/shard_map/jit(_where)/select_n | solution.py:144
  11.6 0.7 convert_element_type.7
  12.9 0.8 %collective-permute-done.2.near_meta = f32[1,512]{1,0:T(1,128)S(1)} collective-permute-done((f32[1,512]{1,0:T(1,128)S(1)}, f32[1,512]{1,0:T(1,128)S(1)}, u32[]{:S(2)}, u32[]{:S(2)}) %collective-permute-start.2) | collective-permute-done | bytes 2080 | tf_op jit(solution)/shard_map/ppermute | solution.py:149
  14.2 0.8 %copy-done.5 = bf16[384,768]{1,0:T(8,128)(2,1)} copy-done((bf16[384,768]{1,0:T(8,128)(2,1)}, bf16[384,768]{1,0:T(8,128)(2,1)S(1)}, u32[]{:S(2)}) %copy-start.5) | copy-done | bytes 589848
  15.0 0.5 collective-permute-start.3
  15.6 1.5 %collective-permute-start.8 = (f32[1,512]{1,0:T(1,128)S(1)}, f32[1,512]{1,0:T(1,128)S(1)}, u32[]{:S(2)}, u32[]{:S(2)}) collective-permute-start(f32[1,512]{1,0:T(1,128)S(1)} %bitcast.9), channel_id=1, source_target_pairs={{0,16},{1,17},{2,18},{3,19},{4,20},{5,21},{6,22},{7,23},{8,24},{9,... | collective-permute-start | bytes 6152 | tf_op jit(solution)/shard_map/ppermute | solution.py:150
  17.1 1.1 %copy-done.3 = bf16[384,1024]{1,0:T(8,128)(2,1)S(1)} copy-done((bf16[384,1024]{1,0:T(8,128)(2,1)S(1)}, bf16[384,1024]{1,0:T(8,128)(2,1)}, u32[]{:S(2)}) %copy-start.3) | copy-done | bytes 786456
  18.2 1.1 %copy-done.4 = bf16[384,768]{1,0:T(8,128)(2,1)S(1)} copy-done((bf16[384,768]{1,0:T(8,128)(2,1)S(1)}, bf16[384,768]{1,0:T(8,128)(2,1)}, u32[]{:S(2)}) %copy-start.4) | copy-done | bytes 589848
  19.3 1.1 %copy-done.6 = bf16[384,768]{1,0:T(8,128)(2,1)S(1)} copy-done((bf16[384,768]{1,0:T(8,128)(2,1)S(1)}, bf16[384,768]{1,0:T(8,128)(2,1)}, u32[]{:S(2)}) %copy-start.6) | copy-done | bytes 589848
  20.4 3.7 %shard_map.59 = (bf16[384,768]{1,0:T(8,128)(2,1)S(1)}, bf16[384,1024]{1,0:T(8,128)(2,1)S(1)}, bf16[384,768]{1,0:T(8,128)(2,1)S(1)}, bf16[384,1024]{1,0:T(8,128)(...) custom-call(bf16[384,768]{1,0:T(8,128)(2,1)S(1)} %copy-done.4, ...), custom_call_target="tpu_custom_call" | custom-call | flops 1509949440 | bytes 6889472 | tf_op jit(solution)/shard_map/pallas_call | solution.py:114
  24.0 10.8 %collective-permute-done.8.far_meta = f32[1,512]{1,0:T(1,128)S(1)} collective-permute-done((f32[1,512]{1,0:T(1,128)S(1)}, f32[1,512]{1,0:T(1,128)S(1)}, u32[]{:S(2)}, u32[]{:S(2)}) %collective-permute-start.8) | collective-permute-done | bytes 2080 | tf_op jit(solution)/shard_map/ppermute | solution.py:150
  34.8 4.8 %collective-permute-start.5 = (f32[1,512]{1,0:T(1,128)S(1)}, f32[1,512]{1,0:T(1,128)S(1)}, u32[]{:S(2)}, u32[]{:S(2)}) collective-permute-start(f32[1,512]{1,0:T(1,128)S(1)} %bitcast.11), channel_id=1, source_target_pairs={{0,14},{1,3},{2,0},{3,5},{4,2},{5,7},{6,4},{7,9},{8,6},{9,11},{10,... | collective-permute-start | bytes 6152 | tf_op jit(solution)/shard_map/ppermute | solution.py:150
  39.5 1.3 %copy-done.1 = f32[384,768]{1,0:T(8,128)S(1)} copy-done((f32[384,768]{1,0:T(8,128)S(1)}, f32[384,768]{1,0:T(8,128)}, u32[]{:S(2)}) %copy-start.1) | copy-done | bytes 1179672
  40.8 1.4 %shard_map.60 = (f32[384,768]{1,0:T(8,128)S(1)}, f32[8,128]{1,0:T(8,128)S(1)}) custom-call(bf16[384,768]{1,0:T(8,128)(2,1)S(1)} %get-tuple-element.15.us, bf16[384,1024]{1,0:T(8,128)(2,1)S(1)} %get-tuple-element.17.ut, bf16[384,768]{1,0:T(8,128)(2,1)S(1)} %collective-permute-done.6.far_s, bf16[384,1024]{1,0:T(8,128)(2,1)S(1)} %collective-permute-done.7.far_t, ...), custom_call_target="tpu_custom_call" | custom-call | flops 754974720 | bytes 5124096 | tf_op jit(solution)/shard_map/pallas_call | solution.py:114
  42.3 1.0 %copy-done.2 = f32[384,768]{1,0:T(8,128)} copy-done((f32[384,768]{1,0:T(8,128)}, f32[384,768]{1,0:T(8,128)S(1)}, u32[]{:S(2)}) %copy-start.2) | copy-done | bytes 1179672
  43.3 4.3 %shard_map.61 = (f32[384,768]{1,0:T(8,128)}, bf16[384,768]{1,0:T(8,128)(2,1)S(1)}, bf16[384,768]{1,0:T(8,128)(2,1)}, f32[8,128]{1,0:T(8,128)S(1)}) custom-call(bf16[384,768]{1,0:T(8,128)(2,1)S(1)} %get-tuple-element.15.us, bf16[384,1024]{1,0:T(8,128)(2,1)S(1)} %get-tuple-element.17.ut, bf16[384,768]{1,0:T(8,128)(2,1)S(1)} %get-tuple-element.18.near_us, ...), custom_call_target="tpu_custom_call" | custom-call | flops 1736441856 | bytes 7682048 | tf_op jit(solution)/shard_map/pallas_call | solution.py:114
  48.1 1.5 %collective-permute-done.11 = f32[8,128]{1,0:T(8,128)S(1)} collective-permute-done((f32[8,128]{1,0:T(8,128)S(1)}, f32[8,128]{1,0:T(8,128)S(1)}, u32[]{:S(2)}, u32[]{:S(2)}) %collective-permute-start.11) | collective-permute-done | bytes 4128 | tf_op jit(solution)/shard_map/ppermute | solution.py:180
  49.6 9.9 %collective-permute-done.12 = f32[8,128]{1,0:T(8,128)S(1)} collective-permute-done((f32[8,128]{1,0:T(8,128)S(1)}, f32[8,128]{1,0:T(8,128)S(1)}, u32[]{:S(2)}, u32[]{:S(2)}) %collective-permute-start.12) | collective-permute-done | bytes 4128 | tf_op jit(solution)/shard_map/ppermute | solution.py:180
  59.5 1.5 %collective-permute-start.13 = (f32[8,128]{1,0:T(8,128)S(1)}, f32[8,128]{1,0:T(8,128)S(1)}, u32[]{:S(2)}, u32[]{:S(2)}) collective-permute-start(f32[8,128]{1,0:T(8,128)S(1)} %add.21), channel_id=1, source_target_pairs={{0,4},{1,5},{2,6},{3,7},{4,0},{5,1},{6,2},{7,3},{8,12},{9,13},{10,... | collective-permute-start | bytes 12296 | tf_op jit(solution)/shard_map/ppermute | solution.py:180
  61.0 2.1 %collective-permute-done.13 = f32[8,128]{1,0:T(8,128)S(1)} collective-permute-done((f32[8,128]{1,0:T(8,128)S(1)}, f32[8,128]{1,0:T(8,128)S(1)}, u32[]{:S(2)}, u32[]{:S(2)}) %collective-permute-start.13) | collective-permute-done | bytes 4128 | tf_op jit(solution)/shard_map/ppermute | solution.py:180
  63.1 2.7 %collective-permute-start.14 = (f32[8,128]{1,0:T(8,128)S(1)}, f32[8,128]{1,0:T(8,128)S(1)}, u32[]{:S(2)}, u32[]{:S(2)}) collective-permute-start(f32[8,128]{1,0:T(8,128)S(1)} %add.22), channel_id=1, source_target_pairs={{0,8},{1,9},{2,10},{3,11},{4,12},{5,13},{6,14},{7,15},{8,0},{9,1},... | collective-permute-start | bytes 12296 | tf_op jit(solution)/shard_map/ppermute | solution.py:180
  65.8 1.8 %collective-permute-done.14 = f32[8,128]{1,0:T(8,128)S(1)} collective-permute-done((f32[8,128]{1,0:T(8,128)S(1)}, f32[8,128]{1,0:T(8,128)S(1)}, u32[]{:S(2)}, u32[]{:S(2)}) %collective-permute-start.14) | collective-permute-done | bytes 4128 | tf_op jit(solution)/shard_map/ppermute | solution.py:180
  67.6 1.5 %collective-permute-start.15 = (f32[8,128]{1,0:T(8,128)S(1)}, f32[8,128]{1,0:T(8,128)S(1)}, u32[]{:S(2)}, u32[]{:S(2)}) collective-permute-start(f32[8,128]{1,0:T(8,128)S(1)} %add.23), channel_id=1, source_target_pairs={{0,16},{1,17},{2,18},{3,19},{4,20},{5,21},{6,22},{7,23},{8,24},{9,... | collective-permute-start | bytes 12296 | tf_op jit(solution)/shard_map/ppermute | solution.py:184
  69.2 2.1 %collective-permute-done.15 = f32[8,128]{1,0:T(8,128)S(1)} collective-permute-done((f32[8,128]{1,0:T(8,128)S(1)}, f32[8,128]{1,0:T(8,128)S(1)}, u32[]{:S(2)}, u32[]{:S(2)}) %collective-permute-start.15) | collective-permute-done | bytes 4128 | tf_op jit(solution)/shard_map/ppermute | solution.py:184
  71.2 0.6 slice_reduce_fusion
  73.2 1.3 %copy-done = f32[384,768]{1,0:T(8,128)S(1)} copy-done((f32[384,768]{1,0:T(8,128)S(1)}, f32[384,768]{1,0:T(8,128)}, u32[]{:S(2)}) %copy-start) | copy-done | bytes 1179672
  74.5 1.5 %shard_map.62 = f32[384,768]{1,0:T(8,128)} custom-call(bf16[384,768]{1,0:T(8,128)(2,1)S(1)} %get-tuple-element.15.us, f32[384,128]{1,0:T(8,128)S(1)} %get-tuple-element.16.scale, f32[384,768]{1,0:T(8,128)S(1)} %copy-done, bf16[384,768]{1,0:T(8,128)(2,1)S(1)} %collective-permute-done.9.from_near, bf16[384,768]{1,0:T(8,128)(2,1)S(1)} %collective-permute-done.10.from_far), custom_call_target="tpu_custom_call" | custom-call | bytes 4325376 | tf_op jit(solution)/shard_map/pallas_call | solution.py:114
  (32 shorter events, 1.7 us)
Async XLA Ops:
  0.6 15.0 %collective-permute-start.1 = (bf16[384,1024]{1,0:T(8,128)(2,1)}, bf16[384,1024]{1,0:T(8,128)(2,1)S(1)}, u32[]{:S(2)}, u32[]{:S(2)}) collective-permute-start(bf16[384,1024]{1,0:T(8,128)(2,1)} %t.1), channel_id=1, source_target_pairs={{0,1},{1,0},{2,3},{3,2},{4,5},{5,4},{6,7},{7,6},{8,9},{9,8},{10,11... | collective-permute-start | bytes 2359304 | tf_op jit(solution)/shard_map/ppermute | solution.py:149
  1.1 38.4 %collective-permute-start.7 = (bf16[384,1024]{1,0:T(8,128)(2,1)}, bf16[384,1024]{1,0:T(8,128)(2,1)S(1)}, u32[]{:S(2)}, u32[]{:S(2)}) collective-permute-start(bf16[384,1024]{1,0:T(8,128)(2,1)} %t.1), channel_id=1, source_target_pairs={{0,16},{1,17},{2,18},{3,19},{4,20},{5,21},{6,22},{7,23},{8,24},{9,... | collective-permute-start | bytes 2359304 | tf_op jit(solution)/shard_map/ppermute | solution.py:148
  3.7 39.5 %collective-permute-start.4 = (bf16[384,1024]{1,0:T(8,128)(2,1)}, bf16[384,1024]{1,0:T(8,128)(2,1)S(1)}, u32[]{:S(2)}, u32[]{:S(2)}) collective-permute-start(bf16[384,1024]{1,0:T(8,128)(2,1)} %t.1), channel_id=1, source_target_pairs={{0,14},{1,3},{2,0},{3,5},{4,2},{5,7},{6,4},{7,9},{8,6},{9,11},{10,... | collective-permute-start | bytes 2359304 | tf_op jit(solution)/shard_map/ppermute | solution.py:147
  8.3 6.0 %collective-permute-start = (bf16[384,768]{1,0:T(8,128)(2,1)}, bf16[384,768]{1,0:T(8,128)(2,1)S(1)}, u32[]{:S(2)}, u32[]{:S(2)}) collective-permute-start(bf16[384,768]{1,0:T(8,128)(2,1)} %s.1), channel_id=1, source_target_pairs={{0,1},{1,0},{2,3},{3,2},{4,5},{5,4},{6,7},{7,6},{8,9},{9,8},{10,11... | collective-permute-start | bytes 1769480 | tf_op jit(solution)/shard_map/ppermute | solution.py:149
  12.4 1.3 %collective-permute-start.2 = (f32[1,512]{1,0:T(1,128)S(1)}, f32[1,512]{1,0:T(1,128)S(1)}, u32[]{:S(2)}, u32[]{:S(2)}) collective-permute-start(f32[1,512]{1,0:T(1,128)S(1)} %bitcast.8), channel_id=1, source_target_pairs={{0,1},{1,0},{2,3},{3,2},{4,5},{5,4},{6,7},{7,6},{8,9},{9,8},{10,11... | collective-permute-start | bytes 6152 | tf_op jit(solution)/shard_map/ppermute | solution.py:149
  13.7 25.8 %collective-permute-start.6 = (bf16[384,768]{1,0:T(8,128)(2,1)}, bf16[384,768]{1,0:T(8,128)(2,1)S(1)}, u32[]{:S(2)}, u32[]{:S(2)}) collective-permute-start(bf16[384,768]{1,0:T(8,128)(2,1)} %s.1), channel_id=1, source_target_pairs={{0,16},{1,17},{2,18},{3,19},{4,20},{5,21},{6,22},{7,23},{8,24},{9,... | collective-permute-start | bytes 1769480 | tf_op jit(solution)/shard_map/ppermute | solution.py:148
  14.2 0.8 %copy-start.5 = (bf16[384,768]{1,0:T(8,128)(2,1)}, bf16[384,768]{1,0:T(8,128)(2,1)S(1)}, u32[]{:S(2)}) copy-start(bf16[384,768]{1,0:T(8,128)(2,1)S(1)} %collective-permute-done.near_s) | copy-start | bytes 1769476
  15.0 28.2 %collective-permute-start.3 = (bf16[384,768]{1,0:T(8,128)(2,1)}, bf16[384,768]{1,0:T(8,128)(2,1)S(1)}, u32[]{:S(2)}, u32[]{:S(2)}) collective-permute-start(bf16[384,768]{1,0:T(8,128)(2,1)} %s.1), channel_id=1, source_target_pairs={{0,14},{1,3},{2,0},{3,5},{4,2},{5,7},{6,4},{7,9},{8,6},{9,11},{10,... | collective-permute-start | bytes 1769480 | tf_op jit(solution)/shard_map/ppermute | solution.py:147
  15.6 19.2 %collective-permute-start.8 = (f32[1,512]{1,0:T(1,128)S(1)}, f32[1,512]{1,0:T(1,128)S(1)}, u32[]{:S(2)}, u32[]{:S(2)}) collective-permute-start(f32[1,512]{1,0:T(1,128)S(1)} %bitcast.9), channel_id=1, source_target_pairs={{0,16},{1,17},{2,18},{3,19},{4,20},{5,21},{6,22},{7,23},{8,24},{9,... | collective-permute-start | bytes 6152 | tf_op jit(solution)/shard_map/ppermute | solution.py:150
  17.1 1.1 %copy-start.3 = (bf16[384,1024]{1,0:T(8,128)(2,1)S(1)}, bf16[384,1024]{1,0:T(8,128)(2,1)}, u32[]{:S(2)}) copy-start(bf16[384,1024]{1,0:T(8,128)(2,1)} %t.1) | copy-start | bytes 2359300
  18.2 1.1 %copy-start.4 = (bf16[384,768]{1,0:T(8,128)(2,1)S(1)}, bf16[384,768]{1,0:T(8,128)(2,1)}, u32[]{:S(2)}) copy-start(bf16[384,768]{1,0:T(8,128)(2,1)} %s.1) | copy-start | bytes 1769476
  19.3 1.1 %copy-start.6 = (bf16[384,768]{1,0:T(8,128)(2,1)S(1)}, bf16[384,768]{1,0:T(8,128)(2,1)}, u32[]{:S(2)}) copy-start(bf16[384,768]{1,0:T(8,128)(2,1)} %copy-done.5) | copy-start | bytes 1769476
  34.8 8.5 %collective-permute-start.5 = (f32[1,512]{1,0:T(1,128)S(1)}, f32[1,512]{1,0:T(1,128)S(1)}, u32[]{:S(2)}, u32[]{:S(2)}) collective-permute-start(f32[1,512]{1,0:T(1,128)S(1)} %bitcast.11), channel_id=1, source_target_pairs={{0,14},{1,3},{2,0},{3,5},{4,2},{5,7},{6,4},{7,9},{8,6},{9,11},{10,... | collective-permute-start | bytes 6152 | tf_op jit(solution)/shard_map/ppermute | solution.py:150
  39.5 1.3 %copy-start.1 = (f32[384,768]{1,0:T(8,128)S(1)}, f32[384,768]{1,0:T(8,128)}, u32[]{:S(2)}) copy-start(f32[384,768]{1,0:T(8,128)} %get-tuple-element.20.before) | copy-start | bytes 3538948
  42.2 1.0 %copy-start.2 = (f32[384,768]{1,0:T(8,128)}, f32[384,768]{1,0:T(8,128)S(1)}, u32[]{:S(2)}) copy-start(f32[384,768]{1,0:T(8,128)S(1)} %get-tuple-element.22.before) | copy-start | bytes 3538948
  47.6 25.6 %collective-permute-start.10 = (bf16[384,768]{1,0:T(8,128)(2,1)}, bf16[384,768]{1,0:T(8,128)(2,1)S(1)}, u32[]{:S(2)}, u32[]{:S(2)}) collective-permute-start(bf16[384,768]{1,0:T(8,128)(2,1)} %get-tuple-element.26), channel_id=1, source_target_pairs={{0,2},{1,15},{2,4},{3,1},{4,6},{5,3},{6,8},{7,5},{8,10},{9,7},{10,... | collective-permute-start | bytes 1769480 | tf_op jit(solution)/shard_map/ppermute | solution.py:175
  47.6 25.6 %collective-permute-start.9 = (bf16[384,768]{1,0:T(8,128)(2,1)S(1)}, bf16[384,768]{1,0:T(8,128)(2,1)S(1)}, u32[]{:S(2)}, u32[]{:S(2)}) collective-permute-start(bf16[384,768]{1,0:T(8,128)(2,1)S(1)} %get-tuple-element.25), channel_id=1, source_target_pairs={{0,1},{1,0},{2,3},{3,2},{4,5},{5,4},{6,7},{7,6},{8,9},{9,8},{10,11... | collective-permute-start | bytes 1769480 | tf_op jit(solution)/shard_map/ppermute | solution.py:176
  47.6 2.0 %collective-permute-start.11 = (f32[8,128]{1,0:T(8,128)S(1)}, f32[8,128]{1,0:T(8,128)S(1)}, u32[]{:S(2)}, u32[]{:S(2)}) collective-permute-start(f32[8,128]{1,0:T(8,128)S(1)} %get-tuple-element.27), channel_id=1, source_target_pairs={{0,1},{1,0},{2,3},{3,2},{4,5},{5,4},{6,7},{7,6},{8,9},{9,8},{10,11... | collective-permute-start | bytes 12296 | tf_op jit(solution)/shard_map/ppermute | solution.py:180
  49.6 9.9 %collective-permute-start.12 = (f32[8,128]{1,0:T(8,128)S(1)}, f32[8,128]{1,0:T(8,128)S(1)}, u32[]{:S(2)}, u32[]{:S(2)}) collective-permute-start(f32[8,128]{1,0:T(8,128)S(1)} %add.20), channel_id=1, source_target_pairs={{0,2},{1,3},{2,0},{3,1},{4,6},{5,7},{6,4},{7,5},{8,10},{9,11},{10,... | collective-permute-start | bytes 12296 | tf_op jit(solution)/shard_map/ppermute | solution.py:180
  59.5 3.6 %collective-permute-start.13 = (f32[8,128]{1,0:T(8,128)S(1)}, f32[8,128]{1,0:T(8,128)S(1)}, u32[]{:S(2)}, u32[]{:S(2)}) collective-permute-start(f32[8,128]{1,0:T(8,128)S(1)} %add.21), channel_id=1, source_target_pairs={{0,4},{1,5},{2,6},{3,7},{4,0},{5,1},{6,2},{7,3},{8,12},{9,13},{10,... | collective-permute-start | bytes 12296 | tf_op jit(solution)/shard_map/ppermute | solution.py:180
  63.1 4.5 %collective-permute-start.14 = (f32[8,128]{1,0:T(8,128)S(1)}, f32[8,128]{1,0:T(8,128)S(1)}, u32[]{:S(2)}, u32[]{:S(2)}) collective-permute-start(f32[8,128]{1,0:T(8,128)S(1)} %add.22), channel_id=1, source_target_pairs={{0,8},{1,9},{2,10},{3,11},{4,12},{5,13},{6,14},{7,15},{8,0},{9,1},... | collective-permute-start | bytes 12296 | tf_op jit(solution)/shard_map/ppermute | solution.py:180
  67.6 3.6 %collective-permute-start.15 = (f32[8,128]{1,0:T(8,128)S(1)}, f32[8,128]{1,0:T(8,128)S(1)}, u32[]{:S(2)}, u32[]{:S(2)}) collective-permute-start(f32[8,128]{1,0:T(8,128)S(1)} %add.23), channel_id=1, source_target_pairs={{0,16},{1,17},{2,18},{3,19},{4,20},{5,21},{6,22},{7,23},{8,24},{9,... | collective-permute-start | bytes 12296 | tf_op jit(solution)/shard_map/ppermute | solution.py:184
  73.2 1.3 %copy-start = (f32[384,768]{1,0:T(8,128)S(1)}, f32[384,768]{1,0:T(8,128)}, u32[]{:S(2)}) copy-start(f32[384,768]{1,0:T(8,128)} %get-tuple-element.24.total) | copy-start | bytes 3538948

commit v2 on v1

v2 whole, which is shorter than its diff:
```python
import functools

import jax
import jax.numpy as jnp
from jax import lax
from jax.experimental import pallas as pl
from jax.experimental.pallas import tpu as pltpu
from jax.sharding import PartitionSpec as P

EPS = 1e-06
AXES = ("group", "member")
F32 = jnp.float32
BF16 = jnp.bfloat16
META, RING_META = 8, 16
PIECES = 4


def units(raw):
    wide = raw.astype(F32)
    scale = lax.rsqrt(jnp.sum(wide * wide, axis=-1, keepdims=True) + EPS)
    return (wide * scale).astype(BF16), scale


def similarity(left, right):
    return lax.dot_general(left, right, (((1,), (1,)), ((), ())), preferred_element_type=F32)


def dot(left, right):
    return jnp.dot(left, right, preferred_element_type=F32)


def dot_transposed(left, right):
    return lax.dot_general(left, right, (((0,), (0,)), ((), ())), preferred_element_type=F32)


def column(row):
    wide = jnp.broadcast_to(row, (128, row.shape[1]))
    return jnp.transpose(wide)[:, :1]


def lanes(values):
    row = jnp.sum(values, axis=0, keepdims=True)
    return sum(row[:, k : k + 128] for k in range(0, row.shape[1], 128))


def weigh(mismatch, weight_column, weight_row):
    weight = weight_column * weight_row
    weighted = weight * mismatch
    return weighted.astype(BF16), lanes(weighted * mismatch), lanes(weight)


def tile(loss, weight):
    rows = lax.broadcasted_iota(jnp.int32, (8, 128), 0)
    zero = jnp.zeros((8, 128), F32)
    return jnp.where(rows == 0, loss, zero) + jnp.where(rows == 1, weight, zero)


class Packed:
    def __init__(self, ref, rows, ds):
        self.ref, self.rows, self.ds = ref, rows, ds

    @property
    def s(self):
        return self.ref[: self.rows, : self.ds]

    @property
    def t(self):
        return self.ref[: self.rows, self.ds :]

    def meta(self):
        return self.ref[self.rows :, : self.ds].astype(F32)

    def counts(self):
        return self.meta()[0:1, : self.rows]

    def switch(self, if_even, if_odd):
        odd = lax.axis_index("member") % 2 == 1
        plan = self.meta()[1:2, :128]
        return jnp.where(odd, plan[:, if_odd : if_odd + 1], plan[:, if_even : if_even + 1])


def pack_kernel(counts_hbm, plan_hbm, s_hbm, t_hbm, both, ring, scale, counts, plan, s, t, arrived):
    rows, ds = s.shape
    pieces = [pl.ds(i * (rows // PIECES), rows // PIECES) for i in range(PIECES)]
    copies = [
        pltpu.make_async_copy(source.at[piece], target.at[piece], arrived.at[i, k])
        for i, piece in enumerate(pieces)
        for k, (source, target) in enumerate(((s_hbm, s), (t_hbm, t)))
    ]
    small = [
        pltpu.make_async_copy(source, target, arrived.at[PIECES, k])
        for k, (source, target) in enumerate(((counts_hbm, counts), (plan_hbm, plan)))
    ]
    for copy in copies + small:
        copy.start()
    for i, piece in enumerate(pieces):
        copies[2 * i].wait()
        unit, factor = units(s[piece])
        scale[piece] = jnp.broadcast_to(factor, (rows // PIECES, 128))
        both[piece, :ds] = unit
        ring[piece, :ds] = unit
        copies[2 * i + 1].wait()
        unit, _ = units(t[piece])
        both[piece, ds:] = unit
        ring[piece, ds:] = unit

    def widen(values):
        return jnp.concatenate([values, jnp.zeros((1, ds - values.shape[1]), F32)], axis=1)

    for copy in small:
        copy.wait()
    at = lax.broadcasted_iota(jnp.int32, (RING_META, ds), 0)
    meta = jnp.where(at == 0, widen(counts[...].astype(F32).reshape(1, rows)), 0.0)
    meta = jnp.where(at == 1, widen(plan[...].astype(F32)), meta).astype(BF16)
    both[rows:, :ds] = meta[:META]
    ring[rows:, :ds] = meta
    both[rows:, ds:] = jnp.zeros((META, t.shape[1]), BF16)
    ring[rows:, ds:] = jnp.zeros((RING_META, t.shape[1]), BF16)


def local_kernel(rows, ds, own, near, total, sums):
    own, near = Packed(own, rows, ds), Packed(near, rows, ds)
    own_column = column(own.counts())
    mismatch = similarity(own.s, own.s) - similarity(own.t, own.t)
    coefficient, loss, weight = weigh(mismatch, own_column, own.counts())
    total[...] = dot(coefficient, own.s)
    mismatch = similarity(own.s, near.s) - similarity(own.t, near.t)
    coefficient, loss_2, weight_2 = weigh(mismatch, own_column, near.counts() * own.switch(2, 0))
    total[...] += dot(coefficient, near.s)
    sums[...] = tile(loss + loss_2, weight + weight_2)


def cross_kernel(rows, ds, own, far, before, sums_before, total, give, sums):
    own, far = Packed(own, rows, ds), Packed(far, rows, ds)
    mismatch = similarity(own.s, far.s) - similarity(own.t, far.t)
    coefficient, loss, weight = weigh(mismatch, column(own.counts()), far.counts() * own.switch(4, 4))
    give[...] = dot_transposed(coefficient, own.s).astype(BF16)
    total[...] = before[...] + dot(coefficient, far.s)
    sums[...] = sums_before[...] + tile(2.0 * loss, 2.0 * weight)


def ring_kernel(rows, ds, own, near, far, coefficients, near_coefficients, sums):
    own, near, far = Packed(own, rows, ds), Packed(near, rows, ds), Packed(far, rows, ds)
    mismatch = similarity(own.s, far.s) - similarity(own.t, far.t)
    coefficients[...], loss, weight = weigh(mismatch, column(own.counts()), far.counts() * own.switch(3, 1))
    mismatch = similarity(near.s, far.s) - similarity(near.t, far.t)
    near_coefficients[...], loss_2, weight_2 = weigh(
        mismatch, column(near.counts()), far.counts() * near.switch(2, 0)
    )
    sums[...] = tile(2.0 * loss + loss_2, 2.0 * weight + weight_2)


def ring_mix_kernel(rows, ds, own, far, coefficients, near_coefficients, total, to_near, to_far):
    own, far = Packed(own, rows, ds), Packed(far, rows, ds)
    to_far[...] = dot_transposed(coefficients[...], own.s).astype(BF16)
    to_near[...] = dot(near_coefficients[...], far.s).astype(BF16)
    total[...] = dot(coefficients[...], far.s)


def final_kernel(rows, ds, own, scale, total, ring_total, from_near, from_far, from_cross, grad):
    unit = Packed(own, rows, ds).s.astype(F32)
    received = from_near[...].astype(F32) + from_far[...].astype(F32) + from_cross[...].astype(F32)
    summed = total[...] + ring_total[...] + received
    along = jnp.sum(summed * unit, axis=-1, keepdims=True)
    grad[...] = 4.0 * scale[:, :1] * (summed - along * unit)


def loss_kernel(width, sums, loss):
    total = jnp.sum(sums[...], axis=1, keepdims=True)
    loss[...] = width * total[0:1] / total[1:2]


def call(kernel, outs, vmem_mib, *operands, flops=0, **options):
    return pl.pallas_call(
        kernel,
        out_shape=outs,
        compiler_params=pltpu.CompilerParams(vmem_limit_bytes=vmem_mib << 20),
        cost_estimate=pl.CostEstimate(flops=flops, bytes_accessed=0, transcendentals=0),
        **options,
    )(*operands)


def powers(first, end):
    return [first << i for i in range(end.bit_length()) if first << i < end]


def per_device(student, teacher, counts, plan):
    groups, members = lax.axis_size("group"), lax.axis_size("member")
    rows, ds = student.shape
    dt = teacher.shape[1]

    def route(target):
        pairs = []
        for g in range(groups):
            for m in range(members):
                to_g, to_m = target(g, m)
                if to_g is not None:
                    pairs.append((g * members + m, to_g * members + to_m % members))
        return functools.partial(lax.ppermute, axis_name=AXES, perm=pairs)

    to_ring = route(lambda g, m: (g, m - 2 + 4 * (m % 2)))
    ring_back = route(lambda g, m: (g, m + 2 - 4 * (m % 2)))
    to_near = route(lambda g, m: (g, m ^ 1))
    to_cross = route(lambda g, m: (g ^ 1 if (g + m) % 2 == 0 else None, m))
    cross_back = route(lambda g, m: (g ^ 1 if (g + m) % 2 == 1 else None, m))

    f = jax.ShapeDtypeStruct
    acc, half, sums_shape = f((rows, ds), F32), f((rows, ds), BF16), f((8, 128), F32)

    def on_blocks(kernel):
        return functools.partial(kernel, rows, ds)

    own, own_ring, scale = call(
        pack_kernel,
        (f((rows + META, ds + dt), BF16), f((rows + RING_META, ds + dt), BF16), f((rows, 128), F32)),
        24,
        *(pltpu.with_memory_space_constraint(x, pltpu.HBM) for x in (counts, plan.reshape(1, -1), student, teacher)),
        in_specs=[pl.BlockSpec(memory_space=pltpu.HBM)] * 4,
        scratch_shapes=[
            pltpu.VMEM((rows,), jnp.int32),
            pltpu.VMEM((1, plan.size), jnp.int32),
            pltpu.VMEM((rows, ds), BF16),
            pltpu.VMEM((rows, dt), BF16),
            pltpu.SemaphoreType.DMA((PIECES + 1, 2)),
        ],
    )
    near, cross, ring = to_near(own), to_cross(own), to_ring(own_ring)

    total, sums = call(on_blocks(local_kernel), (acc, sums_shape), 24, own, near)
    total, give_cross, sums = call(
        on_blocks(cross_kernel), (acc, half, sums_shape), 24, own, cross, total, sums
    )
    from_cross = cross_back(give_cross)
    pair_shape = f((rows, rows), BF16)
    coefficients, near_coefficients, ring_sums = call(
        on_blocks(ring_kernel), (pair_shape, pair_shape, sums_shape), 24, own, near, ring, flops=10**10
    )
    ring_total, give_near, give_ring = call(
        on_blocks(ring_mix_kernel), (acc, half, half), 24, own, ring, coefficients, near_coefficients, flops=10**9
    )

    sums = sums + ring_sums
    sums = sums + to_near(sums)
    sums, from_cross, give_near, give_ring = lax.optimization_barrier((sums, from_cross, give_near, give_ring))
    from_near = to_near(give_near)
    from_ring = ring_back(give_ring)
    routes = [route(lambda g, m, bit=bit: (g ^ bit, m)) for bit in powers(1, groups)]
    routes += [route(lambda g, m, bit=bit: (g, m ^ bit)) for bit in reversed(powers(2, members))]
    for exchange in routes[:-1]:
        sums = sums + exchange(sums)
    received = routes[-1](sums)

    (grad,) = call(
        on_blocks(final_kernel), (acc,), 24, own, scale, total, ring_total, from_near, from_ring, from_cross
    )
    sums, grad = lax.optimization_barrier((sums, grad))
    (loss,) = call(functools.partial(loss_kernel, ds), (f((1, 1), F32),), 24, sums + received)
    return grad, loss.reshape(())


def solution(mesh):
    return jax.shard_map(
        per_device,
        mesh=mesh,
        in_specs=(
            P(AXES, None),
            P(AXES, None),
            P(AXES),
            P("group", "member", None),
        ),
        out_specs=(P(AXES, None), P()),
        check_vma=False,
    )
```

time: 77.6 us -> 59.8 us (0.77)
  local copies, waits for them, and re-layouts: 8.31 us -> 0 us
  other arithmetic: 4.04 us -> 0.02 us
  between operations: 3.17 us -> 0.71 us
  waiting for transfers between devices: 29 us -> 27.3 us
  starting transfers between devices: 21.7 us -> 20.2 us
    unnamed x14 -> x0, local copies, waits for them, and re-layouts: 7.62 us -> none
    select_n x1 -> x0, other arithmetic: 1.99 us -> none  [per_device(): slots = jnp.where(odd == 1, odd_slots, even_slots)]
    ppermute x15 -> x10, waiting for transfers between devices: 29 us -> 27.3 us  [the longest x3 20.2 us: per_device(): near, cross, ring = (to_near(own), to_cross(own), to_ring(own_ring))]
    ppermute x15 -> x10, starting transfers between devices: 21.7 us -> 20.2 us  [the longest x3 9.53 us: per_device(): near, cross, ring = (to_near(own), to_cross(own), to_ring(own_ring))]
    convert_element_type x2 -> x0, other arithmetic: 1.34 us -> none  [the longest x1 0.69 us: per_device(): counts.astype(F32)]
    pallas_call x4 -> x7, Pallas kernels: 11 us -> 11.3 us  [call(): pl.pallas_call(kernel, out_shape=outs, compiler_params=pltpu.CompilerPara...]
  transfers between devices with their start and end apart: 16 -> 11, of which waited for: 7 -> 6; matrix products, arithmetic and copies ran while one was open for 6% -> 0% of each run, Pallas kernels for 7% -> 15%
where the time goes in v2:
time: 59.8 us; the launch traced here: 59.6 us
  waiting for transfers between devices  27.3 us (46%)
  starting transfers between devices  20.2 us (34%)
  Pallas kernels  11.3 us (19%)
  between operations  0.71 us (1%)
    ppermute x3, waiting for transfers between devices, per_device(): near, cross, ring = (to_near(own), to_cross(own), to_ring(own_ring))  20.2 us
    pallas_call x7, Pallas kernels, call(): pl.pallas_call(kernel, out_shape=outs, compiler_params=pltpu.CompilerPara...  11.3 us
    ppermute x3, starting transfers between devices, per_device(): near, cross, ring = (to_near(own), to_cross(own), to_ring(own_ring))  9.53 us
    ppermute x3, waiting for transfers between devices, per_device(): sums = sums + exchange(sums)  6.17 us
    ppermute x3, starting transfers between devices, per_device(): sums = sums + exchange(sums)  5.66 us
    ppermute x1, starting transfers between devices, per_device(): received = routes[-1](sums)  3.5 us
    ppermute x1, starting transfers between devices, per_device(): from_cross = cross_back(give_cross)  1.29 us
  transfers between devices with their start and end apart: 11, of which 6 were waited for; matrix products, arithmetic and copies ran while one was open for 0% of the time, Pallas kernels for 15%

profile of v2, /device:TPU:0, one launch (start us, length us, event | category | flops | bytes accessed | tf_op | source)
XLA Modules:
  0.0 59.6 jit_solution(16175037511783989067)
XLA Ops:
  0.6 2.0 %shard_map.59 = (bf16[392,1792]{1,0:T(8,128)(2,1)S(1)}, bf16[400,1792]{1,0:T(8,128)(2,1)S(1)}, f32[384,128]{1,0:T(8,128)S(1)}) custom-call(s32[384]{0:T(512)} %counts_hbm.1, s32[1,5]{1,0:T(1,128)} %bitcast.2, bf16[384,768]{1,0:T(8,128)(2,1)} %s_hbm.1, bf16[384,1024]{1,0:T(8,128)(2,1)} %t_hbm.1), custom_call_target="tpu_custom_call" | custom-call | tf_op jit(solution)/shard_map/pallas_call | solution.py:174
  2.6 6.0 %collective-permute-start.2 = (bf16[400,1792]{1,0:T(8,128)(2,1)S(1)}, bf16[400,1792]{1,0:T(8,128)(2,1)S(1)}, u32[]{:S(2)}, u32[]{:S(2)}) collective-permute-start(bf16[400,1792]{1,0:T(8,128)(2,1)S(1)} %get-tuple-element.26), channel_id=1, source_target_pairs={{0,14},{1,3},{2,0},{3,5},{4,2},{5,7},{6,4},{7,9},{8,6},{9,11},{10,... | collective-permute-start | bytes 4300808 | tf_op jit(solution)/shard_map/ppermute | solution.py:227
  8.7 0.0 collective-permute-start.1
  8.7 3.5 %collective-permute-start = (bf16[392,1792]{1,0:T(8,128)(2,1)S(1)}, bf16[392,1792]{1,0:T(8,128)(2,1)S(1)}, u32[]{:S(2)}, u32[]{:S(2)}) collective-permute-start(bf16[392,1792]{1,0:T(8,128)(2,1)S(1)} %get-tuple-element.22.own), channel_id=1, source_target_pairs={{0,16},{2,18},{4,20},{6,22},{8,24},{10,26},{12,28},{14,30},{17,1},... | collective-permute-start | bytes 4214792 | tf_op jit(solution)/shard_map/ppermute | solution.py:227
  12.2 0.0 collective-permute-done.1.near
  12.2 2.5 %shard_map.60 = (f32[384,768]{1,0:T(8,128)S(1)}, f32[8,128]{1,0:T(8,128)S(1)}) custom-call(bf16[392,1792]{1,0:T(8,128)(2,1)S(1)} %get-tuple-element.22.own, bf16[392,1792]{1,0:T(8,128)(2,1)S(1)} %collective-permute-done.1.near), custom_call_target="tpu_custom_call" | custom-call | tf_op jit(solution)/shard_map/pallas_call | solution.py:174
  14.7 13.5 %collective-permute-done.far = bf16[392,1792]{1,0:T(8,128)(2,1)S(1)} collective-permute-done((bf16[392,1792]{1,0:T(8,128)(2,1)S(1)}, bf16[392,1792]{1,0:T(8,128)(2,1)S(1)}, u32[]{:S(2)}, u32[]{:S(2)}) %collective-permute-start) | collective-permute-done | bytes 1404960 | tf_op jit(solution)/shard_map/ppermute | solution.py:227
  28.2 1.8 %shard_map.61 = (f32[384,768]{1,0:T(8,128)S(1)}, bf16[384,768]{1,0:T(8,128)(2,1)S(1)}, f32[8,128]{1,0:T(8,128)S(1)}) custom-call(bf16[392,1792]{1,0:T(8,128)(2,1)S(1)} %get-tuple-element.22.own, bf16[392,1792]{1,0:T(8,128)(2,1)S(1)} %collective-permute-done.far, f32[384,768]{1,0:T(8,128)S(1)} %get-tuple-element.23.before, ...), custom_call_target="tpu_custom_call" | custom-call | tf_op jit(solution)/shard_map/pallas_call | solution.py:174
  30.0 1.3 %collective-permute-start.4 = (bf16[384,768]{1,0:T(8,128)(2,1)S(1)}, bf16[384,768]{1,0:T(8,128)(2,1)S(1)}, u32[]{:S(2)}, u32[]{:S(2)}) collective-permute-start(bf16[384,768]{1,0:T(8,128)(2,1)S(1)} %get-tuple-element.28), channel_id=1, source_target_pairs={{1,17},{3,19},{5,21},{7,23},{9,25},{11,27},{13,29},{15,31},{16,0},... | collective-permute-start | bytes 1769480 | tf_op jit(solution)/shard_map/ppermute | solution.py:233
  31.3 6.6 %collective-permute-done.2.far = bf16[400,1792]{1,0:T(8,128)(2,1)S(1)} collective-permute-done((bf16[400,1792]{1,0:T(8,128)(2,1)S(1)}, bf16[400,1792]{1,0:T(8,128)(2,1)S(1)}, u32[]{:S(2)}, u32[]{:S(2)}) %collective-permute-start.2) | collective-permute-done | bytes 1433632 | tf_op jit(solution)/shard_map/ppermute | solution.py:227
  37.9 1.6 %shard_map.62 = (bf16[384,384]{1,0:T(8,128)(2,1)S(1)}, bf16[384,384]{1,0:T(8,128)(2,1)S(1)}, f32[8,128]{1,0:T(8,128)S(1)}) custom-call(bf16[392,1792]{1,0:T(8,128)(2,1)S(1)} %get-tuple-element.22.own, bf16[392,1792]{1,0:T(8,128)(2,1)S(1)} %collective-permute-done.1.near, bf16[400,1792]{1,0:T(8,128)(2,1)S(1)} %collective-permute-done.2.far), custom_call_target="tpu_custom_call" | custom-call | flops 10000000000 | tf_op jit(solution)/shard_map/pallas_call | solution.py:174
  39.5 0.1 collective-permute-start.3
  39.6 1.1 %shard_map.63 = (f32[384,768]{1,0:T(8,128)S(1)}, bf16[384,768]{1,0:T(8,128)(2,1)S(1)}, bf16[384,768]{1,0:T(8,128)(2,1)S(1)}) custom-call(bf16[392,1792]{1,0:T(8,128)(2,1)S(1)} %get-tuple-element.22.own, bf16[400,1792]{1,0:T(8,128)(2,1)S(1)} %collective-permute-done.2.far, bf16[384,384]{1,0:T(8,128)(2,1)S(1)} %get-tuple-element.29.coefficients, ...), custom_call_target="tpu_custom_call" | custom-call | flops 1000000000 | tf_op jit(solution)/shard_map/pallas_call | solution.py:174
  40.7 0.0 collective-permute-done.3
  40.8 1.0 %collective-permute-done.4.from_cross = bf16[384,768]{1,0:T(8,128)(2,1)S(1)} collective-permute-done((bf16[384,768]{1,0:T(8,128)(2,1)S(1)}, bf16[384,768]{1,0:T(8,128)(2,1)S(1)}, u32[]{:S(2)}, u32[]{:S(2)}) %collective-permute-start.4) | collective-permute-done | bytes 589856 | tf_op jit(solution)/shard_map/ppermute | solution.py:233
  41.8 0.0 collective-permute-start.8
  41.8 0.1 collective-permute-start.9
  41.9 1.5 %collective-permute-start.5 = (f32[8,128]{1,0:T(8,128)S(1)}, f32[8,128]{1,0:T(8,128)S(1)}, u32[]{:S(2)}, u32[]{:S(2)}) collective-permute-start(f32[8,128]{1,0:T(8,128)S(1)} %add.19), channel_id=1, source_target_pairs={{0,16},{1,17},{2,18},{3,19},{4,20},{5,21},{6,22},{7,23},{8,24},{9,... | collective-permute-start | bytes 12296 | tf_op jit(solution)/shard_map/ppermute | solution.py:250
  43.4 2.1 %collective-permute-done.5 = f32[8,128]{1,0:T(8,128)S(1)} collective-permute-done((f32[8,128]{1,0:T(8,128)S(1)}, f32[8,128]{1,0:T(8,128)S(1)}, u32[]{:S(2)}, u32[]{:S(2)}) %collective-permute-start.5) | collective-permute-done | bytes 4128 | tf_op jit(solution)/shard_map/ppermute | solution.py:250
  45.5 2.6 %collective-permute-start.6 = (f32[8,128]{1,0:T(8,128)S(1)}, f32[8,128]{1,0:T(8,128)S(1)}, u32[]{:S(2)}, u32[]{:S(2)}) collective-permute-start(f32[8,128]{1,0:T(8,128)S(1)} %add.20), channel_id=1, source_target_pairs={{0,8},{1,9},{2,10},{3,11},{4,12},{5,13},{6,14},{7,15},{8,0},{9,1},... | collective-permute-start | bytes 12296 | tf_op jit(solution)/shard_map/ppermute | solution.py:250
  48.1 2.0 %collective-permute-done.6 = f32[8,128]{1,0:T(8,128)S(1)} collective-permute-done((f32[8,128]{1,0:T(8,128)S(1)}, f32[8,128]{1,0:T(8,128)S(1)}, u32[]{:S(2)}, u32[]{:S(2)}) %collective-permute-start.6) | collective-permute-done | bytes 4128 | tf_op jit(solution)/shard_map/ppermute | solution.py:250
  50.1 1.6 %collective-permute-start.7 = (f32[8,128]{1,0:T(8,128)S(1)}, f32[8,128]{1,0:T(8,128)S(1)}, u32[]{:S(2)}, u32[]{:S(2)}) collective-permute-start(f32[8,128]{1,0:T(8,128)S(1)} %add.21), channel_id=1, source_target_pairs={{0,4},{1,5},{2,6},{3,7},{4,0},{5,1},{6,2},{7,3},{8,12},{9,13},{10,... | collective-permute-start | bytes 12296 | tf_op jit(solution)/shard_map/ppermute | solution.py:250
  51.7 2.0 %collective-permute-done.7 = f32[8,128]{1,0:T(8,128)S(1)} collective-permute-done((f32[8,128]{1,0:T(8,128)S(1)}, f32[8,128]{1,0:T(8,128)S(1)}, u32[]{:S(2)}, u32[]{:S(2)}) %collective-permute-start.7) | collective-permute-done | bytes 4128 | tf_op jit(solution)/shard_map/ppermute | solution.py:250
  53.7 3.5 %collective-permute-start.10 = (f32[8,128]{1,0:T(8,128)S(1)}, f32[8,128]{1,0:T(8,128)S(1)}, u32[]{:S(2)}, u32[]{:S(2)}) collective-permute-start(f32[8,128]{1,0:T(8,128)S(1)} %add.22), channel_id=1, source_target_pairs={{0,2},{1,3},{2,0},{3,1},{4,6},{5,7},{6,4},{7,5},{8,10},{9,11},{10,... | collective-permute-start | bytes 12296 | tf_op jit(solution)/shard_map/ppermute | solution.py:251
  57.2 0.0 collective-permute-done.8.from_near
  57.2 0.0 collective-permute-done.9.from_far
  57.2 1.7 %shard_map.64 = f32[384,768]{1,0:T(8,128)} custom-call(bf16[392,1792]{1,0:T(8,128)(2,1)S(1)} %get-tuple-element.22.own, f32[384,128]{1,0:T(8,128)S(1)} %get-tuple-element.34.scale, f32[384,768]{1,0:T(8,128)S(1)} %get-tuple-element.35.total, f32[384,768]{1,0:T(8,128)S(1)} %get-tuple-element.36.ring_total, ...), custom_call_target="tpu_custom_call" | custom-call | tf_op jit(solution)/shard_map/pallas_call | solution.py:174
  59.0 0.0 collective-permute-done.10
  59.0 0.6 %shard_map.65 = f32[1,1]{1,0:T(1,128)} custom-call(f32[8,128]{1,0:T(8,128)S(1)} %add.23.sums), custom_call_target="tpu_custom_call" | custom-call | tf_op jit(solution)/shard_map/pallas_call | solution.py:174
  (6 shorter events, 0.0 us)
Async XLA Ops:
  2.6 35.3 %collective-permute-start.2 = (bf16[400,1792]{1,0:T(8,128)(2,1)S(1)}, bf16[400,1792]{1,0:T(8,128)(2,1)S(1)}, u32[]{:S(2)}, u32[]{:S(2)}) collective-permute-start(bf16[400,1792]{1,0:T(8,128)(2,1)S(1)} %get-tuple-element.26), channel_id=1, source_target_pairs={{0,14},{1,3},{2,0},{3,5},{4,2},{5,7},{6,4},{7,9},{8,6},{9,11},{10,... | collective-permute-start | bytes 4300808 | tf_op jit(solution)/shard_map/ppermute | solution.py:227
  8.7 3.5 %collective-permute-start.1 = (bf16[392,1792]{1,0:T(8,128)(2,1)S(1)}, bf16[392,1792]{1,0:T(8,128)(2,1)S(1)}, u32[]{:S(2)}, u32[]{:S(2)}) collective-permute-start(bf16[392,1792]{1,0:T(8,128)(2,1)S(1)} %get-tuple-element.22.own), channel_id=1, source_target_pairs={{0,1},{1,0},{2,3},{3,2},{4,5},{5,4},{6,7},{7,6},{8,9},{9,8},{10,11... | collective-permute-start | bytes 4214792 | tf_op jit(solution)/shard_map/ppermute | solution.py:227
  8.7 19.5 %collective-permute-start = (bf16[392,1792]{1,0:T(8,128)(2,1)S(1)}, bf16[392,1792]{1,0:T(8,128)(2,1)S(1)}, u32[]{:S(2)}, u32[]{:S(2)}) collective-permute-start(bf16[392,1792]{1,0:T(8,128)(2,1)S(1)} %get-tuple-element.22.own), channel_id=1, source_target_pairs={{0,16},{2,18},{4,20},{6,22},{8,24},{10,26},{12,28},{14,30},{17,1},... | collective-permute-start | bytes 4214792 | tf_op jit(solution)/shard_map/ppermute | solution.py:227
  30.0 11.8 %collective-permute-start.4 = (bf16[384,768]{1,0:T(8,128)(2,1)S(1)}, bf16[384,768]{1,0:T(8,128)(2,1)S(1)}, u32[]{:S(2)}, u32[]{:S(2)}) collective-permute-start(bf16[384,768]{1,0:T(8,128)(2,1)S(1)} %get-tuple-element.28), channel_id=1, source_target_pairs={{1,17},{3,19},{5,21},{7,23},{9,25},{11,27},{13,29},{15,31},{16,0},... | collective-permute-start | bytes 1769480 | tf_op jit(solution)/shard_map/ppermute | solution.py:233
  39.5 1.2 %collective-permute-start.3 = (f32[8,128]{1,0:T(8,128)S(1)}, f32[8,128]{1,0:T(8,128)S(1)}, u32[]{:S(2)}, u32[]{:S(2)}) collective-permute-start(f32[8,128]{1,0:T(8,128)S(1)} %add.18), channel_id=1, source_target_pairs={{0,1},{1,0},{2,3},{3,2},{4,5},{5,4},{6,7},{7,6},{8,9},{9,8},{10,11... | collective-permute-start | bytes 12296 | tf_op jit(solution)/shard_map/ppermute | solution.py:243
  41.8 15.5 %collective-permute-start.8 = (bf16[384,768]{1,0:T(8,128)(2,1)S(1)}, bf16[384,768]{1,0:T(8,128)(2,1)S(1)}, u32[]{:S(2)}, u32[]{:S(2)}) collective-permute-start(bf16[384,768]{1,0:T(8,128)(2,1)S(1)} %get-tuple-element.37), channel_id=1, source_target_pairs={{0,1},{1,0},{2,3},{3,2},{4,5},{5,4},{6,7},{7,6},{8,9},{9,8},{10,11... | collective-permute-start | bytes 1769480 | tf_op jit(solution)/shard_map/ppermute | solution.py:245
  41.8 15.5 %collective-permute-start.9 = (bf16[384,768]{1,0:T(8,128)(2,1)S(1)}, bf16[384,768]{1,0:T(8,128)(2,1)S(1)}, u32[]{:S(2)}, u32[]{:S(2)}) collective-permute-start(bf16[384,768]{1,0:T(8,128)(2,1)S(1)} %get-tuple-element.38), channel_id=1, source_target_pairs={{0,2},{1,15},{2,4},{3,1},{4,6},{5,3},{6,8},{7,5},{8,10},{9,7},{10,... | collective-permute-start | bytes 1769480 | tf_op jit(solution)/shard_map/ppermute | solution.py:246
  41.9 3.6 %collective-permute-start.5 = (f32[8,128]{1,0:T(8,128)S(1)}, f32[8,128]{1,0:T(8,128)S(1)}, u32[]{:S(2)}, u32[]{:S(2)}) collective-permute-start(f32[8,128]{1,0:T(8,128)S(1)} %add.19), channel_id=1, source_target_pairs={{0,16},{1,17},{2,18},{3,19},{4,20},{5,21},{6,22},{7,23},{8,24},{9,... | collective-permute-start | bytes 12296 | tf_op jit(solution)/shard_map/ppermute | solution.py:250
  45.5 4.6 %collective-permute-start.6 = (f32[8,128]{1,0:T(8,128)S(1)}, f32[8,128]{1,0:T(8,128)S(1)}, u32[]{:S(2)}, u32[]{:S(2)}) collective-permute-start(f32[8,128]{1,0:T(8,128)S(1)} %add.20), channel_id=1, source_target_pairs={{0,8},{1,9},{2,10},{3,11},{4,12},{5,13},{6,14},{7,15},{8,0},{9,1},... | collective-permute-start | bytes 12296 | tf_op jit(solution)/shard_map/ppermute | solution.py:250
  50.1 3.6 %collective-permute-start.7 = (f32[8,128]{1,0:T(8,128)S(1)}, f32[8,128]{1,0:T(8,128)S(1)}, u32[]{:S(2)}, u32[]{:S(2)}) collective-permute-start(f32[8,128]{1,0:T(8,128)S(1)} %add.21), channel_id=1, source_target_pairs={{0,4},{1,5},{2,6},{3,7},{4,0},{5,1},{6,2},{7,3},{8,12},{9,13},{10,... | collective-permute-start | bytes 12296 | tf_op jit(solution)/shard_map/ppermute | solution.py:250
  53.7 5.2 %collective-permute-start.10 = (f32[8,128]{1,0:T(8,128)S(1)}, f32[8,128]{1,0:T(8,128)S(1)}, u32[]{:S(2)}, u32[]{:S(2)}) collective-permute-start(f32[8,128]{1,0:T(8,128)S(1)} %add.22), channel_id=1, source_target_pairs={{0,2},{1,3},{2,0},{3,1},{4,6},{5,7},{6,4},{7,5},{8,10},{9,11},{10,... | collective-permute-start | bytes 12296 | tf_op jit(solution)/shard_map/ppermute | solution.py:251

commit v3 on v2

v3 whole, which is shorter than its diff:
```python
import functools

import jax
import jax.numpy as jnp
from jax import lax
from jax.experimental import pallas as pl
from jax.experimental.pallas import tpu as pltpu
from jax.sharding import PartitionSpec as P

EPS = 1e-06
AXES = ("group", "member")
F32 = jnp.float32
BF16 = jnp.bfloat16
META = 16
PIECES = 3


def units(raw):
    wide = raw.astype(F32)
    scale = lax.rsqrt(jnp.sum(wide * wide, axis=-1, keepdims=True) + EPS)
    return (wide * scale).astype(BF16), scale


def similarity(left, right):
    return lax.dot_general(left, right, (((1,), (1,)), ((), ())), preferred_element_type=F32)


def dot(left, right):
    return jnp.dot(left, right, preferred_element_type=F32)


def dot_transposed(left, right):
    return lax.dot_general(left, right, (((0,), (0,)), ((), ())), preferred_element_type=F32)


def column(row):
    wide = jnp.broadcast_to(row, (128, row.shape[1]))
    return jnp.transpose(wide)[:, :1]


def lanes(values):
    row = jnp.sum(values, axis=0, keepdims=True)
    return sum(row[:, k : k + 128] for k in range(0, row.shape[1], 128))


def weigh(mismatch, weight_column, weight_row, twice=0):
    weight = weight_column * weight_row
    weighted = weight * mismatch
    loss = weighted * mismatch
    sums = [lanes(loss) + lanes(loss[:, :twice]), lanes(weight) + lanes(weight[:, :twice])] if twice else [lanes(loss), lanes(weight)]
    return weighted.astype(BF16), *sums


def tile(loss, weight):
    rows = lax.broadcasted_iota(jnp.int32, (8, 128), 0)
    zero = jnp.zeros((8, 128), F32)
    return jnp.where(rows == 0, loss, zero) + jnp.where(rows == 1, weight, zero)


class Packed:
    def __init__(self, student, teacher, rows):
        self.student, self.teacher, self.rows = student, teacher, rows

    @property
    def s(self):
        return self.student[: self.rows]

    @property
    def t(self):
        return self.teacher[...]

    def counts(self):
        return self.student[self.rows :].astype(F32)[0:1, : self.rows]

    def switch(self, if_even, if_odd):
        odd = lax.axis_index("member") % 2 == 1
        plan = self.student[self.rows :].astype(F32)[1:2, :128]
        return jnp.where(odd, plan[:, if_odd : if_odd + 1], plan[:, if_even : if_even + 1])


def pack_kernel(counts_hbm, plan_hbm, s_hbm, t_hbm, both, student, teacher, scale, counts, plan, s, t, arrived):
    rows, ds = s.shape
    copies = [
        pltpu.make_async_copy(source, target, arrived.at[i])
        for i, (source, target) in enumerate(((s_hbm, s), (t_hbm, t), (counts_hbm, counts), (plan_hbm, plan)))
    ]
    for copy in copies:
        copy.start()
    copies[0].wait()
    unit, factor = units(s[...])
    scale[...] = jnp.broadcast_to(factor, scale.shape)
    both[:, :ds] = unit
    student[:rows] = unit
    copies[1].wait()
    unit, _ = units(t[...])
    both[:, ds:] = unit
    teacher[...] = unit

    def widen(values):
        return jnp.concatenate([values, jnp.zeros((1, ds - values.shape[1]), F32)], axis=1)

    copies[2].wait()
    copies[3].wait()
    at = lax.broadcasted_iota(jnp.int32, (META, ds), 0)
    meta = jnp.where(at == 0, widen(counts[...].astype(F32).reshape(1, rows)), 0.0)
    student[rows:] = jnp.where(at == 1, widen(plan[...].astype(F32)), meta).astype(BF16)


def local_kernel(rows, both, own_s, own_t, near_s, near_t, mates, total, sums):
    own, near = Packed(own_s, own_t, rows), Packed(near_s, near_t, rows)
    mates[:rows] = both[...]
    mates[rows:] = jnp.concatenate([near.s, near.t], axis=1)
    own_column = column(own.counts())
    mismatch = similarity(own.s, own.s) - similarity(own.t, own.t)
    coefficient, loss, weight = weigh(mismatch, own_column, own.counts())
    total[...] = dot(coefficient, own.s)
    mismatch = similarity(own.s, near.s) - similarity(own.t, near.t)
    coefficient, loss_2, weight_2 = weigh(mismatch, own_column, near.counts() * own.switch(2, 0))
    total[...] += dot(coefficient, near.s)
    sums[...] = tile(loss + loss_2, weight + weight_2)


def cross_kernel(rows, own_s, own_t, far_s, far_t, before, sums_before, total, give, sums):
    own, far = Packed(own_s, own_t, rows), Packed(far_s, far_t, rows)
    mismatch = similarity(own.s, far.s) - similarity(own.t, far.t)
    coefficient, loss, weight = weigh(mismatch, column(own.counts()), far.counts() * own.switch(4, 4))
    give[...] = dot_transposed(coefficient, own.s).astype(BF16)
    total[...] = before[...] + dot(coefficient, far.s)
    sums[...] = sums_before[...] + tile(2.0 * loss, 2.0 * weight)


def ring_kernel(rows, own_s, near_s, mates, far, far_counts, sums_before, coefficients, to_far, sums):
    own, near, ds = Packed(own_s, None, rows), Packed(near_s, None, rows), own_s.shape[1]
    mismatch = similarity(far[:, :ds], mates[:, :ds]) - similarity(far[:, ds:], mates[:, ds:])
    mates_row = jnp.concatenate([own.counts() * own.switch(3, 1), near.counts() * near.switch(2, 0)], axis=1)
    far_column = column(far_counts[...].astype(F32).reshape(1, rows))
    coefficients[...], loss, weight = weigh(mismatch, far_column, mates_row, twice=rows)
    to_far[...] = dot(coefficients[:, :rows], own.s).astype(BF16)
    sums[...] = sums_before[...] + tile(loss, weight)


def ring_mix_kernel(rows, far, coefficients, before, total, to_near):
    far_s = far[:, : before.shape[1]]
    to_near[...] = dot_transposed(coefficients[:, rows:], far_s).astype(BF16)
    total[...] = before[...] + dot_transposed(coefficients[:, :rows], far_s)


def final_kernel(rows, own, scale, total, from_near, from_far, from_cross, grad, result, sent):
    size = rows // PIECES
    copies = []
    for i in range(PIECES):
        piece = pl.ds(i * size, size)
        unit = own[piece].astype(F32)
        received = from_near[piece].astype(F32) + from_far[piece].astype(F32) + from_cross[piece].astype(F32)
        summed = total[piece] + received
        along = jnp.sum(summed * unit, axis=-1, keepdims=True)
        result[piece] = 4.0 * scale[piece, :1] * (summed - along * unit)
        copies.append(pltpu.make_async_copy(result.at[piece], grad.at[piece], sent.at[i]))
        copies[-1].start()
    for copy in copies:
        copy.wait()


def loss_kernel(width, sums, loss):
    total = jnp.sum(sums[...], axis=1, keepdims=True)
    loss[...] = width * total[0:1] / total[1:2]


def call(kernel, outs, vmem_mib, *operands, flops=0, **options):
    return pl.pallas_call(
        kernel,
        out_shape=outs,
        compiler_params=pltpu.CompilerParams(vmem_limit_bytes=vmem_mib << 20),
        cost_estimate=pl.CostEstimate(flops=flops, bytes_accessed=0, transcendentals=0),
        **options,
    )(*operands)


def powers(first, end):
    return [first << i for i in range(end.bit_length()) if first << i < end]


def per_device(student, teacher, counts, plan):
    groups, members = lax.axis_size("group"), lax.axis_size("member")
    rows, ds = student.shape
    dt = teacher.shape[1]

    def route(target):
        pairs = []
        for g in range(groups):
            for m in range(members):
                to_g, to_m = target(g, m)
                if to_g is not None:
                    pairs.append((g * members + m, to_g * members + to_m % members))
        return functools.partial(lax.ppermute, axis_name=AXES, perm=pairs)

    to_ring = route(lambda g, m: (g, m - 2 + 4 * (m % 2)))
    ring_back = route(lambda g, m: (g, m + 2 - 4 * (m % 2)))
    to_near = route(lambda g, m: (g, m ^ 1))
    to_cross = route(lambda g, m: (g ^ 1 if (g + m) % 2 == 0 else None, m))
    cross_back = route(lambda g, m: (g ^ 1 if (g + m) % 2 == 1 else None, m))

    f = jax.ShapeDtypeStruct
    acc, half, sums_shape = f((rows, ds), F32), f((rows, ds), BF16), f((8, 128), F32)

    def on_blocks(kernel):
        return functools.partial(kernel, rows)

    both, own_s, own_t, scale = call(
        pack_kernel,
        (f((rows, ds + dt), BF16), f((rows + META, ds), BF16), f((rows, dt), BF16), f((rows, 128), F32)),
        24,
        *(pltpu.with_memory_space_constraint(x, pltpu.HBM) for x in (counts, plan.reshape(1, -1), student, teacher)),
        in_specs=[pl.BlockSpec(memory_space=pltpu.HBM)] * 4,
        scratch_shapes=[
            pltpu.VMEM((rows,), jnp.int32),
            pltpu.VMEM((1, plan.size), jnp.int32),
            pltpu.VMEM((rows, ds), BF16),
            pltpu.VMEM((rows, dt), BF16),
            pltpu.SemaphoreType.DMA((4,)),
        ],
    )
    ring, ring_counts = to_ring(both), to_ring(counts)
    near, cross = (to_near(own_s), to_near(own_t)), (to_cross(own_s), to_cross(own_t))

    mates, total, sums = call(
        on_blocks(local_kernel), (f((2 * rows, ds + dt), BF16), acc, sums_shape), 24, both, own_s, own_t, *near
    )
    total, give_cross, sums = call(
        on_blocks(cross_kernel), (acc, half, sums_shape), 24, own_s, own_t, *cross, total, sums
    )
    from_cross = cross_back(give_cross)
    coefficients, give_ring, sums = call(
        on_blocks(ring_kernel), (f((rows, 2 * rows), BF16), half, sums_shape), 24,
        own_s, near[0], mates, ring, ring_counts, sums,
        flops=10**10,
    )
    total, give_near = call(on_blocks(ring_mix_kernel), (acc, half), 24, ring, coefficients, total)
    from_ring = ring_back(give_ring)
    across = [route(lambda g, m, bit=bit: (g ^ bit, m)) for bit in powers(1, groups)]
    along = [route(lambda g, m, bit=bit: (g, m ^ bit)) for bit in powers(2, members)]
    sums = sums + along[0](sums)
    sums, from_cross, give_near = lax.optimization_barrier((sums, from_cross, give_near))
    from_near = to_near(give_near)
    for exchange in [to_near] + across + along[:1:-1]:
        sums = sums + exchange(sums)
    received = along[1](sums)

    (grad,) = call(
        on_blocks(final_kernel), (acc,), 24, own_s, scale, total, from_near, from_ring, from_cross,
        out_specs=(pl.BlockSpec(memory_space=pltpu.HBM),),
        scratch_shapes=[pltpu.VMEM((rows, ds), F32), pltpu.SemaphoreType.DMA((PIECES,))],
    )
    sums, grad = lax.optimization_barrier((sums, grad))
    (loss,) = call(functools.partial(loss_kernel, ds), (f((1, 1), F32),), 24, sums + received)
    return grad, loss.reshape(())


def solution(mesh):
    return jax.shard_map(
        per_device,
        mesh=mesh,
        in_specs=(
            P(AXES, None),
            P(AXES, None),
            P(AXES),
            P("group", "member", None),
        ),
        out_specs=(P(AXES, None), P()),
        check_vma=False,
    )
```

time: 59.8 us -> 57 us (0.953)
  waiting for transfers between devices: 27.3 us -> 23.4 us
  starting transfers between devices: 20.2 us -> 21.9 us
  Pallas kernels: 11.3 us -> 10.6 us
    ppermute x5 -> x8, waiting for transfers between devices: 20.2 us -> 17.2 us  [the longest x1 10.1 us: per_device(): to_cross(own_s)]
    ppermute x3, starting transfers between devices: 5.66 us -> 3.56 us  [per_device(): sums = sums + exchange(sums)]
    ppermute x1, starting transfers between devices: 0.14 us -> 2.01 us  [per_device(): from_ring = ring_back(give_ring)]
    ppermute x1, starting transfers between devices: 0.01 us -> 1.08 us  [per_device(): from_near = to_near(give_near)]
    ppermute x1, waiting for transfers between devices: 0.99 us -> 0.01 us  [per_device(): from_cross = cross_back(give_cross)]
    ppermute x5 -> x8, starting transfers between devices: 13.1 us -> 14 us  [the longest x2 6.62 us: per_device(): ring, ring_counts = (to_ring(both), to_ring(counts))]
    pallas_call x7, Pallas kernels: 11.3 us -> 10.6 us  [call(): pl.pallas_call(kernel, out_shape=outs, compiler_params=pltpu.CompilerPara...]
  transfers between devices with their start and end apart: 11 -> 14, of which waited for: 6 -> 7; matrix products, arithmetic and copies ran while one was open for 0% -> 0% of each run, Pallas kernels for 15% -> 15%
where the time goes in v3:
time: 57 us; the launch traced here: 56.8 us
  waiting for transfers between devices  23.4 us (41%)
  starting transfers between devices  21.9 us (38%)
  Pallas kernels  10.6 us (19%)
  between operations  0.75 us (1%)
    pallas_call x7, Pallas kernels, call(): pl.pallas_call(kernel, out_shape=outs, compiler_params=pltpu.CompilerPara...  10.6 us
    ppermute x1, waiting for transfers between devices, per_device(): to_cross(own_s)  10.1 us
    ppermute x2, starting transfers between devices, per_device(): ring, ring_counts = (to_ring(both), to_ring(counts))  6.62 us
    ppermute x3, waiting for transfers between devices, per_device(): sums = sums + exchange(sums)  6.2 us
    ppermute x2, waiting for transfers between devices, per_device(): ring, ring_counts = (to_ring(both), to_ring(counts))  5.48 us
    ppermute x3, starting transfers between devices, per_device(): sums = sums + exchange(sums)  3.56 us
    ppermute x1, starting transfers between devices, per_device(): to_cross(own_t)  3.46 us
    ppermute x1, starting transfers between devices, per_device(): to_cross(own_s)  2.65 us
  transfers between devices with their start and end apart: 14, of which 7 were waited for; matrix products, arithmetic and copies ran while one was open for 0% of the time, Pallas kernels for 15%

profile of v3, /device:TPU:0, one launch (start us, length us, event | category | flops | bytes accessed | tf_op | source)
XLA Modules:
  0.0 56.8 jit_solution(3334759898798692438)
XLA Ops:
  0.6 1.6 %shard_map.59 = (bf16[384,1792]{1,0:T(8,128)(2,1)S(1)}, bf16[400,768]{1,0:T(8,128)(2,1)S(1)}, bf16[384,1024]{1,0:T(8,128)(2,1)S(1)}, f32[384,128]{1,0:T(8,128)S(1)}) custom-call(s32[384]{0:T(512)} %counts_hbm.1, s32[1,5]{1,0:T(1,128)} %bitcast.2, bf16[384,768]{1,0:T(8,128)(2,1)} %s_hbm.1, bf16[384,1024]{1,0:T(8,128)(2,1)} %t_hbm.1), custom_call_target="tpu_custom_call" | custom-call | tf_op jit(solution)/shard_map/pallas_call | solution.py:170
  2.3 6.0 %collective-permute-start.2 = (bf16[384,1792]{1,0:T(8,128)(2,1)S(1)}, bf16[384,1792]{1,0:T(8,128)(2,1)S(1)}, u32[]{:S(2)}, u32[]{:S(2)}) collective-permute-start(bf16[384,1792]{1,0:T(8,128)(2,1)S(1)} %get-tuple-element.23.both), channel_id=1, source_target_pairs={{0,14},{1,3},{2,0},{3,5},{4,2},{5,7},{6,4},{7,9},{8,6},{9,11},{10,... | collective-permute-start | bytes 4128776 | tf_op jit(solution)/shard_map/ppermute | solution.py:223
  8.3 0.0 collective-permute-start.1
  8.3 3.5 %collective-permute-start.5 = (bf16[384,1024]{1,0:T(8,128)(2,1)S(1)}, bf16[384,1024]{1,0:T(8,128)(2,1)S(1)}, u32[]{:S(2)}, u32[]{:S(2)}) collective-permute-start(bf16[384,1024]{1,0:T(8,128)(2,1)S(1)} %get-tuple-element.24.own_t), channel_id=1, source_target_pairs={{0,16},{2,18},{4,20},{6,22},{8,24},{10,26},{12,28},{14,30},{17,1},... | collective-permute-start | bytes 2359304 | tf_op jit(solution)/shard_map/ppermute | solution.py:224
  11.8 0.1 collective-permute-start
  11.9 2.7 %collective-permute-start.4 = (bf16[400,768]{1,0:T(8,128)(2,1)S(1)}, bf16[400,768]{1,0:T(8,128)(2,1)S(1)}, u32[]{:S(2)}, u32[]{:S(2)}) collective-permute-start(bf16[400,768]{1,0:T(8,128)(2,1)S(1)} %get-tuple-element.22.own_s.own), channel_id=1, source_target_pairs={{0,16},{2,18},{4,20},{6,22},{8,24},{10,26},{12,28},{14,30},{17,1},... | collective-permute-start | bytes 1843208 | tf_op jit(solution)/shard_map/ppermute | solution.py:224
  14.5 0.0 collective-permute-done.near_s
  14.5 0.6 %collective-permute-start.3 = (s32[384]{0:T(512)S(1)}, s32[384]{0:T(512)S(1)}, u32[]{:S(2)}, u32[]{:S(2)}) collective-permute-start(s32[384]{0:T(512)S(1)} %copy-done), channel_id=1, source_target_pairs={{0,14},{1,3},{2,0},{3,5},{4,2},{5,7},{6,4},{7,9},{8,6},{9,11},{10,... | collective-permute-start | bytes 4616 | tf_op jit(solution)/shard_map/ppermute | solution.py:223
  15.1 0.0 collective-permute-done.1.near_t
  15.1 2.6 %shard_map.60 = (bf16[768,1792]{1,0:T(8,128)(2,1)S(1)}, f32[384,768]{1,0:T(8,128)S(1)}, f32[8,128]{1,0:T(8,128)S(1)}) custom-call(bf16[384,1792]{1,0:T(8,128)(2,1)S(1)} %get-tuple-element.23.both, bf16[400,768]{1,0:T(8,128)(2,1)S(1)} %get-tuple-element.22.own_s.own, bf16[384,1024]{1,0:T(8,128)(2,1)S(1)} %get-tuple-element.24.own_t, ...), custom_call_target="tpu_custom_call" | custom-call | tf_op jit(solution)/shard_map/pallas_call | solution.py:170
  17.7 10.1 %collective-permute-done.4.far_s = bf16[400,768]{1,0:T(8,128)(2,1)S(1)} collective-permute-done((bf16[400,768]{1,0:T(8,128)(2,1)S(1)}, bf16[400,768]{1,0:T(8,128)(2,1)S(1)}, u32[]{:S(2)}, u32[]{:S(2)}) %collective-permute-start.4) | collective-permute-done | bytes 614432 | tf_op jit(solution)/shard_map/ppermute | solution.py:224
  27.8 0.0 collective-permute-done.5.far_t
  27.8 1.8 %shard_map.61 = (f32[384,768]{1,0:T(8,128)S(1)}, bf16[384,768]{1,0:T(8,128)(2,1)S(1)}, f32[8,128]{1,0:T(8,128)S(1)}) custom-call(bf16[400,768]{1,0:T(8,128)(2,1)S(1)} %get-tuple-element.22.own_s.own, bf16[384,1024]{1,0:T(8,128)(2,1)S(1)} %get-tuple-element.24.own_t, bf16[400,768]{1,0:T(8,128)(2,1)S(1)} %collective-permute-done.4.far_s, ...), custom_call_target="tpu_custom_call" | custom-call | tf_op jit(solution)/shard_map/pallas_call | solution.py:170
  29.6 1.3 %collective-permute-start.7 = (bf16[384,768]{1,0:T(8,128)(2,1)S(1)}, bf16[384,768]{1,0:T(8,128)(2,1)S(1)}, u32[]{:S(2)}, u32[]{:S(2)}) collective-permute-start(bf16[384,768]{1,0:T(8,128)(2,1)S(1)} %get-tuple-element.30), channel_id=1, source_target_pairs={{1,17},{3,19},{5,21},{7,23},{9,25},{11,27},{13,29},{15,31},{16,0},... | collective-permute-start | bytes 1769480 | tf_op jit(solution)/shard_map/ppermute | solution.py:232
  30.9 5.5 %collective-permute-done.3.far_counts = s32[384]{0:T(512)S(1)} collective-permute-done((s32[384]{0:T(512)S(1)}, s32[384]{0:T(512)S(1)}, u32[]{:S(2)}, u32[]{:S(2)}) %collective-permute-start.3) | collective-permute-done | bytes 1568 | tf_op jit(solution)/shard_map/ppermute | solution.py:223
  36.3 0.0 collective-permute-done.2.far
  36.3 1.6 %shard_map.62 = (bf16[384,768]{1,0:T(8,128)(2,1)S(1)}, bf16[384,768]{1,0:T(8,128)(2,1)S(1)}, f32[8,128]{1,0:T(8,128)S(1)}) custom-call(bf16[400,768]{1,0:T(8,128)(2,1)S(1)} %get-tuple-element.22.own_s.own, bf16[400,768]{1,0:T(8,128)(2,1)S(1)} %collective-permute-done.near_s, bf16[768,1792]{1,0:T(8,128)(2,1)S(1)} %get-tuple-element.25.mates, ...), custom_call_target="tpu_custom_call" | custom-call | flops 10000000000 | tf_op jit(solution)/shard_map/pallas_call | solution.py:170
  38.0 0.1 collective-permute-start.6
  38.1 2.0 %collective-permute-start.12 = (bf16[384,768]{1,0:T(8,128)(2,1)S(1)}, bf16[384,768]{1,0:T(8,128)(2,1)S(1)}, u32[]{:S(2)}, u32[]{:S(2)}) collective-permute-start(bf16[384,768]{1,0:T(8,128)(2,1)S(1)} %get-tuple-element.38), channel_id=1, source_target_pairs={{0,2},{1,15},{2,4},{3,1},{4,6},{5,3},{6,8},{7,5},{8,10},{9,7},{10,... | collective-permute-start | bytes 1769480 | tf_op jit(solution)/shard_map/ppermute | solution.py:239
  40.1 0.8 %shard_map.63 = (f32[384,768]{1,0:T(8,128)S(1)}, bf16[384,768]{1,0:T(8,128)(2,1)S(1)}) custom-call(bf16[384,1792]{1,0:T(8,128)(2,1)S(1)} %collective-permute-done.2.far, bf16[384,768]{1,0:T(8,128)(2,1)S(1)} %get-tuple-element.31.coefficients, f32[384,768]{1,0:T(8,128)S(1)} %get-tuple-element.32.before), custom_call_target="tpu_custom_call" | custom-call | tf_op jit(solution)/shard_map/pallas_call | solution.py:170
  40.9 0.8 %collective-permute-done.6 = f32[8,128]{1,0:T(8,128)S(1)} collective-permute-done((f32[8,128]{1,0:T(8,128)S(1)}, f32[8,128]{1,0:T(8,128)S(1)}, u32[]{:S(2)}, u32[]{:S(2)}) %collective-permute-start.6) | collective-permute-done | bytes 4128 | tf_op jit(solution)/shard_map/ppermute | solution.py:242
  41.7 1.1 %collective-permute-start.11 = (bf16[384,768]{1,0:T(8,128)(2,1)S(1)}, bf16[384,768]{1,0:T(8,128)(2,1)S(1)}, u32[]{:S(2)}, u32[]{:S(2)}) collective-permute-start(bf16[384,768]{1,0:T(8,128)(2,1)S(1)} %get-tuple-element.37), channel_id=1, source_target_pairs={{0,1},{1,0},{2,3},{3,2},{4,5},{5,4},{6,7},{7,6},{8,9},{9,8},{10,11... | collective-permute-start | bytes 1769480 | tf_op jit(solution)/shard_map/ppermute | solution.py:244
  42.8 0.1 collective-permute-start.8
  42.9 1.6 %collective-permute-done.8 = f32[8,128]{1,0:T(8,128)S(1)} collective-permute-done((f32[8,128]{1,0:T(8,128)S(1)}, f32[8,128]{1,0:T(8,128)S(1)}, u32[]{:S(2)}, u32[]{:S(2)}) %collective-permute-start.8) | collective-permute-done | bytes 4128 | tf_op jit(solution)/shard_map/ppermute | solution.py:246
  44.4 1.4 %collective-permute-start.9 = (f32[8,128]{1,0:T(8,128)S(1)}, f32[8,128]{1,0:T(8,128)S(1)}, u32[]{:S(2)}, u32[]{:S(2)}) collective-permute-start(f32[8,128]{1,0:T(8,128)S(1)} %add.16), channel_id=1, source_target_pairs={{0,16},{1,17},{2,18},{3,19},{4,20},{5,21},{6,22},{7,23},{8,24},{9,... | collective-permute-start | bytes 12296 | tf_op jit(solution)/shard_map/ppermute | solution.py:246
  45.8 2.3 %collective-permute-done.9 = f32[8,128]{1,0:T(8,128)S(1)} collective-permute-done((f32[8,128]{1,0:T(8,128)S(1)}, f32[8,128]{1,0:T(8,128)S(1)}, u32[]{:S(2)}, u32[]{:S(2)}) %collective-permute-start.9) | collective-permute-done | bytes 4128 | tf_op jit(solution)/shard_map/ppermute | solution.py:246
  48.0 2.1 %collective-permute-start.10 = (f32[8,128]{1,0:T(8,128)S(1)}, f32[8,128]{1,0:T(8,128)S(1)}, u32[]{:S(2)}, u32[]{:S(2)}) collective-permute-start(f32[8,128]{1,0:T(8,128)S(1)} %add.17), channel_id=1, source_target_pairs={{0,8},{1,9},{2,10},{3,11},{4,12},{5,13},{6,14},{7,15},{8,0},{9,1},... | collective-permute-start | bytes 12296 | tf_op jit(solution)/shard_map/ppermute | solution.py:246
  50.2 2.4 %collective-permute-done.10 = f32[8,128]{1,0:T(8,128)S(1)} collective-permute-done((f32[8,128]{1,0:T(8,128)S(1)}, f32[8,128]{1,0:T(8,128)S(1)}, u32[]{:S(2)}, u32[]{:S(2)}) %collective-permute-start.10) | collective-permute-done | bytes 4128 | tf_op jit(solution)/shard_map/ppermute | solution.py:246
  52.5 1.1 %collective-permute-start.13 = (f32[8,128]{1,0:T(8,128)S(1)}, f32[8,128]{1,0:T(8,128)S(1)}, u32[]{:S(2)}, u32[]{:S(2)}) collective-permute-start(f32[8,128]{1,0:T(8,128)S(1)} %add.18), channel_id=1, source_target_pairs={{0,4},{1,5},{2,6},{3,7},{4,0},{5,1},{6,2},{7,3},{8,12},{9,13},{10,... | collective-permute-start | bytes 12296 | tf_op jit(solution)/shard_map/ppermute | solution.py:247
  53.7 1.6 %shard_map.64 = f32[384,768]{1,0:T(8,128)} custom-call(bf16[400,768]{1,0:T(8,128)(2,1)S(1)} %get-tuple-element.22.own_s.own, f32[384,128]{1,0:T(8,128)S(1)} %get-tuple-element.35.scale, f32[384,768]{1,0:T(8,128)S(1)} %get-tuple-element.36.total, bf16[384,768]{1,0:T(8,128)(2,1)S(1)} %collective-permute-done.11.from_near, ...), custom_call_target="tpu_custom_call" | custom-call | tf_op jit(solution)/shard_map/pallas_call | solution.py:170
  55.3 0.9 %collective-permute-done.13 = f32[8,128]{1,0:T(8,128)S(1)} collective-permute-done((f32[8,128]{1,0:T(8,128)S(1)}, f32[8,128]{1,0:T(8,128)S(1)}, u32[]{:S(2)}, u32[]{:S(2)}) %collective-permute-start.13) | collective-permute-done | bytes 4128 | tf_op jit(solution)/shard_map/ppermute | solution.py:247
  56.2 0.6 %shard_map.65 = f32[1,1]{1,0:T(1,128)} custom-call(f32[8,128]{1,0:T(8,128)S(1)} %add.19.sums), custom_call_target="tpu_custom_call" | custom-call | tf_op jit(solution)/shard_map/pallas_call | solution.py:170
  (10 shorter events, 0.0 us)
Async XLA Ops:
  0.6 13.9 %copy-start = (s32[384]{0:T(512)S(1)}, s32[384]{0:T(512)}, u32[]{:S(2)}) copy-start(s32[384]{0:T(512)} %counts_hbm.1) | copy-start | bytes 4612
  2.3 34.1 %collective-permute-start.2 = (bf16[384,1792]{1,0:T(8,128)(2,1)S(1)}, bf16[384,1792]{1,0:T(8,128)(2,1)S(1)}, u32[]{:S(2)}, u32[]{:S(2)}) collective-permute-start(bf16[384,1792]{1,0:T(8,128)(2,1)S(1)} %get-tuple-element.23.both), channel_id=1, source_target_pairs={{0,14},{1,3},{2,0},{3,5},{4,2},{5,7},{6,4},{7,9},{8,6},{9,11},{10,... | collective-permute-start | bytes 4128776 | tf_op jit(solution)/shard_map/ppermute | solution.py:223
  8.3 6.8 %collective-permute-start.1 = (bf16[384,1024]{1,0:T(8,128)(2,1)S(1)}, bf16[384,1024]{1,0:T(8,128)(2,1)S(1)}, u32[]{:S(2)}, u32[]{:S(2)}) collective-permute-start(bf16[384,1024]{1,0:T(8,128)(2,1)S(1)} %get-tuple-element.24.own_t), channel_id=1, source_target_pairs={{0,1},{1,0},{2,3},{3,2},{4,5},{5,4},{6,7},{7,6},{8,9},{9,8},{10,11... | collective-permute-start | bytes 2359304 | tf_op jit(solution)/shard_map/ppermute | solution.py:224
  8.3 19.5 %collective-permute-start.5 = (bf16[384,1024]{1,0:T(8,128)(2,1)S(1)}, bf16[384,1024]{1,0:T(8,128)(2,1)S(1)}, u32[]{:S(2)}, u32[]{:S(2)}) collective-permute-start(bf16[384,1024]{1,0:T(8,128)(2,1)S(1)} %get-tuple-element.24.own_t), channel_id=1, source_target_pairs={{0,16},{2,18},{4,20},{6,22},{8,24},{10,26},{12,28},{14,30},{17,1},... | collective-permute-start | bytes 2359304 | tf_op jit(solution)/shard_map/ppermute | solution.py:224
  11.8 2.7 %collective-permute-start = (bf16[400,768]{1,0:T(8,128)(2,1)S(1)}, bf16[400,768]{1,0:T(8,128)(2,1)S(1)}, u32[]{:S(2)}, u32[]{:S(2)}) collective-permute-start(bf16[400,768]{1,0:T(8,128)(2,1)S(1)} %get-tuple-element.22.own_s.own), channel_id=1, source_target_pairs={{0,1},{1,0},{2,3},{3,2},{4,5},{5,4},{6,7},{7,6},{8,9},{9,8},{10,11... | collective-permute-start | bytes 1843208 | tf_op jit(solution)/shard_map/ppermute | solution.py:224
  11.9 15.9 %collective-permute-start.4 = (bf16[400,768]{1,0:T(8,128)(2,1)S(1)}, bf16[400,768]{1,0:T(8,128)(2,1)S(1)}, u32[]{:S(2)}, u32[]{:S(2)}) collective-permute-start(bf16[400,768]{1,0:T(8,128)(2,1)S(1)} %get-tuple-element.22.own_s.own), channel_id=1, source_target_pairs={{0,16},{2,18},{4,20},{6,22},{8,24},{10,26},{12,28},{14,30},{17,1},... | collective-permute-start | bytes 1843208 | tf_op jit(solution)/shard_map/ppermute | solution.py:224
  14.5 21.8 %collective-permute-start.3 = (s32[384]{0:T(512)S(1)}, s32[384]{0:T(512)S(1)}, u32[]{:S(2)}, u32[]{:S(2)}) collective-permute-start(s32[384]{0:T(512)S(1)} %copy-done), channel_id=1, source_target_pairs={{0,14},{1,3},{2,0},{3,5},{4,2},{5,7},{6,4},{7,9},{8,6},{9,11},{10,... | collective-permute-start | bytes 4616 | tf_op jit(solution)/shard_map/ppermute | solution.py:223
  29.6 12.1 %collective-permute-start.7 = (bf16[384,768]{1,0:T(8,128)(2,1)S(1)}, bf16[384,768]{1,0:T(8,128)(2,1)S(1)}, u32[]{:S(2)}, u32[]{:S(2)}) collective-permute-start(bf16[384,768]{1,0:T(8,128)(2,1)S(1)} %get-tuple-element.30), channel_id=1, source_target_pairs={{1,17},{3,19},{5,21},{7,23},{9,25},{11,27},{13,29},{15,31},{16,0},... | collective-permute-start | bytes 1769480 | tf_op jit(solution)/shard_map/ppermute | solution.py:232
  38.0 3.7 %collective-permute-start.6 = (f32[8,128]{1,0:T(8,128)S(1)}, f32[8,128]{1,0:T(8,128)S(1)}, u32[]{:S(2)}, u32[]{:S(2)}) collective-permute-start(f32[8,128]{1,0:T(8,128)S(1)} %get-tuple-element.29), channel_id=1, source_target_pairs={{0,2},{1,3},{2,0},{3,1},{4,6},{5,7},{6,4},{7,5},{8,10},{9,11},{10,... | collective-permute-start | bytes 12296 | tf_op jit(solution)/shard_map/ppermute | solution.py:242
  38.1 15.6 %collective-permute-start.12 = (bf16[384,768]{1,0:T(8,128)(2,1)S(1)}, bf16[384,768]{1,0:T(8,128)(2,1)S(1)}, u32[]{:S(2)}, u32[]{:S(2)}) collective-permute-start(bf16[384,768]{1,0:T(8,128)(2,1)S(1)} %get-tuple-element.38), channel_id=1, source_target_pairs={{0,2},{1,15},{2,4},{3,1},{4,6},{5,3},{6,8},{7,5},{8,10},{9,7},{10,... | collective-permute-start | bytes 1769480 | tf_op jit(solution)/shard_map/ppermute | solution.py:239
  41.7 12.0 %collective-permute-start.11 = (bf16[384,768]{1,0:T(8,128)(2,1)S(1)}, bf16[384,768]{1,0:T(8,128)(2,1)S(1)}, u32[]{:S(2)}, u32[]{:S(2)}) collective-permute-start(bf16[384,768]{1,0:T(8,128)(2,1)S(1)} %get-tuple-element.37), channel_id=1, source_target_pairs={{0,1},{1,0},{2,3},{3,2},{4,5},{5,4},{6,7},{7,6},{8,9},{9,8},{10,11... | collective-permute-start | bytes 1769480 | tf_op jit(solution)/shard_map/ppermute | solution.py:244
  42.8 1.6 %collective-permute-start.8 = (f32[8,128]{1,0:T(8,128)S(1)}, f32[8,128]{1,0:T(8,128)S(1)}, u32[]{:S(2)}, u32[]{:S(2)}) collective-permute-start(f32[8,128]{1,0:T(8,128)S(1)} %add.15), channel_id=1, source_target_pairs={{0,1},{1,0},{2,3},{3,2},{4,5},{5,4},{6,7},{7,6},{8,9},{9,8},{10,11... | collective-permute-start | bytes 12296 | tf_op jit(solution)/shard_map/ppermute | solution.py:246
  44.4 3.6 %collective-permute-start.9 = (f32[8,128]{1,0:T(8,128)S(1)}, f32[8,128]{1,0:T(8,128)S(1)}, u32[]{:S(2)}, u32[]{:S(2)}) collective-permute-start(f32[8,128]{1,0:T(8,128)S(1)} %add.16), channel_id=1, source_target_pairs={{0,16},{1,17},{2,18},{3,19},{4,20},{5,21},{6,22},{7,23},{8,24},{9,... | collective-permute-start | bytes 12296 | tf_op jit(solution)/shard_map/ppermute | solution.py:246
  48.0 4.5 %collective-permute-start.10 = (f32[8,128]{1,0:T(8,128)S(1)}, f32[8,128]{1,0:T(8,128)S(1)}, u32[]{:S(2)}, u32[]{:S(2)}) collective-permute-start(f32[8,128]{1,0:T(8,128)S(1)} %add.17), channel_id=1, source_target_pairs={{0,8},{1,9},{2,10},{3,11},{4,12},{5,13},{6,14},{7,15},{8,0},{9,1},... | collective-permute-start | bytes 12296 | tf_op jit(solution)/shard_map/ppermute | solution.py:246
  52.5 3.6 %collective-permute-start.13 = (f32[8,128]{1,0:T(8,128)S(1)}, f32[8,128]{1,0:T(8,128)S(1)}, u32[]{:S(2)}, u32[]{:S(2)}) collective-permute-start(f32[8,128]{1,0:T(8,128)S(1)} %add.18), channel_id=1, source_target_pairs={{0,4},{1,5},{2,6},{3,7},{4,0},{5,1},{6,2},{7,3},{8,12},{9,13},{10,... | collective-permute-start | bytes 12296 | tf_op jit(solution)/shard_map/ppermute | solution.py:247

commit v4 on v3

--- a/solution.py
+++ b/solution.py
@@ -58,28 +58,32 @@
 
 
 class Packed:
-    def __init__(self, student, teacher, rows):
-        self.student, self.teacher, self.rows = student, teacher, rows
+    def __init__(self, first, second, rows, ds):
+        self.first, self.second, self.rows, self.ds = first, second, rows, ds
 
     @property
     def s(self):
-        return self.student[: self.rows]
+        return self.first[: self.rows, : self.ds]
 
     @property
     def t(self):
-        return self.teacher[...]
-
-    def counts(self):
-        return self.student[self.rows :].astype(F32)[0:1, : self.rows]
+        return jnp.concatenate([self.first[: self.rows, self.ds :], self.second[...]], axis=1)
+
+    def meta(self):
+        return self.first[self.rows :, : self.ds].astype(F32)
+
+    def counts(self, count=None):
+        return self.meta()[0:1, : count or self.rows]
 
     def switch(self, if_even, if_odd):
         odd = lax.axis_index("member") % 2 == 1
-        plan = self.student[self.rows :].astype(F32)[1:2, :128]
+        plan = self.meta()[1:2, :128]
         return jnp.where(odd, plan[:, if_odd : if_odd + 1], plan[:, if_even : if_even + 1])
 
 
-def pack_kernel(counts_hbm, plan_hbm, s_hbm, t_hbm, both, student, teacher, scale, counts, plan, s, t, arrived):
+def pack_kernel(counts_hbm, plan_hbm, s_hbm, t_hbm, both, first, second, student, numbers, scale, counts, plan, s, t, arrived):
     rows, ds = s.shape
+    more = first.shape[1] - ds
     copies = [
         pltpu.make_async_copy(source, target, arrived.at[i])
         for i, (source, target) in enumerate(((s_hbm, s), (t_hbm, t), (counts_hbm, counts), (plan_hbm, plan)))
@@ -89,63 +93,74 @@
     copies[0].wait()
     unit, factor = units(s[...])
     scale[...] = jnp.broadcast_to(factor, scale.shape)
+    student[...] = unit
     both[:, :ds] = unit
-    student[:rows] = unit
+    first[:rows, :ds] = unit
     copies[1].wait()
     unit, _ = units(t[...])
     both[:, ds:] = unit
-    teacher[...] = unit
+    first[:rows, ds:] = unit[:, :more]
+    second[...] = unit[:, more:]
 
     def widen(values):
-        return jnp.concatenate([values, jnp.zeros((1, ds - values.shape[1]), F32)], axis=1)
+        return jnp.concatenate([values, jnp.zeros((1, first.shape[1] - values.shape[1]), F32)], axis=1)
 
     copies[2].wait()
     copies[3].wait()
-    at = lax.broadcasted_iota(jnp.int32, (META, ds), 0)
+    at = lax.broadcasted_iota(jnp.int32, (META, first.shape[1]), 0)
     meta = jnp.where(at == 0, widen(counts[...].astype(F32).reshape(1, rows)), 0.0)
-    student[rows:] = jnp.where(at == 1, widen(plan[...].astype(F32)), meta).astype(BF16)
-
-
-def local_kernel(rows, both, own_s, own_t, near_s, near_t, mates, total, sums):
-    own, near = Packed(own_s, own_t, rows), Packed(near_s, near_t, rows)
+    first[rows:] = jnp.where(at == 1, widen(plan[...].astype(F32)), meta).astype(BF16)
+    numbers[...] = first[rows:, :ds]
+
+
+def local_kernel(rows, ds, both, first, near_meta, near_student, near_teacher, mates, total, sums):
+    own, near = Packed(first, None, rows, ds), Packed(near_meta, None, 0, ds)
     mates[:rows] = both[...]
-    mates[rows:] = jnp.concatenate([near.s, near.t], axis=1)
+    mates[rows:, :ds], _ = units(near_student[...])
+    mates[rows:, ds:], _ = units(near_teacher[...])
+    own_s, own_t, near_s, near_t = mates[:rows, :ds], mates[:rows, ds:], mates[rows:, :ds], mates[rows:, ds:]
     own_column = column(own.counts())
-    mismatch = similarity(own.s, own.s) - similarity(own.t, own.t)
+    mismatch = similarity(own_s, own_s) - similarity(own_t, own_t)
     coefficient, loss, weight = weigh(mismatch, own_column, own.counts())
-    total[...] = dot(coefficient, own.s)
-    mismatch = similarity(own.s, near.s) - similarity(own.t, near.t)
-    coefficient, loss_2, weight_2 = weigh(mismatch, own_column, near.counts() * own.switch(2, 0))
-    total[...] += dot(coefficient, near.s)
+    total[...] = dot(coefficient, own_s)
+    mismatch = similarity(own_s, near_s) - similarity(own_t, near_t)
+    coefficient, loss_2, weight_2 = weigh(mismatch, own_column, near.counts(rows) * own.switch(2, 0))
+    total[...] += dot(coefficient, near_s)
     sums[...] = tile(loss + loss_2, weight + weight_2)
 
 
-def cross_kernel(rows, own_s, own_t, far_s, far_t, before, sums_before, total, give, sums):
-    own, far = Packed(own_s, own_t, rows), Packed(far_s, far_t, rows)
-    mismatch = similarity(own.s, far.s) - similarity(own.t, far.t)
+def cross_kernel(rows, ds, both, first, far_first, far_second, before, sums_before, total, give, sums):
+    own, far = Packed(first, None, rows, ds), Packed(far_first, far_second, rows, ds)
+    mismatch = similarity(both[:, :ds], far.s) - similarity(both[:, ds:], far.t)
     coefficient, loss, weight = weigh(mismatch, column(own.counts()), far.counts() * own.switch(4, 4))
-    give[...] = dot_transposed(coefficient, own.s).astype(BF16)
+    give[...] = dot_transposed(coefficient, both[:, :ds]).astype(BF16)
     total[...] = before[...] + dot(coefficient, far.s)
     sums[...] = sums_before[...] + tile(2.0 * loss, 2.0 * weight)
 
 
-def ring_kernel(rows, own_s, near_s, mates, far, far_counts, sums_before, coefficients, to_far, sums):
-    own, near, ds = Packed(own_s, None, rows), Packed(near_s, None, rows), own_s.shape[1]
-    mismatch = similarity(far[:, :ds], mates[:, :ds]) - similarity(far[:, ds:], mates[:, ds:])
-    mates_row = jnp.concatenate([own.counts() * own.switch(3, 1), near.counts() * near.switch(2, 0)], axis=1)
+def ring_teacher_kernel(ds, mates, far, teacher_sim):
+    unit, _ = units(far[...])
+    teacher_sim[...] = similarity(unit, mates[:, ds:])
+
+
+def ring_kernel(
+    rows, ds, first, near_meta, mates, teacher_sim, far_s, far_counts, sums_before, coefficients, to_far, sums
+):
+    own, near = Packed(first, None, rows, ds), Packed(near_meta, None, 0, ds)
+    mismatch = similarity(far_s[...], mates[:, :ds]) - teacher_sim[...]
+    mates_row = jnp.concatenate([own.counts() * own.switch(3, 1), near.counts(rows) * near.switch(2, 0)], axis=1)
     far_column = column(far_counts[...].astype(F32).reshape(1, rows))
     coefficients[...], loss, weight = weigh(mismatch, far_column, mates_row, twice=rows)
-    to_far[...] = dot(coefficients[:, :rows], own.s).astype(BF16)
+    to_far[...] = dot(coefficients[:, :rows], mates[:rows, :ds]).astype(BF16)
     sums[...] = sums_before[...] + tile(loss, weight)
 
 
-def ring_mix_kernel(rows, far, coefficients, before, total, to_near):
-    far_s = far[:, : before.shape[1]]
-    to_near[...] = dot_transposed(coefficients[:, rows:], far_s).astype(BF16)
-    total[...] = before[...] + dot_transposed(coefficients[:, :rows], far_s)
-
-
-def final_kernel(rows, own, scale, total, from_near, from_far, from_cross, grad, result, sent):
+def ring_mix_kernel(rows, ds, far_s, coefficients, before, total, to_near):
+    to_near[...] = dot_transposed(coefficients[:, rows:], far_s[...]).astype(BF16)
+    total[...] = before[...] + dot_transposed(coefficients[:, :rows], far_s[...])
+
+
+def final_kernel(rows, ds, own, scale, total, from_near, from_far, from_cross, grad, result, sent):
     size = rows // PIECES
     copies = []
     for i in range(PIECES):
@@ -204,11 +219,16 @@
     acc, half, sums_shape = f((rows, ds), F32), f((rows, ds), BF16), f((8, 128), F32)
 
     def on_blocks(kernel):
-        return functools.partial(kernel, rows)
-
-    both, own_s, own_t, scale = call(
+        return functools.partial(kernel, rows, ds)
+
+    ring_t, near_t, near_s = to_ring(teacher), to_near(teacher), to_near(student)
+    width = (ds + dt) // 2
+    both, first, second, own_s, own_meta, scale = call(
         pack_kernel,
-        (f((rows, ds + dt), BF16), f((rows + META, ds), BF16), f((rows, dt), BF16), f((rows, 128), F32)),
+        (
+            f((rows, ds + dt), BF16), f((rows + META, width), BF16), f((rows, ds + dt - width), BF16),
+            f((rows, ds), BF16), f((META, ds), BF16), f((rows, 128), F32),
+        ),
         24,
         *(pltpu.with_memory_space_constraint(x, pltpu.HBM) for x in (counts, plan.reshape(1, -1), student, teacher)),
         in_specs=[pl.BlockSpec(memory_space=pltpu.HBM)] * 4,
@@ -220,29 +240,36 @@
             pltpu.SemaphoreType.DMA((4,)),
         ],
     )
-    ring, ring_counts = to_ring(both), to_ring(counts)
-    near, cross = (to_near(own_s), to_near(own_t)), (to_cross(own_s), to_cross(own_t))
+    ring_s, ring_counts = to_ring(own_s), to_ring(counts)
+    near_meta, cross = to_near(own_meta), (to_cross(first), to_cross(second))
 
     mates, total, sums = call(
-        on_blocks(local_kernel), (f((2 * rows, ds + dt), BF16), acc, sums_shape), 24, both, own_s, own_t, *near
+        on_blocks(local_kernel), (f((2 * rows, ds + dt), BF16), acc, sums_shape), 24, both, first, near_meta, near_s, near_t
     )
     total, give_cross, sums = call(
-        on_blocks(cross_kernel), (acc, half, sums_shape), 24, own_s, own_t, *cross, total, sums
+        on_blocks(cross_kernel), (acc, half, sums_shape), 24, both, first, *cross, total, sums
     )
     from_cross = cross_back(give_cross)
+    (teacher_sim,) = call(
+        functools.partial(ring_teacher_kernel, ds), (f((rows, 2 * rows), F32),), 24, mates, ring_t
+    )
     coefficients, give_ring, sums = call(
         on_blocks(ring_kernel), (f((rows, 2 * rows), BF16), half, sums_shape), 24,
-        own_s, near[0], mates, ring, ring_counts, sums,
+        first, near_meta, mates, teacher_sim, ring_s, ring_counts, sums,
         flops=10**10,
     )
-    total, give_near = call(on_blocks(ring_mix_kernel), (acc, half), 24, ring, coefficients, total)
+    total, give_near = call(on_blocks(ring_mix_kernel), (acc, half), 24, ring_s, coefficients, total)
     from_ring = ring_back(give_ring)
     across = [route(lambda g, m, bit=bit: (g ^ bit, m)) for bit in powers(1, groups)]
     along = [route(lambda g, m, bit=bit: (g, m ^ bit)) for bit in powers(2, members)]
     sums = sums + along[0](sums)
-    sums, from_cross, give_near = lax.optimization_barrier((sums, from_cross, give_near))
+    sums, give_near = lax.optimization_barrier((sums, give_near))
     from_near = to_near(give_near)
-    for exchange in [to_near] + across + along[:1:-1]:
+    sums = sums + to_near(sums)
+    for exchange in across:
+        sums = sums + exchange(sums)
+    sums, from_cross = lax.optimization_barrier((sums, from_cross))
+    for exchange in along[:1:-1]:
         sums = sums + exchange(sums)
     received = along[1](sums)
 

time: 57 us -> 55.7 us (0.977)
  waiting for transfers between devices: 23.4 us -> 20.8 us
  starting transfers between devices: 21.9 us -> 23 us
    ppermute x3 -> x2, waiting for transfers between devices: 6.2 us -> 4.75 us  [per_device(): sums = sums + exchange(sums)]
    ppermute x6 -> x9, waiting for transfers between devices: 15.5 us -> 14.4 us  [the longest x3 9.74 us: per_device(): near_meta, cross = (to_near(own_meta), (to_cross(first), to_cross(second)))]
    ppermute x6 -> x9, starting transfers between devices: 12.8 us -> 13.9 us  [the longest x1 5.96 us: per_device(): to_ring(teacher)]
    pallas_call x7 -> x8, Pallas kernels: 10.6 us -> 10.9 us  [call(): pl.pallas_call(kernel, out_shape=outs, compiler_params=pltpu.CompilerPara...]
    ppermute x3 -> x2, starting transfers between devices: 3.56 us -> 3.38 us  [per_device(): sums = sums + exchange(sums)]
  transfers between devices with their start and end apart: 14 -> 16, of which waited for: 7 -> 8; matrix products, arithmetic and copies ran while one was open for 0% -> 0% of each run, Pallas kernels for 15% -> 18%
where the time goes in v4:
time: 55.7 us; the launch traced here: 55.5 us
  starting transfers between devices  23 us (41%)
  waiting for transfers between devices  20.8 us (37%)
  Pallas kernels  10.9 us (20%)
  between operations  0.76 us (1%)
    pallas_call x8, Pallas kernels, call(): pl.pallas_call(kernel, out_shape=outs, compiler_params=pltpu.CompilerPara...  10.9 us
    ppermute x3, waiting for transfers between devices, per_device(): near_meta, cross = (to_near(own_meta), (to_cross(first), to_cross(second)))  9.74 us
    ppermute x1, starting transfers between devices, per_device(): to_ring(teacher)  5.96 us
    ppermute x3, starting transfers between devices, per_device(): near_meta, cross = (to_near(own_meta), (to_cross(first), to_cross(second)))  4.86 us
    ppermute x2, waiting for transfers between devices, per_device(): sums = sums + exchange(sums)  4.75 us
    ppermute x2, starting transfers between devices, per_device(): sums = sums + exchange(sums)  3.38 us
    ppermute x2, waiting for transfers between devices, per_device(): ring_s, ring_counts = (to_ring(own_s), to_ring(counts))  3.06 us
    ppermute x2, starting transfers between devices, per_device(): ring_s, ring_counts = (to_ring(own_s), to_ring(counts))  2.37 us
  transfers between devices with their start and end apart: 16, of which 8 were waited for; matrix products, arithmetic and copies ran while one was open for 0% of the time, Pallas kernels for 18%

profile of v4, /device:TPU:0, one launch (start us, length us, event | category | flops | bytes accessed | tf_op | source)
XLA Modules:
  0.0 55.5 jit_solution(18409674208799330420)
XLA Ops:
  0.6 0.5 collective-permute-start.1
  1.2 0.1 collective-permute-start.2
  1.2 6.0 %collective-permute-start.3 = (bf16[384,1024]{1,0:T(8,128)(2,1)}, bf16[384,1024]{1,0:T(8,128)(2,1)S(1)}, u32[]{:S(2)}, u32[]{:S(2)}) collective-permute-start(bf16[384,1024]{1,0:T(8,128)(2,1)} %t_hbm.1), channel_id=1, source_target_pairs={{0,14},{1,3},{2,0},{3,5},{4,2},{5,7},{6,4},{7,9},{8,6},{9,11},{10,... | collective-permute-start | bytes 2359304 | tf_op jit(solution)/shard_map/ppermute | solution.py:224
  7.2 1.6 %shard_map.59 = (bf16[384,1792]{1,0:T(8,128)(2,1)S(1)}, bf16[400,896]{1,0:T(8,128)(2,1)S(1)}, bf16[384,896]{1,0:T(8,128)(2,1)S(1)}, bf16[384,768]{1,0:T(8,128)(2...) custom-call(s32[384]{0:T(512)} %counts_hbm.1, s32[1,5]{1,0:T(1,128)} %bitcast.2, bf16[384,768]{1,0:T(8,128)(2,1)} %s_hbm.1, ...), custom_call_target="tpu_custom_call" | custom-call | tf_op jit(solution)/shard_map/pallas_call | solution.py:185
  8.8 3.5 %collective-permute-start.6 = (bf16[400,896]{1,0:T(8,128)(2,1)S(1)}, bf16[400,896]{1,0:T(8,128)(2,1)S(1)}, u32[]{:S(2)}, u32[]{:S(2)}) collective-permute-start(bf16[400,896]{1,0:T(8,128)(2,1)S(1)} %get-tuple-element.25.first), channel_id=1, source_target_pairs={{0,16},{2,18},{4,20},{6,22},{8,24},{10,26},{12,28},{14,30},{17,1},... | collective-permute-start | bytes 2150408 | tf_op jit(solution)/shard_map/ppermute | solution.py:244
  12.3 0.1 collective-permute-start
  12.4 1.2 %collective-permute-done.near_meta = bf16[16,768]{1,0:T(8,128)(2,1)S(1)} collective-permute-done((bf16[16,768]{1,0:T(8,128)(2,1)S(1)}, bf16[16,768]{1,0:T(8,128)(2,1)S(1)}, u32[]{:S(2)}, u32[]{:S(2)}) %collective-permute-start) | collective-permute-done | bytes 24608 | tf_op jit(solution)/shard_map/ppermute | solution.py:244
  13.6 1.3 %collective-permute-start.7 = (bf16[384,896]{1,0:T(8,128)(2,1)S(1)}, bf16[384,896]{1,0:T(8,128)(2,1)S(1)}, u32[]{:S(2)}, u32[]{:S(2)}) collective-permute-start(bf16[384,896]{1,0:T(8,128)(2,1)S(1)} %get-tuple-element.30), channel_id=1, source_target_pairs={{0,16},{2,18},{4,20},{6,22},{8,24},{10,26},{12,28},{14,30},{17,1},... | collective-permute-start | bytes 2064392 | tf_op jit(solution)/shard_map/ppermute | solution.py:244
  14.9 0.6 %collective-permute-start.4 = (bf16[384,768]{1,0:T(8,128)(2,1)S(1)}, bf16[384,768]{1,0:T(8,128)(2,1)S(1)}, u32[]{:S(2)}, u32[]{:S(2)}) collective-permute-start(bf16[384,768]{1,0:T(8,128)(2,1)S(1)} %get-tuple-element.29.own), channel_id=1, source_target_pairs={{0,14},{1,3},{2,0},{3,5},{4,2},{5,7},{6,4},{7,9},{8,6},{9,11},{10,... | collective-permute-start | bytes 1769480 | tf_op jit(solution)/shard_map/ppermute | solution.py:243
  15.6 1.7 %collective-permute-start.5 = (s32[384]{0:T(512)S(1)}, s32[384]{0:T(512)S(1)}, u32[]{:S(2)}, u32[]{:S(2)}) collective-permute-start(s32[384]{0:T(512)S(1)} %copy-done), channel_id=1, source_target_pairs={{0,14},{1,3},{2,0},{3,5},{4,2},{5,7},{6,4},{7,9},{8,6},{9,11},{10,... | collective-permute-start | bytes 4616 | tf_op jit(solution)/shard_map/ppermute | solution.py:243
  17.3 2.5 %shard_map.60 = (bf16[768,1792]{1,0:T(8,128)(2,1)S(1)}, f32[384,768]{1,0:T(8,128)S(1)}, f32[8,128]{1,0:T(8,128)S(1)}) custom-call(bf16[384,1792]{1,0:T(8,128)(2,1)S(1)} %get-tuple-element.27.both, bf16[400,896]{1,0:T(8,128)(2,1)S(1)} %get-tuple-element.25.first, bf16[16,768]{1,0:T(8,128)(2,1)S(1)} %collective-permute-done.near_meta, ...), custom_call_target="tpu_custom_call" | custom-call | tf_op jit(solution)/shard_map/pallas_call | solution.py:185
  19.8 8.6 %collective-permute-done.7.far_second = bf16[384,896]{1,0:T(8,128)(2,1)S(1)} collective-permute-done((bf16[384,896]{1,0:T(8,128)(2,1)S(1)}, bf16[384,896]{1,0:T(8,128)(2,1)S(1)}, u32[]{:S(2)}, u32[]{:S(2)}) %collective-permute-start.7) | collective-permute-done | bytes 688160 | tf_op jit(solution)/shard_map/ppermute | solution.py:244
  28.4 1.8 %shard_map.62 = (f32[384,768]{1,0:T(8,128)S(1)}, bf16[384,768]{1,0:T(8,128)(2,1)S(1)}, f32[8,128]{1,0:T(8,128)S(1)}) custom-call(bf16[384,1792]{1,0:T(8,128)(2,1)S(1)} %get-tuple-element.27.both, bf16[400,896]{1,0:T(8,128)(2,1)S(1)} %get-tuple-element.25.first, bf16[400,896]{1,0:T(8,128)(2,1)S(1)} %collective-permute-done.6.far_first, ...), custom_call_target="tpu_custom_call" | custom-call | tf_op jit(solution)/shard_map/pallas_call | solution.py:185
  30.2 1.3 %collective-permute-start.11 = (bf16[384,768]{1,0:T(8,128)(2,1)S(1)}, bf16[384,768]{1,0:T(8,128)(2,1)S(1)}, u32[]{:S(2)}, u32[]{:S(2)}) collective-permute-start(bf16[384,768]{1,0:T(8,128)(2,1)S(1)} %get-tuple-element.39), channel_id=1, source_target_pairs={{1,17},{3,19},{5,21},{7,23},{9,25},{11,27},{13,29},{15,31},{16,0},... | collective-permute-start | bytes 1769480 | tf_op jit(solution)/shard_map/ppermute | solution.py:252
  31.5 0.9 %shard_map.61.teacher_sim = f32[384,768]{1,0:T(8,128)S(1)} custom-call(bf16[768,1792]{1,0:T(8,128)(2,1)S(1)} %get-tuple-element.28.mates, bf16[384,1024]{1,0:T(8,128)(2,1)S(1)} %collective-permute-done.3.far), custom_call_target="tpu_custom_call" | custom-call | tf_op jit(solution)/shard_map/pallas_call | solution.py:185
  32.4 3.1 %collective-permute-done.5.far_counts = s32[384]{0:T(512)S(1)} collective-permute-done((s32[384]{0:T(512)S(1)}, s32[384]{0:T(512)S(1)}, u32[]{:S(2)}, u32[]{:S(2)}) %collective-permute-start.5) | collective-permute-done | bytes 1568 | tf_op jit(solution)/shard_map/ppermute | solution.py:243
  35.4 1.0 %shard_map.63 = (bf16[384,768]{1,0:T(8,128)(2,1)S(1)}, bf16[384,768]{1,0:T(8,128)(2,1)S(1)}, f32[8,128]{1,0:T(8,128)S(1)}) custom-call(bf16[400,896]{1,0:T(8,128)(2,1)S(1)} %get-tuple-element.25.first, bf16[16,768]{1,0:T(8,128)(2,1)S(1)} %collective-permute-done.near_meta, bf16[768,1792]{1,0:T(8,128)(2,1)S(1)} %get-tuple-element.28.mates, ...), custom_call_target="tpu_custom_call" | custom-call | flops 10000000000 | tf_op jit(solution)/shard_map/pallas_call | solution.py:185
  36.5 0.1 collective-permute-start.8
  36.6 2.0 %collective-permute-start.14 = (bf16[384,768]{1,0:T(8,128)(2,1)S(1)}, bf16[384,768]{1,0:T(8,128)(2,1)S(1)}, u32[]{:S(2)}, u32[]{:S(2)}) collective-permute-start(bf16[384,768]{1,0:T(8,128)(2,1)S(1)} %get-tuple-element.44), channel_id=1, source_target_pairs={{0,2},{1,15},{2,4},{3,1},{4,6},{5,3},{6,8},{7,5},{8,10},{9,7},{10,... | collective-permute-start | bytes 1769480 | tf_op jit(solution)/shard_map/ppermute | solution.py:262
  38.6 0.8 %shard_map.64 = (f32[384,768]{1,0:T(8,128)S(1)}, bf16[384,768]{1,0:T(8,128)(2,1)S(1)}) custom-call(bf16[384,768]{1,0:T(8,128)(2,1)S(1)} %collective-permute-done.4.far_s, bf16[384,768]{1,0:T(8,128)(2,1)S(1)} %get-tuple-element.35.coefficients, f32[384,768]{1,0:T(8,128)S(1)} %get-tuple-element.36.before), custom_call_target="tpu_custom_call" | custom-call | tf_op jit(solution)/shard_map/pallas_call | solution.py:185
  39.4 0.8 %collective-permute-done.8 = f32[8,128]{1,0:T(8,128)S(1)} collective-permute-done((f32[8,128]{1,0:T(8,128)S(1)}, f32[8,128]{1,0:T(8,128)S(1)}, u32[]{:S(2)}, u32[]{:S(2)}) %collective-permute-start.8) | collective-permute-done | bytes 4128 | tf_op jit(solution)/shard_map/ppermute | solution.py:265
  40.2 1.3 %collective-permute-start.13 = (bf16[384,768]{1,0:T(8,128)(2,1)S(1)}, bf16[384,768]{1,0:T(8,128)(2,1)S(1)}, u32[]{:S(2)}, u32[]{:S(2)}) collective-permute-start(bf16[384,768]{1,0:T(8,128)(2,1)S(1)} %get-tuple-element.43), channel_id=1, source_target_pairs={{0,1},{1,0},{2,3},{3,2},{4,5},{5,4},{6,7},{7,6},{8,9},{9,8},{10,11... | collective-permute-start | bytes 1769480 | tf_op jit(solution)/shard_map/ppermute | solution.py:267
  41.5 0.1 collective-permute-start.9
  41.6 1.6 %collective-permute-done.9 = f32[8,128]{1,0:T(8,128)S(1)} collective-permute-done((f32[8,128]{1,0:T(8,128)S(1)}, f32[8,128]{1,0:T(8,128)S(1)}, u32[]{:S(2)}, u32[]{:S(2)}) %collective-permute-start.9) | collective-permute-done | bytes 4128 | tf_op jit(solution)/shard_map/ppermute | solution.py:268
  43.2 1.2 %collective-permute-start.10 = (f32[8,128]{1,0:T(8,128)S(1)}, f32[8,128]{1,0:T(8,128)S(1)}, u32[]{:S(2)}, u32[]{:S(2)}) collective-permute-start(f32[8,128]{1,0:T(8,128)S(1)} %add.16), channel_id=1, source_target_pairs={{0,16},{1,17},{2,18},{3,19},{4,20},{5,21},{6,22},{7,23},{8,24},{9,... | collective-permute-start | bytes 12296 | tf_op jit(solution)/shard_map/ppermute | solution.py:270
  44.4 2.4 %collective-permute-done.10 = f32[8,128]{1,0:T(8,128)S(1)} collective-permute-done((f32[8,128]{1,0:T(8,128)S(1)}, f32[8,128]{1,0:T(8,128)S(1)}, u32[]{:S(2)}, u32[]{:S(2)}) %collective-permute-start.10) | collective-permute-done | bytes 4128 | tf_op jit(solution)/shard_map/ppermute | solution.py:270
  46.8 2.1 %collective-permute-start.12 = (f32[8,128]{1,0:T(8,128)S(1)}, f32[8,128]{1,0:T(8,128)S(1)}, u32[]{:S(2)}, u32[]{:S(2)}) collective-permute-start(f32[8,128]{1,0:T(8,128)S(1)} %add.17), channel_id=1, source_target_pairs={{0,8},{1,9},{2,10},{3,11},{4,12},{5,13},{6,14},{7,15},{8,0},{9,1},... | collective-permute-start | bytes 12296 | tf_op jit(solution)/shard_map/ppermute | solution.py:273
  48.9 2.4 %collective-permute-done.12 = f32[8,128]{1,0:T(8,128)S(1)} collective-permute-done((f32[8,128]{1,0:T(8,128)S(1)}, f32[8,128]{1,0:T(8,128)S(1)}, u32[]{:S(2)}, u32[]{:S(2)}) %collective-permute-start.12) | collective-permute-done | bytes 4128 | tf_op jit(solution)/shard_map/ppermute | solution.py:273
  51.3 1.1 %collective-permute-start.15 = (f32[8,128]{1,0:T(8,128)S(1)}, f32[8,128]{1,0:T(8,128)S(1)}, u32[]{:S(2)}, u32[]{:S(2)}) collective-permute-start(f32[8,128]{1,0:T(8,128)S(1)} %add.18), channel_id=1, source_target_pairs={{0,4},{1,5},{2,6},{3,7},{4,0},{5,1},{6,2},{7,3},{8,12},{9,13},{10,... | collective-permute-start | bytes 12296 | tf_op jit(solution)/shard_map/ppermute | solution.py:274
  52.4 1.6 %shard_map.65 = f32[384,768]{1,0:T(8,128)} custom-call(bf16[384,768]{1,0:T(8,128)(2,1)S(1)} %get-tuple-element.29.own, f32[384,128]{1,0:T(8,128)S(1)} %get-tuple-element.41.scale, f32[384,768]{1,0:T(8,128)S(1)} %get-tuple-element.42.total, bf16[384,768]{1,0:T(8,128)(2,1)S(1)} %collective-permute-done.13.from_near, ...), custom_call_target="tpu_custom_call" | custom-call | tf_op jit(solution)/shard_map/pallas_call | solution.py:185
  54.0 0.9 %collective-permute-done.15 = f32[8,128]{1,0:T(8,128)S(1)} collective-permute-done((f32[8,128]{1,0:T(8,128)S(1)}, f32[8,128]{1,0:T(8,128)S(1)}, u32[]{:S(2)}, u32[]{:S(2)}) %collective-permute-start.15) | collective-permute-done | bytes 4128 | tf_op jit(solution)/shard_map/ppermute | solution.py:274
  54.9 0.6 %shard_map.66 = f32[1,1]{1,0:T(1,128)} custom-call(f32[8,128]{1,0:T(8,128)S(1)} %add.19.sums), custom_call_target="tpu_custom_call" | custom-call | tf_op jit(solution)/shard_map/pallas_call | solution.py:185
  (15 shorter events, 0.0 us)
Async XLA Ops:
  0.6 14.9 %copy-start = (s32[384]{0:T(512)S(1)}, s32[384]{0:T(512)}, u32[]{:S(2)}) copy-start(s32[384]{0:T(512)} %counts_hbm.1) | copy-start | bytes 4612
  0.6 14.3 %collective-permute-start.1 = (bf16[384,768]{1,0:T(8,128)(2,1)}, bf16[384,768]{1,0:T(8,128)(2,1)S(1)}, u32[]{:S(2)}, u32[]{:S(2)}) collective-permute-start(bf16[384,768]{1,0:T(8,128)(2,1)} %s_hbm.1), channel_id=1, source_target_pairs={{0,1},{1,0},{2,3},{3,2},{4,5},{5,4},{6,7},{7,6},{8,9},{9,8},{10,11... | collective-permute-start | bytes 1769480 | tf_op jit(solution)/shard_map/ppermute | solution.py:224
  1.2 14.4 %collective-permute-start.2 = (bf16[384,1024]{1,0:T(8,128)(2,1)}, bf16[384,1024]{1,0:T(8,128)(2,1)S(1)}, u32[]{:S(2)}, u32[]{:S(2)}) collective-permute-start(bf16[384,1024]{1,0:T(8,128)(2,1)} %t_hbm.1), channel_id=1, source_target_pairs={{0,1},{1,0},{2,3},{3,2},{4,5},{5,4},{6,7},{7,6},{8,9},{9,8},{10,11... | collective-permute-start | bytes 2359304 | tf_op jit(solution)/shard_map/ppermute | solution.py:224
  1.2 30.2 %collective-permute-start.3 = (bf16[384,1024]{1,0:T(8,128)(2,1)}, bf16[384,1024]{1,0:T(8,128)(2,1)S(1)}, u32[]{:S(2)}, u32[]{:S(2)}) collective-permute-start(bf16[384,1024]{1,0:T(8,128)(2,1)} %t_hbm.1), channel_id=1, source_target_pairs={{0,14},{1,3},{2,0},{3,5},{4,2},{5,7},{6,4},{7,9},{8,6},{9,11},{10,... | collective-permute-start | bytes 2359304 | tf_op jit(solution)/shard_map/ppermute | solution.py:224
  8.8 19.6 %collective-permute-start.6 = (bf16[400,896]{1,0:T(8,128)(2,1)S(1)}, bf16[400,896]{1,0:T(8,128)(2,1)S(1)}, u32[]{:S(2)}, u32[]{:S(2)}) collective-permute-start(bf16[400,896]{1,0:T(8,128)(2,1)S(1)} %get-tuple-element.25.first), channel_id=1, source_target_pairs={{0,16},{2,18},{4,20},{6,22},{8,24},{10,26},{12,28},{14,30},{17,1},... | collective-permute-start | bytes 2150408 | tf_op jit(solution)/shard_map/ppermute | solution.py:244
  12.3 1.3 %collective-permute-start = (bf16[16,768]{1,0:T(8,128)(2,1)S(1)}, bf16[16,768]{1,0:T(8,128)(2,1)S(1)}, u32[]{:S(2)}, u32[]{:S(2)}) collective-permute-start(bf16[16,768]{1,0:T(8,128)(2,1)S(1)} %get-tuple-element.26), channel_id=1, source_target_pairs={{0,1},{1,0},{2,3},{3,2},{4,5},{5,4},{6,7},{7,6},{8,9},{9,8},{10,11... | collective-permute-start | bytes 73736 | tf_op jit(solution)/shard_map/ppermute | solution.py:244
  13.6 14.8 %collective-permute-start.7 = (bf16[384,896]{1,0:T(8,128)(2,1)S(1)}, bf16[384,896]{1,0:T(8,128)(2,1)S(1)}, u32[]{:S(2)}, u32[]{:S(2)}) collective-permute-start(bf16[384,896]{1,0:T(8,128)(2,1)S(1)} %get-tuple-element.30), channel_id=1, source_target_pairs={{0,16},{2,18},{4,20},{6,22},{8,24},{10,26},{12,28},{14,30},{17,1},... | collective-permute-start | bytes 2064392 | tf_op jit(solution)/shard_map/ppermute | solution.py:244
  14.9 20.5 %collective-permute-start.4 = (bf16[384,768]{1,0:T(8,128)(2,1)S(1)}, bf16[384,768]{1,0:T(8,128)(2,1)S(1)}, u32[]{:S(2)}, u32[]{:S(2)}) collective-permute-start(bf16[384,768]{1,0:T(8,128)(2,1)S(1)} %get-tuple-element.29.own), channel_id=1, source_target_pairs={{0,14},{1,3},{2,0},{3,5},{4,2},{5,7},{6,4},{7,9},{8,6},{9,11},{10,... | collective-permute-start | bytes 1769480 | tf_op jit(solution)/shard_map/ppermute | solution.py:243
  15.6 19.9 %collective-permute-start.5 = (s32[384]{0:T(512)S(1)}, s32[384]{0:T(512)S(1)}, u32[]{:S(2)}, u32[]{:S(2)}) collective-permute-start(s32[384]{0:T(512)S(1)} %copy-done), channel_id=1, source_target_pairs={{0,14},{1,3},{2,0},{3,5},{4,2},{5,7},{6,4},{7,9},{8,6},{9,11},{10,... | collective-permute-start | bytes 4616 | tf_op jit(solution)/shard_map/ppermute | solution.py:243
  30.2 16.6 %collective-permute-start.11 = (bf16[384,768]{1,0:T(8,128)(2,1)S(1)}, bf16[384,768]{1,0:T(8,128)(2,1)S(1)}, u32[]{:S(2)}, u32[]{:S(2)}) collective-permute-start(bf16[384,768]{1,0:T(8,128)(2,1)S(1)} %get-tuple-element.39), channel_id=1, source_target_pairs={{1,17},{3,19},{5,21},{7,23},{9,25},{11,27},{13,29},{15,31},{16,0},... | collective-permute-start | bytes 1769480 | tf_op jit(solution)/shard_map/ppermute | solution.py:252
  36.5 3.7 %collective-permute-start.8 = (f32[8,128]{1,0:T(8,128)S(1)}, f32[8,128]{1,0:T(8,128)S(1)}, u32[]{:S(2)}, u32[]{:S(2)}) collective-permute-start(f32[8,128]{1,0:T(8,128)S(1)} %get-tuple-element.34), channel_id=1, source_target_pairs={{0,2},{1,3},{2,0},{3,1},{4,6},{5,7},{6,4},{7,5},{8,10},{9,11},{10,... | collective-permute-start | bytes 12296 | tf_op jit(solution)/shard_map/ppermute | solution.py:265
  36.6 15.8 %collective-permute-start.14 = (bf16[384,768]{1,0:T(8,128)(2,1)S(1)}, bf16[384,768]{1,0:T(8,128)(2,1)S(1)}, u32[]{:S(2)}, u32[]{:S(2)}) collective-permute-start(bf16[384,768]{1,0:T(8,128)(2,1)S(1)} %get-tuple-element.44), channel_id=1, source_target_pairs={{0,2},{1,15},{2,4},{3,1},{4,6},{5,3},{6,8},{7,5},{8,10},{9,7},{10,... | collective-permute-start | bytes 1769480 | tf_op jit(solution)/shard_map/ppermute | solution.py:262
  40.2 12.2 %collective-permute-start.13 = (bf16[384,768]{1,0:T(8,128)(2,1)S(1)}, bf16[384,768]{1,0:T(8,128)(2,1)S(1)}, u32[]{:S(2)}, u32[]{:S(2)}) collective-permute-start(bf16[384,768]{1,0:T(8,128)(2,1)S(1)} %get-tuple-element.43), channel_id=1, source_target_pairs={{0,1},{1,0},{2,3},{3,2},{4,5},{5,4},{6,7},{7,6},{8,9},{9,8},{10,11... | collective-permute-start | bytes 1769480 | tf_op jit(solution)/shard_map/ppermute | solution.py:267
  41.5 1.6 %collective-permute-start.9 = (f32[8,128]{1,0:T(8,128)S(1)}, f32[8,128]{1,0:T(8,128)S(1)}, u32[]{:S(2)}, u32[]{:S(2)}) collective-permute-start(f32[8,128]{1,0:T(8,128)S(1)} %add.15), channel_id=1, source_target_pairs={{0,1},{1,0},{2,3},{3,2},{4,5},{5,4},{6,7},{7,6},{8,9},{9,8},{10,11... | collective-permute-start | bytes 12296 | tf_op jit(solution)/shard_map/ppermute | solution.py:268
  43.2 3.6 %collective-permute-start.10 = (f32[8,128]{1,0:T(8,128)S(1)}, f32[8,128]{1,0:T(8,128)S(1)}, u32[]{:S(2)}, u32[]{:S(2)}) collective-permute-start(f32[8,128]{1,0:T(8,128)S(1)} %add.16), channel_id=1, source_target_pairs={{0,16},{1,17},{2,18},{3,19},{4,20},{5,21},{6,22},{7,23},{8,24},{9,... | collective-permute-start | bytes 12296 | tf_op jit(solution)/shard_map/ppermute | solution.py:270
  46.8 4.5 %collective-permute-start.12 = (f32[8,128]{1,0:T(8,128)S(1)}, f32[8,128]{1,0:T(8,128)S(1)}, u32[]{:S(2)}, u32[]{:S(2)}) collective-permute-start(f32[8,128]{1,0:T(8,128)S(1)} %add.17), channel_id=1, source_target_pairs={{0,8},{1,9},{2,10},{3,11},{4,12},{5,13},{6,14},{7,15},{8,0},{9,1},... | collective-permute-start | bytes 12296 | tf_op jit(solution)/shard_map/ppermute | solution.py:273
  51.3 3.6 %collective-permute-start.15 = (f32[8,128]{1,0:T(8,128)S(1)}, f32[8,128]{1,0:T(8,128)S(1)}, u32[]{:S(2)}, u32[]{:S(2)}) collective-permute-start(f32[8,128]{1,0:T(8,128)S(1)} %add.18), channel_id=1, source_target_pairs={{0,4},{1,5},{2,6},{3,7},{4,0},{5,1},{6,2},{7,3},{8,12},{9,13},{10,... | collective-permute-start | bytes 12296 | tf_op jit(solution)/shard_map/ppermute | solution.py:274

commit v5 on v4

--- a/solution.py
+++ b/solution.py
@@ -43,12 +43,10 @@
     return sum(row[:, k : k + 128] for k in range(0, row.shape[1], 128))
 
 
-def weigh(mismatch, weight_column, weight_row, twice=0):
+def weigh(mismatch, weight_column, weight_row):
     weight = weight_column * weight_row
     weighted = weight * mismatch
-    loss = weighted * mismatch
-    sums = [lanes(loss) + lanes(loss[:, :twice]), lanes(weight) + lanes(weight[:, :twice])] if twice else [lanes(loss), lanes(weight)]
-    return weighted.astype(BF16), *sums
+    return weighted.astype(BF16), lanes(weighted * mismatch), lanes(weight)
 
 
 def tile(loss, weight):
@@ -143,26 +141,38 @@
     teacher_sim[...] = similarity(unit, mates[:, ds:])
 
 
-def ring_kernel(
-    rows, ds, first, near_meta, mates, teacher_sim, far_s, far_counts, sums_before, coefficients, to_far, sums
+def ring_own_kernel(rows, ds, first, mates, teacher_sim, far_s, far_counts, coefficients, to_far, sums):
+    own = Packed(first, None, rows, ds)
+    mismatch = similarity(far_s[...], mates[:rows, :ds]) - teacher_sim[:, :rows]
+    far_column = column(far_counts[...].astype(F32).reshape(1, rows))
+    coefficients[...], loss, weight = weigh(mismatch, far_column, own.counts() * own.switch(3, 1))
+    to_far[...] = dot(coefficients[...], mates[:rows, :ds]).astype(BF16)
+    sums[...] = tile(2.0 * loss, 2.0 * weight)
+
+
+def ring_near_kernel(
+    rows, ds, near_meta, mates, teacher_sim, far_s, far_counts, coefficients, before, sums_before, sums_own,
+    total, to_near, sums,
 ):
-    own, near = Packed(first, None, rows, ds), Packed(near_meta, None, 0, ds)
-    mismatch = similarity(far_s[...], mates[:, :ds]) - teacher_sim[...]
-    mates_row = jnp.concatenate([own.counts() * own.switch(3, 1), near.counts(rows) * near.switch(2, 0)], axis=1)
+    near = Packed(near_meta, None, 0, ds)
+    mismatch = similarity(far_s[...], mates[rows:, :ds]) - teacher_sim[:, rows:]
     far_column = column(far_counts[...].astype(F32).reshape(1, rows))
-    coefficients[...], loss, weight = weigh(mismatch, far_column, mates_row, twice=rows)
-    to_far[...] = dot(coefficients[:, :rows], mates[:rows, :ds]).astype(BF16)
-    sums[...] = sums_before[...] + tile(loss, weight)
-
-
-def ring_mix_kernel(rows, ds, far_s, coefficients, before, total, to_near):
-    to_near[...] = dot_transposed(coefficients[:, rows:], far_s[...]).astype(BF16)
-    total[...] = before[...] + dot_transposed(coefficients[:, :rows], far_s[...])
-
-
-def final_kernel(rows, ds, own, scale, total, from_near, from_far, from_cross, grad, result, sent):
+    near_coefficients, loss, weight = weigh(mismatch, far_column, near.counts(rows) * near.switch(2, 0))
+    to_near[...] = dot_transposed(near_coefficients, far_s[...]).astype(BF16)
+    total[...] = before[...] + dot_transposed(coefficients[...], far_s[...])
+    result = sums_before[...] + sums_own[...] + tile(loss, weight)
+    sums[...] = jnp.broadcast_to(jnp.concatenate([result[0:1], result[1:2]], axis=1), sums.shape)
+
+
+def final_kernel(
+    rows, ds, own, scale, total, from_near, from_far, from_cross, sums, grad, loss, result, result_loss, sent
+):
+    parts = jnp.sum(sums[...], axis=0, keepdims=True)
+    loss_sum, weight_sum = (jnp.sum(parts[:, k : k + 128], axis=1, keepdims=True) for k in (0, 128))
+    result_loss[...] = jnp.broadcast_to(ds * loss_sum / weight_sum, result_loss.shape)
+    copies = [pltpu.make_async_copy(result_loss, loss, sent.at[PIECES])]
+    copies[0].start()
     size = rows // PIECES
-    copies = []
     for i in range(PIECES):
         piece = pl.ds(i * size, size)
         unit = own[piece].astype(F32)
@@ -176,11 +186,6 @@
         copy.wait()
 
 
-def loss_kernel(width, sums, loss):
-    total = jnp.sum(sums[...], axis=1, keepdims=True)
-    loss[...] = width * total[0:1] / total[1:2]
-
-
 def call(kernel, outs, vmem_mib, *operands, flops=0, **options):
     return pl.pallas_call(
         kernel,
@@ -189,10 +194,6 @@
         cost_estimate=pl.CostEstimate(flops=flops, bytes_accessed=0, transcendentals=0),
         **options,
     )(*operands)
-
-
-def powers(first, end):
-    return [first << i for i in range(end.bit_length()) if first << i < end]
 
 
 def per_device(student, teacher, counts, plan):
@@ -253,34 +254,27 @@
     (teacher_sim,) = call(
         functools.partial(ring_teacher_kernel, ds), (f((rows, 2 * rows), F32),), 24, mates, ring_t
     )
-    coefficients, give_ring, sums = call(
-        on_blocks(ring_kernel), (f((rows, 2 * rows), BF16), half, sums_shape), 24,
-        first, near_meta, mates, teacher_sim, ring_s, ring_counts, sums,
+    coefficients, give_ring, own_sums = call(
+        on_blocks(ring_own_kernel), (f((rows, rows), BF16), half, sums_shape), 24,
+        first, mates, teacher_sim, ring_s, ring_counts,
         flops=10**10,
     )
-    total, give_near = call(on_blocks(ring_mix_kernel), (acc, half), 24, ring_s, coefficients, total)
     from_ring = ring_back(give_ring)
-    across = [route(lambda g, m, bit=bit: (g ^ bit, m)) for bit in powers(1, groups)]
-    along = [route(lambda g, m, bit=bit: (g, m ^ bit)) for bit in powers(2, members)]
-    sums = sums + along[0](sums)
-    sums, give_near = lax.optimization_barrier((sums, give_near))
+    total, give_near, sums = call(
+        on_blocks(ring_near_kernel), (acc, half, f((groups * members, 256), F32)), 24,
+        near_meta, mates, teacher_sim, ring_s, ring_counts, coefficients, total, sums, own_sums,
+    )
+    sums, give_near, from_cross = lax.optimization_barrier((sums, give_near, from_cross))
     from_near = to_near(give_near)
-    sums = sums + to_near(sums)
-    for exchange in across:
-        sums = sums + exchange(sums)
-    sums, from_cross = lax.optimization_barrier((sums, from_cross))
-    for exchange in along[:1:-1]:
-        sums = sums + exchange(sums)
-    received = along[1](sums)
-
-    (grad,) = call(
-        on_blocks(final_kernel), (acc,), 24, own_s, scale, total, from_near, from_ring, from_cross,
-        out_specs=(pl.BlockSpec(memory_space=pltpu.HBM),),
-        scratch_shapes=[pltpu.VMEM((rows, ds), F32), pltpu.SemaphoreType.DMA((PIECES,))],
-    )
-    sums, grad = lax.optimization_barrier((sums, grad))
-    (loss,) = call(functools.partial(loss_kernel, ds), (f((1, 1), F32),), 24, sums + received)
-    return grad, loss.reshape(())
+    sums = lax.all_to_all(sums, AXES, 0, 0, tiled=True)
+    grad, loss = call(
+        on_blocks(final_kernel), (acc, f((1, 128), F32)), 24, own_s, scale, total, from_near, from_ring, from_cross, sums,
+        out_specs=(pl.BlockSpec(memory_space=pltpu.HBM),) * 2,
+        scratch_shapes=[
+            pltpu.VMEM((rows, ds), F32), pltpu.VMEM((1, 128), F32), pltpu.SemaphoreType.DMA((PIECES + 1,)),
+        ],
+    )
+    return grad, loss[0, 0]
 
 
 def solution(mesh):

time: 55.7 us -> 54 us (0.969)
  blocking collectives: 0 us -> 10.2 us
  starting transfers between devices: 23 us -> 15.1 us
  waiting for transfers between devices: 20.8 us -> 16.9 us
    all_to_all x0 -> x1, blocking collectives: none -> 10.2 us  [per_device(): sums = lax.all_to_all(sums, AXES, 0, 0, tiled=True)]
    ppermute x5 -> x0, waiting for transfers between devices: 8.02 us -> none  [the longest x2 4.75 us: per_device(): sums = sums + exchange(sums)]
    ppermute x5 -> x0, starting transfers between devices: 4.64 us -> none  [the longest x2 3.38 us: per_device(): sums = sums + exchange(sums)]
    ppermute x1, waiting for transfers between devices: 0.01 us -> 4.07 us  [per_device(): from_cross = cross_back(give_cross)]
    ppermute x1, starting transfers between devices: 2.01 us -> 0.06 us  [per_device(): from_ring = ring_back(give_ring)]
    ppermute x1, starting transfers between devices: 1.31 us -> 0.01 us  [per_device(): from_near = to_near(give_near)]
    pallas_call x8 -> x7, Pallas kernels: 10.9 us -> 10.8 us  [call(): pl.pallas_call(kernel, out_shape=outs, compiler_params=pltpu.CompilerPara...]
  transfers between devices with their start and end apart: 16 -> 11, of which waited for: 8 -> 4; matrix products, arithmetic and copies ran while one was open for 0% -> 0% of each run, Pallas kernels for 18% -> 17%
where the time goes in v5:
time: 54 us; the launch traced here: 53.8 us
  waiting for transfers between devices  16.9 us (31%)
  starting transfers between devices  15.1 us (28%)
  Pallas kernels  10.8 us (20%)
  blocking collectives  10.2 us (19%)
  between operations  0.76 us (1%)
    pallas_call x7, Pallas kernels, call(): pl.pallas_call(kernel, out_shape=outs, compiler_params=pltpu.CompilerPara...  10.8 us
    all_to_all x1, blocking collectives, per_device(): sums = lax.all_to_all(sums, AXES, 0, 0, tiled=True)  10.2 us
    ppermute x3, waiting for transfers between devices, per_device(): near_meta, cross = (to_near(own_meta), (to_cross(first), to_cross(second)))  9.74 us
    ppermute x1, starting transfers between devices, per_device(): to_ring(teacher)  5.96 us
    ppermute x3, starting transfers between devices, per_device(): near_meta, cross = (to_near(own_meta), (to_cross(first), to_cross(second)))  4.86 us
    ppermute x1, waiting for transfers between devices, per_device(): from_cross = cross_back(give_cross)  4.07 us
    ppermute x2, waiting for transfers between devices, per_device(): ring_s, ring_counts = (to_ring(own_s), to_ring(counts))  3.06 us
    ppermute x2, starting transfers between devices, per_device(): ring_s, ring_counts = (to_ring(own_s), to_ring(counts))  2.37 us
  transfers between devices with their start and end apart: 11, of which 4 were waited for; matrix products, arithmetic and copies ran while one was open for 0% of the time, Pallas kernels for 17%

profile of v5, /device:TPU:0, one launch (start us, length us, event | category | flops | bytes accessed | tf_op | source)
XLA Modules:
  0.0 53.8 jit_solution(9821807488076229885)
XLA Ops:
  0.6 0.0 copy-start
  0.6 0.5 collective-permute-start.1
  1.2 0.1 collective-permute-start.2
  1.2 6.0 %collective-permute-start.3 = (bf16[384,1024]{1,0:T(8,128)(2,1)}, bf16[384,1024]{1,0:T(8,128)(2,1)S(1)}, u32[]{:S(2)}, u32[]{:S(2)}) collective-permute-start(bf16[384,1024]{1,0:T(8,128)(2,1)} %t_hbm.1), channel_id=1, source_target_pairs={{0,14},{1,3},{2,0},{3,5},{4,2},{5,7},{6,4},{7,9},{8,6},{9,11},{10,... | collective-permute-start | bytes 2359304 | tf_op jit(solution)/shard_map/ppermute | solution.py:225
  7.2 1.6 %shard_map.59 = (bf16[384,1792]{1,0:T(8,128)(2,1)S(1)}, bf16[400,896]{1,0:T(8,128)(2,1)S(1)}, bf16[384,896]{1,0:T(8,128)(2,1)S(1)}, bf16[384,768]{1,0:T(8,128)(2...) custom-call(s32[384]{0:T(512)} %counts_hbm.1, s32[1,5]{1,0:T(1,128)} %bitcast.9, bf16[384,768]{1,0:T(8,128)(2,1)} %s_hbm.1, ...), custom_call_target="tpu_custom_call" | custom-call | tf_op jit(solution)/shard_map/pallas_call | solution.py:190
  8.8 3.5 %collective-permute-start.6 = (bf16[400,896]{1,0:T(8,128)(2,1)S(1)}, bf16[400,896]{1,0:T(8,128)(2,1)S(1)}, u32[]{:S(2)}, u32[]{:S(2)}) collective-permute-start(bf16[400,896]{1,0:T(8,128)(2,1)S(1)} %get-tuple-element.29.first), channel_id=1, source_target_pairs={{0,16},{2,18},{4,20},{6,22},{8,24},{10,26},{12,28},{14,30},{17,1},... | collective-permute-start | bytes 2150408 | tf_op jit(solution)/shard_map/ppermute | solution.py:245
  12.3 0.1 collective-permute-start
  12.4 1.2 %collective-permute-done.near_meta = bf16[16,768]{1,0:T(8,128)(2,1)S(1)} collective-permute-done((bf16[16,768]{1,0:T(8,128)(2,1)S(1)}, bf16[16,768]{1,0:T(8,128)(2,1)S(1)}, u32[]{:S(2)}, u32[]{:S(2)}) %collective-permute-start) | collective-permute-done | bytes 24608 | tf_op jit(solution)/shard_map/ppermute | solution.py:245
  13.6 1.3 %collective-permute-start.7 = (bf16[384,896]{1,0:T(8,128)(2,1)S(1)}, bf16[384,896]{1,0:T(8,128)(2,1)S(1)}, u32[]{:S(2)}, u32[]{:S(2)}) collective-permute-start(bf16[384,896]{1,0:T(8,128)(2,1)S(1)} %get-tuple-element.32), channel_id=1, source_target_pairs={{0,16},{2,18},{4,20},{6,22},{8,24},{10,26},{12,28},{14,30},{17,1},... | collective-permute-start | bytes 2064392 | tf_op jit(solution)/shard_map/ppermute | solution.py:245
  14.9 0.0 collective-permute-done.1.near_student
  14.9 0.6 %collective-permute-start.4 = (bf16[384,768]{1,0:T(8,128)(2,1)S(1)}, bf16[384,768]{1,0:T(8,128)(2,1)S(1)}, u32[]{:S(2)}, u32[]{:S(2)}) collective-permute-start(bf16[384,768]{1,0:T(8,128)(2,1)S(1)} %get-tuple-element.25.own), channel_id=1, source_target_pairs={{0,14},{1,3},{2,0},{3,5},{4,2},{5,7},{6,4},{7,9},{8,6},{9,11},{10,... | collective-permute-start | bytes 1769480 | tf_op jit(solution)/shard_map/ppermute | solution.py:244
  15.6 0.0 collective-permute-done.2.near_teacher
  15.6 0.0 copy-done
  15.6 1.7 %collective-permute-start.5 = (s32[384]{0:T(512)S(1)}, s32[384]{0:T(512)S(1)}, u32[]{:S(2)}, u32[]{:S(2)}) collective-permute-start(s32[384]{0:T(512)S(1)} %copy-done), channel_id=1, source_target_pairs={{0,14},{1,3},{2,0},{3,5},{4,2},{5,7},{6,4},{7,9},{8,6},{9,11},{10,... | collective-permute-start | bytes 4616 | tf_op jit(solution)/shard_map/ppermute | solution.py:244
  17.3 2.5 %shard_map.60 = (bf16[768,1792]{1,0:T(8,128)(2,1)S(1)}, f32[384,768]{1,0:T(8,128)S(1)}, f32[8,128]{1,0:T(8,128)S(1)}) custom-call(bf16[384,1792]{1,0:T(8,128)(2,1)S(1)} %get-tuple-element.28.both, bf16[400,896]{1,0:T(8,128)(2,1)S(1)} %get-tuple-element.29.first, bf16[16,768]{1,0:T(8,128)(2,1)S(1)} %collective-permute-done.near_meta, ...), custom_call_target="tpu_custom_call" | custom-call | tf_op jit(solution)/shard_map/pallas_call | solution.py:190
  19.8 8.6 %collective-permute-done.7.far_second = bf16[384,896]{1,0:T(8,128)(2,1)S(1)} collective-permute-done((bf16[384,896]{1,0:T(8,128)(2,1)S(1)}, bf16[384,896]{1,0:T(8,128)(2,1)S(1)}, u32[]{:S(2)}, u32[]{:S(2)}) %collective-permute-start.7) | collective-permute-done | bytes 688160 | tf_op jit(solution)/shard_map/ppermute | solution.py:245
  28.4 0.0 collective-permute-done.6.far_first
  28.4 1.8 %shard_map.63 = (f32[384,768]{1,0:T(8,128)S(1)}, bf16[384,768]{1,0:T(8,128)(2,1)S(1)}, f32[8,128]{1,0:T(8,128)S(1)}) custom-call(bf16[384,1792]{1,0:T(8,128)(2,1)S(1)} %get-tuple-element.28.both, bf16[400,896]{1,0:T(8,128)(2,1)S(1)} %get-tuple-element.29.first, bf16[400,896]{1,0:T(8,128)(2,1)S(1)} %collective-permute-done.6.far_first, ...), custom_call_target="tpu_custom_call" | custom-call | tf_op jit(solution)/shard_map/pallas_call | solution.py:190
  30.2 1.3 %collective-permute-start.8 = (bf16[384,768]{1,0:T(8,128)(2,1)S(1)}, bf16[384,768]{1,0:T(8,128)(2,1)S(1)}, u32[]{:S(2)}, u32[]{:S(2)}) collective-permute-start(bf16[384,768]{1,0:T(8,128)(2,1)S(1)} %get-tuple-element.41), channel_id=1, source_target_pairs={{1,17},{3,19},{5,21},{7,23},{9,25},{11,27},{13,29},{15,31},{16,0},... | collective-permute-start | bytes 1769480 | tf_op jit(solution)/shard_map/ppermute | solution.py:253
  31.5 0.0 collective-permute-done.3.far
  31.5 0.9 %shard_map.61.teacher_sim = f32[384,768]{1,0:T(8,128)S(1)} custom-call(bf16[768,1792]{1,0:T(8,128)(2,1)S(1)} %get-tuple-element.30.mates, bf16[384,1024]{1,0:T(8,128)(2,1)S(1)} %collective-permute-done.3.far), custom_call_target="tpu_custom_call" | custom-call | tf_op jit(solution)/shard_map/pallas_call | solution.py:190
  32.4 3.1 %collective-permute-done.5.far_counts = s32[384]{0:T(512)S(1)} collective-permute-done((s32[384]{0:T(512)S(1)}, s32[384]{0:T(512)S(1)}, u32[]{:S(2)}, u32[]{:S(2)}) %collective-permute-start.5) | collective-permute-done | bytes 1568 | tf_op jit(solution)/shard_map/ppermute | solution.py:244
  35.4 0.0 collective-permute-done.4.far_s
  35.4 0.9 %shard_map.62 = (bf16[384,384]{1,0:T(8,128)(2,1)S(1)}, bf16[384,768]{1,0:T(8,128)(2,1)S(1)}, f32[8,128]{1,0:T(8,128)S(1)}) custom-call(bf16[400,896]{1,0:T(8,128)(2,1)S(1)} %get-tuple-element.29.first, bf16[768,1792]{1,0:T(8,128)(2,1)S(1)} %get-tuple-element.30.mates, f32[384,768]{1,0:T(8,128)S(1)} %shard_map.61.teacher_sim, ...), custom_call_target="tpu_custom_call" | custom-call | flops 10000000000 | tf_op jit(solution)/shard_map/pallas_call | solution.py:190
  36.4 0.1 collective-permute-start.10
  36.5 1.4 %shard_map.64 = (f32[384,768]{1,0:T(8,128)S(1)}, bf16[384,768]{1,0:T(8,128)(2,1)S(1)}, f32[32,256]{1,0:T(8,128)S(1)}) custom-call(bf16[16,768]{1,0:T(8,128)(2,1)S(1)} %collective-permute-done.near_meta, bf16[768,1792]{1,0:T(8,128)(2,1)S(1)} %get-tuple-element.30.mates, f32[384,768]{1,0:T(8,128)S(1)} %shard_map.61.teacher_sim, ...), custom_call_target="tpu_custom_call" | custom-call | tf_op jit(solution)/shard_map/pallas_call | solution.py:190
  37.9 4.1 %collective-permute-done.8.from_cross = bf16[384,768]{1,0:T(8,128)(2,1)S(1)} collective-permute-done((bf16[384,768]{1,0:T(8,128)(2,1)S(1)}, bf16[384,768]{1,0:T(8,128)(2,1)S(1)}, u32[]{:S(2)}, u32[]{:S(2)}) %collective-permute-start.8) | collective-permute-done | bytes 589856 | tf_op jit(solution)/shard_map/ppermute | solution.py:253
  41.9 0.0 collective-permute-start.9
  42.0 10.2 %all_to_all.11 = f32[32,1,256]{2,1,0:T(1,128)S(1)} all-to-all(f32[32,1,256]{2,1,0:T(1,128)S(1)} %copy.6), channel_id=1, replica_groups=mesh['group'=2,'member'=16] {'group','member'}, dimensions={0} | all-to-all | bytes 65536 | tf_op jit(solution)/shard_map/all_to_all | solution.py:269
  52.2 0.0 collective-permute-done.10.from_far
  52.2 0.0 collective-permute-done.9.from_near
  52.2 1.6 %shard_map.65 = (f32[384,768]{1,0:T(8,128)}, f32[1,128]{1,0:T(1,128)}) custom-call(bf16[384,768]{1,0:T(8,128)(2,1)S(1)} %get-tuple-element.25.own, f32[384,128]{1,0:T(8,128)S(1)} %get-tuple-element.26.scale, f32[384,768]{1,0:T(8,128)S(1)} %get-tuple-element.38.total, bf16[384,768]{1,0:T(8,128)(2,1)S(1)} %collective-permute-done.9.from_near, ...), custom_call_target="tpu_custom_call" | custom-call | tf_op jit(solution)/shard_map/pallas_call | solution.py:190
  (2 shorter events, 0.0 us)
Async XLA Ops:
  0.6 14.9 %copy-start = (s32[384]{0:T(512)S(1)}, s32[384]{0:T(512)}, u32[]{:S(2)}) copy-start(s32[384]{0:T(512)} %counts_hbm.1) | copy-start | bytes 4612
  0.6 14.3 %collective-permute-start.1 = (bf16[384,768]{1,0:T(8,128)(2,1)}, bf16[384,768]{1,0:T(8,128)(2,1)S(1)}, u32[]{:S(2)}, u32[]{:S(2)}) collective-permute-start(bf16[384,768]{1,0:T(8,128)(2,1)} %s_hbm.1), channel_id=1, source_target_pairs={{0,1},{1,0},{2,3},{3,2},{4,5},{5,4},{6,7},{7,6},{8,9},{9,8},{10,11... | collective-permute-start | bytes 1769480 | tf_op jit(solution)/shard_map/ppermute | solution.py:225
  1.2 14.4 %collective-permute-start.2 = (bf16[384,1024]{1,0:T(8,128)(2,1)}, bf16[384,1024]{1,0:T(8,128)(2,1)S(1)}, u32[]{:S(2)}, u32[]{:S(2)}) collective-permute-start(bf16[384,1024]{1,0:T(8,128)(2,1)} %t_hbm.1), channel_id=1, source_target_pairs={{0,1},{1,0},{2,3},{3,2},{4,5},{5,4},{6,7},{7,6},{8,9},{9,8},{10,11... | collective-permute-start | bytes 2359304 | tf_op jit(solution)/shard_map/ppermute | solution.py:225
  1.2 30.2 %collective-permute-start.3 = (bf16[384,1024]{1,0:T(8,128)(2,1)}, bf16[384,1024]{1,0:T(8,128)(2,1)S(1)}, u32[]{:S(2)}, u32[]{:S(2)}) collective-permute-start(bf16[384,1024]{1,0:T(8,128)(2,1)} %t_hbm.1), channel_id=1, source_target_pairs={{0,14},{1,3},{2,0},{3,5},{4,2},{5,7},{6,4},{7,9},{8,6},{9,11},{10,... | collective-permute-start | bytes 2359304 | tf_op jit(solution)/shard_map/ppermute | solution.py:225
  8.8 19.6 %collective-permute-start.6 = (bf16[400,896]{1,0:T(8,128)(2,1)S(1)}, bf16[400,896]{1,0:T(8,128)(2,1)S(1)}, u32[]{:S(2)}, u32[]{:S(2)}) collective-permute-start(bf16[400,896]{1,0:T(8,128)(2,1)S(1)} %get-tuple-element.29.first), channel_id=1, source_target_pairs={{0,16},{2,18},{4,20},{6,22},{8,24},{10,26},{12,28},{14,30},{17,1},... | collective-permute-start | bytes 2150408 | tf_op jit(solution)/shard_map/ppermute | solution.py:245
  12.3 1.3 %collective-permute-start = (bf16[16,768]{1,0:T(8,128)(2,1)S(1)}, bf16[16,768]{1,0:T(8,128)(2,1)S(1)}, u32[]{:S(2)}, u32[]{:S(2)}) collective-permute-start(bf16[16,768]{1,0:T(8,128)(2,1)S(1)} %get-tuple-element.27), channel_id=1, source_target_pairs={{0,1},{1,0},{2,3},{3,2},{4,5},{5,4},{6,7},{7,6},{8,9},{9,8},{10,11... | collective-permute-start | bytes 73736 | tf_op jit(solution)/shard_map/ppermute | solution.py:245
  13.6 14.8 %collective-permute-start.7 = (bf16[384,896]{1,0:T(8,128)(2,1)S(1)}, bf16[384,896]{1,0:T(8,128)(2,1)S(1)}, u32[]{:S(2)}, u32[]{:S(2)}) collective-permute-start(bf16[384,896]{1,0:T(8,128)(2,1)S(1)} %get-tuple-element.32), channel_id=1, source_target_pairs={{0,16},{2,18},{4,20},{6,22},{8,24},{10,26},{12,28},{14,30},{17,1},... | collective-permute-start | bytes 2064392 | tf_op jit(solution)/shard_map/ppermute | solution.py:245
  14.9 20.5 %collective-permute-start.4 = (bf16[384,768]{1,0:T(8,128)(2,1)S(1)}, bf16[384,768]{1,0:T(8,128)(2,1)S(1)}, u32[]{:S(2)}, u32[]{:S(2)}) collective-permute-start(bf16[384,768]{1,0:T(8,128)(2,1)S(1)} %get-tuple-element.25.own), channel_id=1, source_target_pairs={{0,14},{1,3},{2,0},{3,5},{4,2},{5,7},{6,4},{7,9},{8,6},{9,11},{10,... | collective-permute-start | bytes 1769480 | tf_op jit(solution)/shard_map/ppermute | solution.py:244
  15.6 19.9 %collective-permute-start.5 = (s32[384]{0:T(512)S(1)}, s32[384]{0:T(512)S(1)}, u32[]{:S(2)}, u32[]{:S(2)}) collective-permute-start(s32[384]{0:T(512)S(1)} %copy-done), channel_id=1, source_target_pairs={{0,14},{1,3},{2,0},{3,5},{4,2},{5,7},{6,4},{7,9},{8,6},{9,11},{10,... | collective-permute-start | bytes 4616 | tf_op jit(solution)/shard_map/ppermute | solution.py:244
  30.2 11.8 %collective-permute-start.8 = (bf16[384,768]{1,0:T(8,128)(2,1)S(1)}, bf16[384,768]{1,0:T(8,128)(2,1)S(1)}, u32[]{:S(2)}, u32[]{:S(2)}) collective-permute-start(bf16[384,768]{1,0:T(8,128)(2,1)S(1)} %get-tuple-element.41), channel_id=1, source_target_pairs={{1,17},{3,19},{5,21},{7,23},{9,25},{11,27},{13,29},{15,31},{16,0},... | collective-permute-start | bytes 1769480 | tf_op jit(solution)/shard_map/ppermute | solution.py:253
  36.4 15.8 %collective-permute-start.10 = (bf16[384,768]{1,0:T(8,128)(2,1)S(1)}, bf16[384,768]{1,0:T(8,128)(2,1)S(1)}, u32[]{:S(2)}, u32[]{:S(2)}) collective-permute-start(bf16[384,768]{1,0:T(8,128)(2,1)S(1)} %get-tuple-element.43), channel_id=1, source_target_pairs={{0,2},{1,15},{2,4},{3,1},{4,6},{5,3},{6,8},{7,5},{8,10},{9,7},{10,... | collective-permute-start | bytes 1769480 | tf_op jit(solution)/shard_map/ppermute | solution.py:262
  41.9 10.2 %collective-permute-start.9 = (bf16[384,768]{1,0:T(8,128)(2,1)S(1)}, bf16[384,768]{1,0:T(8,128)(2,1)S(1)}, u32[]{:S(2)}, u32[]{:S(2)}) collective-permute-start(bf16[384,768]{1,0:T(8,128)(2,1)S(1)} %get-tuple-element.42), channel_id=1, source_target_pairs={{0,1},{1,0},{2,3},{3,2},{4,5},{5,4},{6,7},{7,6},{8,9},{9,8},{10,11... | collective-permute-start | bytes 1769480 | tf_op jit(solution)/shard_map/ppermute | solution.py:268

commit v6 on v5

--- a/solution.py
+++ b/solution.py
@@ -46,7 +46,8 @@
 def weigh(mismatch, weight_column, weight_row):
     weight = weight_column * weight_row
     weighted = weight * mismatch
-    return weighted.astype(BF16), lanes(weighted * mismatch), lanes(weight)
+    weight_sum = lanes(weight_row * jnp.sum(weight_column, axis=0, keepdims=True))
+    return weighted.astype(BF16), lanes(weighted * mismatch), weight_sum
 
 
 def tile(loss, weight):
@@ -172,9 +173,9 @@
     result_loss[...] = jnp.broadcast_to(ds * loss_sum / weight_sum, result_loss.shape)
     copies = [pltpu.make_async_copy(result_loss, loss, sent.at[PIECES])]
     copies[0].start()
-    size = rows // PIECES
+    size = rows // (PIECES * (PIECES + 1) // 2)
     for i in range(PIECES):
-        piece = pl.ds(i * size, size)
+        piece = pl.ds(size * (i * (i + 1) // 2), size * (i + 1))
         unit = own[piece].astype(F32)
         received = from_near[piece].astype(F32) + from_far[piece].astype(F32) + from_cross[piece].astype(F32)
         summed = total[piece] + received

time: 54 us -> 54 us (level)
  no operation moved by 1% of the time
where the time goes in v6:
time: 54 us; the launch traced here: 53.8 us
  waiting for transfers between devices  16.9 us (31%)
  starting transfers between devices  15.1 us (28%)
  Pallas kernels  10.7 us (20%)
  blocking collectives  10.2 us (19%)
  between operations  0.76 us (1%)
    pallas_call x7, Pallas kernels, call(): pl.pallas_call(kernel, out_shape=outs, compiler_params=pltpu.CompilerPara...  10.7 us
    all_to_all x1, blocking collectives, per_device(): sums = lax.all_to_all(sums, AXES, 0, 0, tiled=True)  10.2 us
    ppermute x3, waiting for transfers between devices, per_device(): near_meta, cross = (to_near(own_meta), (to_cross(first), to_cross(second)))  9.76 us
    ppermute x1, starting transfers between devices, per_device(): to_ring(teacher)  5.96 us
    ppermute x3, starting transfers between devices, per_device(): near_meta, cross = (to_near(own_meta), (to_cross(first), to_cross(second)))  4.86 us
    ppermute x1, waiting for transfers between devices, per_device(): from_cross = cross_back(give_cross)  4.09 us
    ppermute x2, waiting for transfers between devices, per_device(): ring_s, ring_counts = (to_ring(own_s), to_ring(counts))  3.05 us
    ppermute x2, starting transfers between devices, per_device(): ring_s, ring_counts = (to_ring(own_s), to_ring(counts))  2.37 us
  transfers between devices with their start and end apart: 11, of which 4 were waited for; matrix products, arithmetic and copies ran while one was open for 0% of the time, Pallas kernels for 17%

profile of v6, /device:TPU:0, one launch (start us, length us, event | category | flops | bytes accessed | tf_op | source)
XLA Modules:
  0.0 53.8 jit_solution(3528343975437313872)
XLA Ops:
  0.6 0.0 copy-start
  0.6 0.5 collective-permute-start.1
  1.2 0.1 collective-permute-start.2
  1.2 6.0 %collective-permute-start.3 = (bf16[384,1024]{1,0:T(8,128)(2,1)}, bf16[384,1024]{1,0:T(8,128)(2,1)S(1)}, u32[]{:S(2)}, u32[]{:S(2)}) collective-permute-start(bf16[384,1024]{1,0:T(8,128)(2,1)} %t_hbm.1), channel_id=1, source_target_pairs={{0,14},{1,3},{2,0},{3,5},{4,2},{5,7},{6,4},{7,9},{8,6},{9,11},{10,... | collective-permute-start | bytes 2359304 | tf_op jit(solution)/shard_map/ppermute | solution.py:226
  7.2 1.6 %shard_map.59 = (bf16[384,1792]{1,0:T(8,128)(2,1)S(1)}, bf16[400,896]{1,0:T(8,128)(2,1)S(1)}, bf16[384,896]{1,0:T(8,128)(2,1)S(1)}, bf16[384,768]{1,0:T(8,128)(2...) custom-call(s32[384]{0:T(512)} %counts_hbm.1, s32[1,5]{1,0:T(1,128)} %bitcast.9, bf16[384,768]{1,0:T(8,128)(2,1)} %s_hbm.1, ...), custom_call_target="tpu_custom_call" | custom-call | tf_op jit(solution)/shard_map/pallas_call | solution.py:191
  8.8 3.5 %collective-permute-start.6 = (bf16[400,896]{1,0:T(8,128)(2,1)S(1)}, bf16[400,896]{1,0:T(8,128)(2,1)S(1)}, u32[]{:S(2)}, u32[]{:S(2)}) collective-permute-start(bf16[400,896]{1,0:T(8,128)(2,1)S(1)} %get-tuple-element.29.first), channel_id=1, source_target_pairs={{0,16},{2,18},{4,20},{6,22},{8,24},{10,26},{12,28},{14,30},{17,1},... | collective-permute-start | bytes 2150408 | tf_op jit(solution)/shard_map/ppermute | solution.py:246
  12.3 0.1 collective-permute-start
  12.4 1.2 %collective-permute-done.near_meta = bf16[16,768]{1,0:T(8,128)(2,1)S(1)} collective-permute-done((bf16[16,768]{1,0:T(8,128)(2,1)S(1)}, bf16[16,768]{1,0:T(8,128)(2,1)S(1)}, u32[]{:S(2)}, u32[]{:S(2)}) %collective-permute-start) | collective-permute-done | bytes 24608 | tf_op jit(solution)/shard_map/ppermute | solution.py:246
  13.6 1.3 %collective-permute-start.7 = (bf16[384,896]{1,0:T(8,128)(2,1)S(1)}, bf16[384,896]{1,0:T(8,128)(2,1)S(1)}, u32[]{:S(2)}, u32[]{:S(2)}) collective-permute-start(bf16[384,896]{1,0:T(8,128)(2,1)S(1)} %get-tuple-element.32), channel_id=1, source_target_pairs={{0,16},{2,18},{4,20},{6,22},{8,24},{10,26},{12,28},{14,30},{17,1},... | collective-permute-start | bytes 2064392 | tf_op jit(solution)/shard_map/ppermute | solution.py:246
  14.9 0.0 collective-permute-done.1.near_student
  14.9 0.6 %collective-permute-start.4 = (bf16[384,768]{1,0:T(8,128)(2,1)S(1)}, bf16[384,768]{1,0:T(8,128)(2,1)S(1)}, u32[]{:S(2)}, u32[]{:S(2)}) collective-permute-start(bf16[384,768]{1,0:T(8,128)(2,1)S(1)} %get-tuple-element.25.own), channel_id=1, source_target_pairs={{0,14},{1,3},{2,0},{3,5},{4,2},{5,7},{6,4},{7,9},{8,6},{9,11},{10,... | collective-permute-start | bytes 1769480 | tf_op jit(solution)/shard_map/ppermute | solution.py:245
  15.6 0.0 collective-permute-done.2.near_teacher
  15.6 0.0 copy-done
  15.6 1.7 %collective-permute-start.5 = (s32[384]{0:T(512)S(1)}, s32[384]{0:T(512)S(1)}, u32[]{:S(2)}, u32[]{:S(2)}) collective-permute-start(s32[384]{0:T(512)S(1)} %copy-done), channel_id=1, source_target_pairs={{0,14},{1,3},{2,0},{3,5},{4,2},{5,7},{6,4},{7,9},{8,6},{9,11},{10,... | collective-permute-start | bytes 4616 | tf_op jit(solution)/shard_map/ppermute | solution.py:245
  17.3 2.5 %shard_map.60 = (bf16[768,1792]{1,0:T(8,128)(2,1)S(1)}, f32[384,768]{1,0:T(8,128)S(1)}, f32[8,128]{1,0:T(8,128)S(1)}) custom-call(bf16[384,1792]{1,0:T(8,128)(2,1)S(1)} %get-tuple-element.28.both, bf16[400,896]{1,0:T(8,128)(2,1)S(1)} %get-tuple-element.29.first, bf16[16,768]{1,0:T(8,128)(2,1)S(1)} %collective-permute-done.near_meta, ...), custom_call_target="tpu_custom_call" | custom-call | tf_op jit(solution)/shard_map/pallas_call | solution.py:191
  19.8 8.6 %collective-permute-done.7.far_second = bf16[384,896]{1,0:T(8,128)(2,1)S(1)} collective-permute-done((bf16[384,896]{1,0:T(8,128)(2,1)S(1)}, bf16[384,896]{1,0:T(8,128)(2,1)S(1)}, u32[]{:S(2)}, u32[]{:S(2)}) %collective-permute-start.7) | collective-permute-done | bytes 688160 | tf_op jit(solution)/shard_map/ppermute | solution.py:246
  28.4 0.0 collective-permute-done.6.far_first
  28.4 1.8 %shard_map.63 = (f32[384,768]{1,0:T(8,128)S(1)}, bf16[384,768]{1,0:T(8,128)(2,1)S(1)}, f32[8,128]{1,0:T(8,128)S(1)}) custom-call(bf16[384,1792]{1,0:T(8,128)(2,1)S(1)} %get-tuple-element.28.both, bf16[400,896]{1,0:T(8,128)(2,1)S(1)} %get-tuple-element.29.first, bf16[400,896]{1,0:T(8,128)(2,1)S(1)} %collective-permute-done.6.far_first, ...), custom_call_target="tpu_custom_call" | custom-call | tf_op jit(solution)/shard_map/pallas_call | solution.py:191
  30.2 1.3 %collective-permute-start.8 = (bf16[384,768]{1,0:T(8,128)(2,1)S(1)}, bf16[384,768]{1,0:T(8,128)(2,1)S(1)}, u32[]{:S(2)}, u32[]{:S(2)}) collective-permute-start(bf16[384,768]{1,0:T(8,128)(2,1)S(1)} %get-tuple-element.41), channel_id=1, source_target_pairs={{1,17},{3,19},{5,21},{7,23},{9,25},{11,27},{13,29},{15,31},{16,0},... | collective-permute-start | bytes 1769480 | tf_op jit(solution)/shard_map/ppermute | solution.py:254
  31.5 0.0 collective-permute-done.3.far
  31.5 0.9 %shard_map.61.teacher_sim = f32[384,768]{1,0:T(8,128)S(1)} custom-call(bf16[768,1792]{1,0:T(8,128)(2,1)S(1)} %get-tuple-element.30.mates, bf16[384,1024]{1,0:T(8,128)(2,1)S(1)} %collective-permute-done.3.far), custom_call_target="tpu_custom_call" | custom-call | tf_op jit(solution)/shard_map/pallas_call | solution.py:191
  32.4 3.1 %collective-permute-done.5.far_counts = s32[384]{0:T(512)S(1)} collective-permute-done((s32[384]{0:T(512)S(1)}, s32[384]{0:T(512)S(1)}, u32[]{:S(2)}, u32[]{:S(2)}) %collective-permute-start.5) | collective-permute-done | bytes 1568 | tf_op jit(solution)/shard_map/ppermute | solution.py:245
  35.4 0.0 collective-permute-done.4.far_s
  35.4 0.9 %shard_map.62 = (bf16[384,384]{1,0:T(8,128)(2,1)S(1)}, bf16[384,768]{1,0:T(8,128)(2,1)S(1)}, f32[8,128]{1,0:T(8,128)S(1)}) custom-call(bf16[400,896]{1,0:T(8,128)(2,1)S(1)} %get-tuple-element.29.first, bf16[768,1792]{1,0:T(8,128)(2,1)S(1)} %get-tuple-element.30.mates, f32[384,768]{1,0:T(8,128)S(1)} %shard_map.61.teacher_sim, ...), custom_call_target="tpu_custom_call" | custom-call | flops 10000000000 | tf_op jit(solution)/shard_map/pallas_call | solution.py:191
  36.4 0.1 collective-permute-start.10
  36.4 1.4 %shard_map.64 = (f32[384,768]{1,0:T(8,128)S(1)}, bf16[384,768]{1,0:T(8,128)(2,1)S(1)}, f32[32,256]{1,0:T(8,128)S(1)}) custom-call(bf16[16,768]{1,0:T(8,128)(2,1)S(1)} %collective-permute-done.near_meta, bf16[768,1792]{1,0:T(8,128)(2,1)S(1)} %get-tuple-element.30.mates, f32[384,768]{1,0:T(8,128)S(1)} %shard_map.61.teacher_sim, ...), custom_call_target="tpu_custom_call" | custom-call | tf_op jit(solution)/shard_map/pallas_call | solution.py:191
  37.9 4.1 %collective-permute-done.8.from_cross = bf16[384,768]{1,0:T(8,128)(2,1)S(1)} collective-permute-done((bf16[384,768]{1,0:T(8,128)(2,1)S(1)}, bf16[384,768]{1,0:T(8,128)(2,1)S(1)}, u32[]{:S(2)}, u32[]{:S(2)}) %collective-permute-start.8) | collective-permute-done | bytes 589856 | tf_op jit(solution)/shard_map/ppermute | solution.py:254
  41.9 0.0 collective-permute-start.9
  42.0 10.2 %all_to_all.11 = f32[32,1,256]{2,1,0:T(1,128)S(1)} all-to-all(f32[32,1,256]{2,1,0:T(1,128)S(1)} %copy.6), channel_id=1, replica_groups=mesh['group'=2,'member'=16] {'group','member'}, dimensions={0} | all-to-all | bytes 65536 | tf_op jit(solution)/shard_map/all_to_all | solution.py:270
  52.2 0.0 collective-permute-done.10.from_far
  52.2 0.0 collective-permute-done.9.from_near
  52.2 1.6 %shard_map.65 = (f32[384,768]{1,0:T(8,128)}, f32[1,128]{1,0:T(1,128)}) custom-call(bf16[384,768]{1,0:T(8,128)(2,1)S(1)} %get-tuple-element.25.own, f32[384,128]{1,0:T(8,128)S(1)} %get-tuple-element.26.scale, f32[384,768]{1,0:T(8,128)S(1)} %get-tuple-element.38.total, bf16[384,768]{1,0:T(8,128)(2,1)S(1)} %collective-permute-done.9.from_near, ...), custom_call_target="tpu_custom_call" | custom-call | tf_op jit(solution)/shard_map/pallas_call | solution.py:191
  (2 shorter events, 0.0 us)
Async XLA Ops:
  0.6 14.9 %copy-start = (s32[384]{0:T(512)S(1)}, s32[384]{0:T(512)}, u32[]{:S(2)}) copy-start(s32[384]{0:T(512)} %counts_hbm.1) | copy-start | bytes 4612
  0.6 14.3 %collective-permute-start.1 = (bf16[384,768]{1,0:T(8,128)(2,1)}, bf16[384,768]{1,0:T(8,128)(2,1)S(1)}, u32[]{:S(2)}, u32[]{:S(2)}) collective-permute-start(bf16[384,768]{1,0:T(8,128)(2,1)} %s_hbm.1), channel_id=1, source_target_pairs={{0,1},{1,0},{2,3},{3,2},{4,5},{5,4},{6,7},{7,6},{8,9},{9,8},{10,11... | collective-permute-start | bytes 1769480 | tf_op jit(solution)/shard_map/ppermute | solution.py:226
  1.2 14.4 %collective-permute-start.2 = (bf16[384,1024]{1,0:T(8,128)(2,1)}, bf16[384,1024]{1,0:T(8,128)(2,1)S(1)}, u32[]{:S(2)}, u32[]{:S(2)}) collective-permute-start(bf16[384,1024]{1,0:T(8,128)(2,1)} %t_hbm.1), channel_id=1, source_target_pairs={{0,1},{1,0},{2,3},{3,2},{4,5},{5,4},{6,7},{7,6},{8,9},{9,8},{10,11... | collective-permute-start | bytes 2359304 | tf_op jit(solution)/shard_map/ppermute | solution.py:226
  1.2 30.2 %collective-permute-start.3 = (bf16[384,1024]{1,0:T(8,128)(2,1)}, bf16[384,1024]{1,0:T(8,128)(2,1)S(1)}, u32[]{:S(2)}, u32[]{:S(2)}) collective-permute-start(bf16[384,1024]{1,0:T(8,128)(2,1)} %t_hbm.1), channel_id=1, source_target_pairs={{0,14},{1,3},{2,0},{3,5},{4,2},{5,7},{6,4},{7,9},{8,6},{9,11},{10,... | collective-permute-start | bytes 2359304 | tf_op jit(solution)/shard_map/ppermute | solution.py:226
  8.8 19.6 %collective-permute-start.6 = (bf16[400,896]{1,0:T(8,128)(2,1)S(1)}, bf16[400,896]{1,0:T(8,128)(2,1)S(1)}, u32[]{:S(2)}, u32[]{:S(2)}) collective-permute-start(bf16[400,896]{1,0:T(8,128)(2,1)S(1)} %get-tuple-element.29.first), channel_id=1, source_target_pairs={{0,16},{2,18},{4,20},{6,22},{8,24},{10,26},{12,28},{14,30},{17,1},... | collective-permute-start | bytes 2150408 | tf_op jit(solution)/shard_map/ppermute | solution.py:246
  12.3 1.3 %collective-permute-start = (bf16[16,768]{1,0:T(8,128)(2,1)S(1)}, bf16[16,768]{1,0:T(8,128)(2,1)S(1)}, u32[]{:S(2)}, u32[]{:S(2)}) collective-permute-start(bf16[16,768]{1,0:T(8,128)(2,1)S(1)} %get-tuple-element.27), channel_id=1, source_target_pairs={{0,1},{1,0},{2,3},{3,2},{4,5},{5,4},{6,7},{7,6},{8,9},{9,8},{10,11... | collective-permute-start | bytes 73736 | tf_op jit(solution)/shard_map/ppermute | solution.py:246
  13.6 14.8 %collective-permute-start.7 = (bf16[384,896]{1,0:T(8,128)(2,1)S(1)}, bf16[384,896]{1,0:T(8,128)(2,1)S(1)}, u32[]{:S(2)}, u32[]{:S(2)}) collective-permute-start(bf16[384,896]{1,0:T(8,128)(2,1)S(1)} %get-tuple-element.32), channel_id=1, source_target_pairs={{0,16},{2,18},{4,20},{6,22},{8,24},{10,26},{12,28},{14,30},{17,1},... | collective-permute-start | bytes 2064392 | tf_op jit(solution)/shard_map/ppermute | solution.py:246
  14.9 20.5 %collective-permute-start.4 = (bf16[384,768]{1,0:T(8,128)(2,1)S(1)}, bf16[384,768]{1,0:T(8,128)(2,1)S(1)}, u32[]{:S(2)}, u32[]{:S(2)}) collective-permute-start(bf16[384,768]{1,0:T(8,128)(2,1)S(1)} %get-tuple-element.25.own), channel_id=1, source_target_pairs={{0,14},{1,3},{2,0},{3,5},{4,2},{5,7},{6,4},{7,9},{8,6},{9,11},{10,... | collective-permute-start | bytes 1769480 | tf_op jit(solution)/shard_map/ppermute | solution.py:245
  15.6 19.9 %collective-permute-start.5 = (s32[384]{0:T(512)S(1)}, s32[384]{0:T(512)S(1)}, u32[]{:S(2)}, u32[]{:S(2)}) collective-permute-start(s32[384]{0:T(512)S(1)} %copy-done), channel_id=1, source_target_pairs={{0,14},{1,3},{2,0},{3,5},{4,2},{5,7},{6,4},{7,9},{8,6},{9,11},{10,... | collective-permute-start | bytes 4616 | tf_op jit(solution)/shard_map/ppermute | solution.py:245
  30.2 11.8 %collective-permute-start.8 = (bf16[384,768]{1,0:T(8,128)(2,1)S(1)}, bf16[384,768]{1,0:T(8,128)(2,1)S(1)}, u32[]{:S(2)}, u32[]{:S(2)}) collective-permute-start(bf16[384,768]{1,0:T(8,128)(2,1)S(1)} %get-tuple-element.41), channel_id=1, source_target_pairs={{1,17},{3,19},{5,21},{7,23},{9,25},{11,27},{13,29},{15,31},{16,0},... | collective-permute-start | bytes 1769480 | tf_op jit(solution)/shard_map/ppermute | solution.py:254
  36.4 15.8 %collective-permute-start.10 = (bf16[384,768]{1,0:T(8,128)(2,1)S(1)}, bf16[384,768]{1,0:T(8,128)(2,1)S(1)}, u32[]{:S(2)}, u32[]{:S(2)}) collective-permute-start(bf16[384,768]{1,0:T(8,128)(2,1)S(1)} %get-tuple-element.43), channel_id=1, source_target_pairs={{0,2},{1,15},{2,4},{3,1},{4,6},{5,3},{6,8},{7,5},{8,10},{9,7},{10,... | collective-permute-start | bytes 1769480 | tf_op jit(solution)/shard_map/ppermute | solution.py:263
  41.9 10.3 %collective-permute-start.9 = (bf16[384,768]{1,0:T(8,128)(2,1)S(1)}, bf16[384,768]{1,0:T(8,128)(2,1)S(1)}, u32[]{:S(2)}, u32[]{:S(2)}) collective-permute-start(bf16[384,768]{1,0:T(8,128)(2,1)S(1)} %get-tuple-element.42), channel_id=1, source_target_pairs={{0,1},{1,0},{2,3},{3,2},{4,5},{5,4},{6,7},{7,6},{8,9},{9,8},{10,11... | collective-permute-start | bytes 1769480 | tf_op jit(solution)/shard_map/ppermute | solution.py:269

commit v7 on v5

--- a/solution.py
+++ b/solution.py
@@ -252,12 +252,11 @@
     )
     from_cross = cross_back(give_cross)
     (teacher_sim,) = call(
-        functools.partial(ring_teacher_kernel, ds), (f((rows, 2 * rows), F32),), 24, mates, ring_t
+        functools.partial(ring_teacher_kernel, ds), (f((rows, 2 * rows), F32),), 24, mates, ring_t, flops=10**10
     )
     coefficients, give_ring, own_sums = call(
         on_blocks(ring_own_kernel), (f((rows, rows), BF16), half, sums_shape), 24,
         first, mates, teacher_sim, ring_s, ring_counts,
-        flops=10**10,
     )
     from_ring = ring_back(give_ring)
     total, give_near, sums = call(

time: 54 us -> 53.9 us (level)
    ppermute x1, waiting for transfers between devices: 0.01 us -> 1.84 us  [per_device(): to_near(student)]
    ppermute x3, waiting for transfers between devices: 9.74 us -> 8.19 us  [per_device(): near_meta, cross = (to_near(own_meta), (to_cross(first), to_cross(second)))]
  transfers between devices with their start and end apart: 11 -> 11, of which waited for: 4 -> 5; matrix products, arithmetic and copies ran while one was open for 0% -> 0% of each run, Pallas kernels for 17% -> 17%
where the time goes in v7:
time: 53.9 us; the launch traced here: 53.7 us
  waiting for transfers between devices  17.2 us (32%)
  starting transfers between devices  14.8 us (27%)
  Pallas kernels  10.8 us (20%)
  blocking collectives  10.2 us (19%)
  between operations  0.76 us (1%)
    pallas_call x7, Pallas kernels, call(): pl.pallas_call(kernel, out_shape=outs, compiler_params=pltpu.CompilerPara...  10.8 us
    all_to_all x1, blocking collectives, per_device(): sums = lax.all_to_all(sums, AXES, 0, 0, tiled=True)  10.2 us
    ppermute x3, waiting for transfers between devices, per_device(): near_meta, cross = (to_near(own_meta), (to_cross(first), to_cross(second)))  8.19 us
    ppermute x1, starting transfers between devices, per_device(): to_ring(teacher)  5.59 us
    ppermute x3, starting transfers between devices, per_device(): near_meta, cross = (to_near(own_meta), (to_cross(first), to_cross(second)))  4.87 us
    ppermute x1, waiting for transfers between devices, per_device(): from_cross = cross_back(give_cross)  4.06 us
    ppermute x2, waiting for transfers between devices, per_device(): ring_s, ring_counts = (to_ring(own_s), to_ring(counts))  3.06 us
    ppermute x2, starting transfers between devices, per_device(): ring_s, ring_counts = (to_ring(own_s), to_ring(counts))  1.91 us
  transfers between devices with their start and end apart: 11, of which 5 were waited for; matrix products, arithmetic and copies ran while one was open for 0% of the time, Pallas kernels for 17%

profile of v7, /device:TPU:0, one launch (start us, length us, event | category | flops | bytes accessed | tf_op | source)
XLA Modules:
  0.0 53.7 jit_solution(13194245624973847274)
XLA Ops:
  0.6 0.0 copy-start
  0.7 0.5 collective-permute-start.2
  1.2 5.6 %collective-permute-start.3 = (bf16[384,1024]{1,0:T(8,128)(2,1)}, bf16[384,1024]{1,0:T(8,128)(2,1)S(1)}, u32[]{:S(2)}, u32[]{:S(2)}) collective-permute-start(bf16[384,1024]{1,0:T(8,128)(2,1)} %t_hbm.1), channel_id=1, source_target_pairs={{0,14},{1,3},{2,0},{3,5},{4,2},{5,7},{6,4},{7,9},{8,6},{9,11},{10,... | collective-permute-start | bytes 2359304 | tf_op jit(solution)/shard_map/ppermute | solution.py:225
  6.8 1.6 %shard_map.59 = (bf16[384,1792]{1,0:T(8,128)(2,1)S(1)}, bf16[400,896]{1,0:T(8,128)(2,1)S(1)}, bf16[384,896]{1,0:T(8,128)(2,1)S(1)}, bf16[384,768]{1,0:T(8,128)(2...) custom-call(s32[384]{0:T(512)} %counts_hbm.1, s32[1,5]{1,0:T(1,128)} %bitcast.9, bf16[384,768]{1,0:T(8,128)(2,1)} %s_hbm.1, ...), custom_call_target="tpu_custom_call" | custom-call | tf_op jit(solution)/shard_map/pallas_call | solution.py:190
  8.4 3.5 %collective-permute-start.6 = (bf16[400,896]{1,0:T(8,128)(2,1)S(1)}, bf16[400,896]{1,0:T(8,128)(2,1)S(1)}, u32[]{:S(2)}, u32[]{:S(2)}) collective-permute-start(bf16[400,896]{1,0:T(8,128)(2,1)S(1)} %get-tuple-element.29.first), channel_id=1, source_target_pairs={{0,16},{2,18},{4,20},{6,22},{8,24},{10,26},{12,28},{14,30},{17,1},... | collective-permute-start | bytes 2150408 | tf_op jit(solution)/shard_map/ppermute | solution.py:245
  11.9 1.3 %collective-permute-start.7 = (bf16[384,896]{1,0:T(8,128)(2,1)S(1)}, bf16[384,896]{1,0:T(8,128)(2,1)S(1)}, u32[]{:S(2)}, u32[]{:S(2)}) collective-permute-start(bf16[384,896]{1,0:T(8,128)(2,1)S(1)} %get-tuple-element.32), channel_id=1, source_target_pairs={{0,16},{2,18},{4,20},{6,22},{8,24},{10,26},{12,28},{14,30},{17,1},... | collective-permute-start | bytes 2064392 | tf_op jit(solution)/shard_map/ppermute | solution.py:245
  13.2 0.1 collective-permute-start
  13.3 1.2 %collective-permute-done.near_meta = bf16[16,768]{1,0:T(8,128)(2,1)S(1)} collective-permute-done((bf16[16,768]{1,0:T(8,128)(2,1)S(1)}, bf16[16,768]{1,0:T(8,128)(2,1)S(1)}, u32[]{:S(2)}, u32[]{:S(2)}) %collective-permute-start) | collective-permute-done | bytes 24608 | tf_op jit(solution)/shard_map/ppermute | solution.py:245
  14.5 0.0 copy-done
  14.5 0.2 collective-permute-start.1
  14.7 1.8 %collective-permute-done.1.near_student = bf16[384,768]{1,0:T(8,128)(2,1)S(1)} collective-permute-done((bf16[384,768]{1,0:T(8,128)(2,1)S(1)}, bf16[384,768]{1,0:T(8,128)(2,1)S(1)}, u32[]{:S(2)}, u32[]{:S(2)}) %collective-permute-start.1) | collective-permute-done | bytes 589856 | tf_op jit(solution)/shard_map/ppermute | solution.py:225
  16.5 0.5 collective-permute-start.5
  17.0 0.0 collective-permute-done.2.near_teacher
  17.0 1.4 %collective-permute-start.4 = (bf16[384,768]{1,0:T(8,128)(2,1)S(1)}, bf16[384,768]{1,0:T(8,128)(2,1)S(1)}, u32[]{:S(2)}, u32[]{:S(2)}) collective-permute-start(bf16[384,768]{1,0:T(8,128)(2,1)S(1)} %get-tuple-element.25.own), channel_id=1, source_target_pairs={{0,14},{1,3},{2,0},{3,5},{4,2},{5,7},{6,4},{7,9},{8,6},{9,11},{10,... | collective-permute-start | bytes 1769480 | tf_op jit(solution)/shard_map/ppermute | solution.py:244
  18.4 2.5 %shard_map.60 = (bf16[768,1792]{1,0:T(8,128)(2,1)S(1)}, f32[384,768]{1,0:T(8,128)S(1)}, f32[8,128]{1,0:T(8,128)S(1)}) custom-call(bf16[384,1792]{1,0:T(8,128)(2,1)S(1)} %get-tuple-element.28.both, bf16[400,896]{1,0:T(8,128)(2,1)S(1)} %get-tuple-element.29.first, bf16[16,768]{1,0:T(8,128)(2,1)S(1)} %collective-permute-done.near_meta, ...), custom_call_target="tpu_custom_call" | custom-call | tf_op jit(solution)/shard_map/pallas_call | solution.py:190
  21.0 7.0 %collective-permute-done.7.far_second = bf16[384,896]{1,0:T(8,128)(2,1)S(1)} collective-permute-done((bf16[384,896]{1,0:T(8,128)(2,1)S(1)}, bf16[384,896]{1,0:T(8,128)(2,1)S(1)}, u32[]{:S(2)}, u32[]{:S(2)}) %collective-permute-start.7) | collective-permute-done | bytes 688160 | tf_op jit(solution)/shard_map/ppermute | solution.py:245
  28.0 0.0 collective-permute-done.6.far_first
  28.0 1.8 %shard_map.63 = (f32[384,768]{1,0:T(8,128)S(1)}, bf16[384,768]{1,0:T(8,128)(2,1)S(1)}, f32[8,128]{1,0:T(8,128)S(1)}) custom-call(bf16[384,1792]{1,0:T(8,128)(2,1)S(1)} %get-tuple-element.28.both, bf16[400,896]{1,0:T(8,128)(2,1)S(1)} %get-tuple-element.29.first, bf16[400,896]{1,0:T(8,128)(2,1)S(1)} %collective-permute-done.6.far_first, ...), custom_call_target="tpu_custom_call" | custom-call | tf_op jit(solution)/shard_map/pallas_call | solution.py:190
  29.7 1.3 %collective-permute-start.8 = (bf16[384,768]{1,0:T(8,128)(2,1)S(1)}, bf16[384,768]{1,0:T(8,128)(2,1)S(1)}, u32[]{:S(2)}, u32[]{:S(2)}) collective-permute-start(bf16[384,768]{1,0:T(8,128)(2,1)S(1)} %get-tuple-element.41), channel_id=1, source_target_pairs={{1,17},{3,19},{5,21},{7,23},{9,25},{11,27},{13,29},{15,31},{16,0},... | collective-permute-start | bytes 1769480 | tf_op jit(solution)/shard_map/ppermute | solution.py:253
  31.0 0.0 collective-permute-done.3.far
  31.0 0.9 %shard_map.61.teacher_sim = f32[384,768]{1,0:T(8,128)S(1)} custom-call(bf16[768,1792]{1,0:T(8,128)(2,1)S(1)} %get-tuple-element.30.mates, bf16[384,1024]{1,0:T(8,128)(2,1)S(1)} %collective-permute-done.3.far), custom_call_target="tpu_custom_call" | custom-call | flops 10000000000 | tf_op jit(solution)/shard_map/pallas_call | solution.py:190
  31.9 0.0 collective-permute-done.5.far_counts
  32.0 3.1 %collective-permute-done.4.far_s = bf16[384,768]{1,0:T(8,128)(2,1)S(1)} collective-permute-done((bf16[384,768]{1,0:T(8,128)(2,1)S(1)}, bf16[384,768]{1,0:T(8,128)(2,1)S(1)}, u32[]{:S(2)}, u32[]{:S(2)}) %collective-permute-start.4) | collective-permute-done | bytes 589856 | tf_op jit(solution)/shard_map/ppermute | solution.py:244
  35.0 0.9 %shard_map.62 = (bf16[384,384]{1,0:T(8,128)(2,1)S(1)}, bf16[384,768]{1,0:T(8,128)(2,1)S(1)}, f32[8,128]{1,0:T(8,128)S(1)}) custom-call(bf16[400,896]{1,0:T(8,128)(2,1)S(1)} %get-tuple-element.29.first, bf16[768,1792]{1,0:T(8,128)(2,1)S(1)} %get-tuple-element.30.mates, f32[384,768]{1,0:T(8,128)S(1)} %shard_map.61.teacher_sim, ...), custom_call_target="tpu_custom_call" | custom-call | tf_op jit(solution)/shard_map/pallas_call | solution.py:190
  36.0 0.1 collective-permute-start.10
  36.0 1.4 %shard_map.64 = (f32[384,768]{1,0:T(8,128)S(1)}, bf16[384,768]{1,0:T(8,128)(2,1)S(1)}, f32[32,256]{1,0:T(8,128)S(1)}) custom-call(bf16[16,768]{1,0:T(8,128)(2,1)S(1)} %collective-permute-done.near_meta, bf16[768,1792]{1,0:T(8,128)(2,1)S(1)} %get-tuple-element.30.mates, f32[384,768]{1,0:T(8,128)S(1)} %shard_map.61.teacher_sim, ...), custom_call_target="tpu_custom_call" | custom-call | tf_op jit(solution)/shard_map/pallas_call | solution.py:190
  37.4 4.1 %collective-permute-done.8.from_cross = bf16[384,768]{1,0:T(8,128)(2,1)S(1)} collective-permute-done((bf16[384,768]{1,0:T(8,128)(2,1)S(1)}, bf16[384,768]{1,0:T(8,128)(2,1)S(1)}, u32[]{:S(2)}, u32[]{:S(2)}) %collective-permute-start.8) | collective-permute-done | bytes 589856 | tf_op jit(solution)/shard_map/ppermute | solution.py:253
  41.5 0.4 collective-permute-start.9
  41.9 10.2 %all_to_all.11 = f32[32,1,256]{2,1,0:T(1,128)S(1)} all-to-all(f32[32,1,256]{2,1,0:T(1,128)S(1)} %copy.6), channel_id=1, replica_groups=mesh['group'=2,'member'=16] {'group','member'}, dimensions={0} | all-to-all | bytes 65536 | tf_op jit(solution)/shard_map/all_to_all | solution.py:268
  52.1 0.0 collective-permute-done.10.from_far
  52.1 0.0 collective-permute-done.9.from_near
  52.1 1.6 %shard_map.65 = (f32[384,768]{1,0:T(8,128)}, f32[1,128]{1,0:T(1,128)}) custom-call(bf16[384,768]{1,0:T(8,128)(2,1)S(1)} %get-tuple-element.25.own, f32[384,128]{1,0:T(8,128)S(1)} %get-tuple-element.26.scale, f32[384,768]{1,0:T(8,128)S(1)} %get-tuple-element.38.total, bf16[384,768]{1,0:T(8,128)(2,1)S(1)} %collective-permute-done.9.from_near, ...), custom_call_target="tpu_custom_call" | custom-call | tf_op jit(solution)/shard_map/pallas_call | solution.py:190
  (4 shorter events, 0.0 us)
Async XLA Ops:
  0.6 13.9 %copy-start = (bf16[384,768]{1,0:T(8,128)(2,1)S(1)}, bf16[384,768]{1,0:T(8,128)(2,1)}, u32[]{:S(2)}) copy-start(bf16[384,768]{1,0:T(8,128)(2,1)} %s_hbm.1) | copy-start | bytes 1769476
  0.6 15.9 %copy-start.1 = (s32[384]{0:T(512)S(1)}, s32[384]{0:T(512)}, u32[]{:S(2)}) copy-start(s32[384]{0:T(512)} %counts_hbm.1) | copy-start | bytes 4612
  0.7 16.4 %collective-permute-start.2 = (bf16[384,1024]{1,0:T(8,128)(2,1)}, bf16[384,1024]{1,0:T(8,128)(2,1)S(1)}, u32[]{:S(2)}, u32[]{:S(2)}) collective-permute-start(bf16[384,1024]{1,0:T(8,128)(2,1)} %t_hbm.1), channel_id=1, source_target_pairs={{0,1},{1,0},{2,3},{3,2},{4,5},{5,4},{6,7},{7,6},{8,9},{9,8},{10,11... | collective-permute-start | bytes 2359304 | tf_op jit(solution)/shard_map/ppermute | solution.py:225
  1.2 29.9 %collective-permute-start.3 = (bf16[384,1024]{1,0:T(8,128)(2,1)}, bf16[384,1024]{1,0:T(8,128)(2,1)S(1)}, u32[]{:S(2)}, u32[]{:S(2)}) collective-permute-start(bf16[384,1024]{1,0:T(8,128)(2,1)} %t_hbm.1), channel_id=1, source_target_pairs={{0,14},{1,3},{2,0},{3,5},{4,2},{5,7},{6,4},{7,9},{8,6},{9,11},{10,... | collective-permute-start | bytes 2359304 | tf_op jit(solution)/shard_map/ppermute | solution.py:225
  8.4 19.6 %collective-permute-start.6 = (bf16[400,896]{1,0:T(8,128)(2,1)S(1)}, bf16[400,896]{1,0:T(8,128)(2,1)S(1)}, u32[]{:S(2)}, u32[]{:S(2)}) collective-permute-start(bf16[400,896]{1,0:T(8,128)(2,1)S(1)} %get-tuple-element.29.first), channel_id=1, source_target_pairs={{0,16},{2,18},{4,20},{6,22},{8,24},{10,26},{12,28},{14,30},{17,1},... | collective-permute-start | bytes 2150408 | tf_op jit(solution)/shard_map/ppermute | solution.py:245
  11.9 16.1 %collective-permute-start.7 = (bf16[384,896]{1,0:T(8,128)(2,1)S(1)}, bf16[384,896]{1,0:T(8,128)(2,1)S(1)}, u32[]{:S(2)}, u32[]{:S(2)}) collective-permute-start(bf16[384,896]{1,0:T(8,128)(2,1)S(1)} %get-tuple-element.32), channel_id=1, source_target_pairs={{0,16},{2,18},{4,20},{6,22},{8,24},{10,26},{12,28},{14,30},{17,1},... | collective-permute-start | bytes 2064392 | tf_op jit(solution)/shard_map/ppermute | solution.py:245
  13.2 1.3 %collective-permute-start = (bf16[16,768]{1,0:T(8,128)(2,1)S(1)}, bf16[16,768]{1,0:T(8,128)(2,1)S(1)}, u32[]{:S(2)}, u32[]{:S(2)}) collective-permute-start(bf16[16,768]{1,0:T(8,128)(2,1)S(1)} %get-tuple-element.27), channel_id=1, source_target_pairs={{0,1},{1,0},{2,3},{3,2},{4,5},{5,4},{6,7},{7,6},{8,9},{9,8},{10,11... | collective-permute-start | bytes 73736 | tf_op jit(solution)/shard_map/ppermute | solution.py:245
  14.5 2.0 %collective-permute-start.1 = (bf16[384,768]{1,0:T(8,128)(2,1)S(1)}, bf16[384,768]{1,0:T(8,128)(2,1)S(1)}, u32[]{:S(2)}, u32[]{:S(2)}) collective-permute-start(bf16[384,768]{1,0:T(8,128)(2,1)S(1)} %copy-done), channel_id=1, source_target_pairs={{0,1},{1,0},{2,3},{3,2},{4,5},{5,4},{6,7},{7,6},{8,9},{9,8},{10,11... | collective-permute-start | bytes 1769480 | tf_op jit(solution)/shard_map/ppermute | solution.py:225
  16.5 15.4 %collective-permute-start.5 = (s32[384]{0:T(512)S(1)}, s32[384]{0:T(512)S(1)}, u32[]{:S(2)}, u32[]{:S(2)}) collective-permute-start(s32[384]{0:T(512)S(1)} %copy-done.1), channel_id=1, source_target_pairs={{0,14},{1,3},{2,0},{3,5},{4,2},{5,7},{6,4},{7,9},{8,6},{9,11},{10,... | collective-permute-start | bytes 4616 | tf_op jit(solution)/shard_map/ppermute | solution.py:244
  17.0 18.0 %collective-permute-start.4 = (bf16[384,768]{1,0:T(8,128)(2,1)S(1)}, bf16[384,768]{1,0:T(8,128)(2,1)S(1)}, u32[]{:S(2)}, u32[]{:S(2)}) collective-permute-start(bf16[384,768]{1,0:T(8,128)(2,1)S(1)} %get-tuple-element.25.own), channel_id=1, source_target_pairs={{0,14},{1,3},{2,0},{3,5},{4,2},{5,7},{6,4},{7,9},{8,6},{9,11},{10,... | collective-permute-start | bytes 1769480 | tf_op jit(solution)/shard_map/ppermute | solution.py:244
  29.7 11.8 %collective-permute-start.8 = (bf16[384,768]{1,0:T(8,128)(2,1)S(1)}, bf16[384,768]{1,0:T(8,128)(2,1)S(1)}, u32[]{:S(2)}, u32[]{:S(2)}) collective-permute-start(bf16[384,768]{1,0:T(8,128)(2,1)S(1)} %get-tuple-element.41), channel_id=1, source_target_pairs={{1,17},{3,19},{5,21},{7,23},{9,25},{11,27},{13,29},{15,31},{16,0},... | collective-permute-start | bytes 1769480 | tf_op jit(solution)/shard_map/ppermute | solution.py:253
  36.0 16.2 %collective-permute-start.10 = (bf16[384,768]{1,0:T(8,128)(2,1)S(1)}, bf16[384,768]{1,0:T(8,128)(2,1)S(1)}, u32[]{:S(2)}, u32[]{:S(2)}) collective-permute-start(bf16[384,768]{1,0:T(8,128)(2,1)S(1)} %get-tuple-element.43), channel_id=1, source_target_pairs={{0,2},{1,15},{2,4},{3,1},{4,6},{5,3},{6,8},{7,5},{8,10},{9,7},{10,... | collective-permute-start | bytes 1769480 | tf_op jit(solution)/shard_map/ppermute | solution.py:261
  41.5 10.6 %collective-permute-start.9 = (bf16[384,768]{1,0:T(8,128)(2,1)S(1)}, bf16[384,768]{1,0:T(8,128)(2,1)S(1)}, u32[]{:S(2)}, u32[]{:S(2)}) collective-permute-start(bf16[384,768]{1,0:T(8,128)(2,1)S(1)} %get-tuple-element.42), channel_id=1, source_target_pairs={{0,1},{1,0},{2,3},{3,2},{4,5},{5,4},{6,7},{7,6},{8,9},{9,8},{10,11... | collective-permute-start | bytes 1769480 | tf_op jit(solution)/shard_map/ppermute | solution.py:267
